TPU v7x, 32 devices: a whole 2x2x4 slice. The times are simulated.
32 devices in a mesh: wave: 8 (over y, x, core), freq: 4 (over z).
Axes of the slice: x: 2, y: 2, z: 4, core: 2. Of those that a mesh axis runs over, the one named last changes fastest.
Arguments:
- res_re: float32 [2048, 8192], P('wave', 'freq'), may hold values from -6 to 6
- res_im: float32 [2048, 8192], P('wave', 'freq'), may hold values from -6 to 6
- basis_re: float32 [256, 8192], P(None, 'freq'), may hold values from -0.046875 to 0.046875
- basis_im: float32 [256, 8192], P(None, 'freq'), may hold values from -0.046875 to 0.046875
- lengths: int32 [2048], P('wave'), may hold values from 8 to 64
- pivots: int32 [128], replicated, may hold values from 0 to 2047, as said below
Outputs:
- coef_re: float32 [2048, 128], P('wave')
- coef_im: float32 [2048, 128], P('wave')
- new_re: float32 [2048, 8192], P('wave', 'freq')
- new_im: float32 [2048, 8192], P('wave', 'freq')
- errors: float32 [2048], P('wave')
Inputs may be any that keep to these rules, and one draw needn't show every extreme that they name: The 128 pivots are distinct waveform indices.
All inputs are finite; a program needn't handle non-finite values. Where the computation divides by a largest or mean magnitude, that divisor is 1e-20 or more.
Results may differ from a plain program's by a relative error of at most 0.0003.
Values sent between devices are 32-bit elements; how exact they have to be, the bound alone decides.
No kernel may reach another device: no remote copies, remote signals or barrier semaphores. Data moves between devices by JAX's collectives and lax.ppermute only.
A program may use at most 64 MiB of HBM per device.

v0:
```python
import jax
import jax.numpy as jnp
from jax import lax
from jax.sharding import PartitionSpec as P

BIN_BLOCK = 128
NS_STEPS = 6


epsilon = 1e-06


def plain(left, right):
    return jnp.dot(left, right, precision=lax.Precision.HIGHEST, preferred_element_type=jnp.float32)


def against(left, right):
    return lax.dot_general(
        left,
        right,
        (((1,), (1,)), ((), ())),
        precision=lax.Precision.HIGHEST,
        preferred_element_type=jnp.float32,
    )


def product(left_re, left_im, right_re, right_im):
    return (
        plain(left_re, right_re) - plain(left_im, right_im),
        plain(left_re, right_im) + plain(left_im, right_re),
    )


def inner(left_re, left_im, right_re, right_im):
    return (
        against(left_re, right_re) + against(left_im, right_im),
        against(left_im, right_re) - against(left_re, right_im),
    )


def whiten(gram_re, gram_im, pivot_re, pivot_im):
    scale = 1.0 / jnp.sqrt(jnp.diagonal(gram_re) + epsilon)
    outer = scale[:, None] * scale[None, :]
    gram_re = gram_re * outer
    gram_im = gram_im * outer
    unit_re = pivot_re * scale[:, None]
    unit_im = pivot_im * scale[:, None]
    bound = jnp.max(jnp.sum(jnp.abs(gram_re) + jnp.abs(gram_im), axis=1))
    ident = jnp.eye(gram_re.shape[0], dtype=jnp.float32)
    your_re = gram_re / bound
    your_im = gram_im / bound
    zed_re = ident
    zed_im = jnp.zeros_like(ident)
    for step in range(NS_STEPS):
        mix_re, mix_im = product(zed_re, zed_im, your_re, your_im)
        step_re = 1.5 * ident - 0.5 * mix_re
        step_im = -0.5 * mix_im
        your_re, your_im = product(your_re, your_im, step_re, step_im)
        zed_re, zed_im = product(step_re, step_im, zed_re, zed_im)
    factor = 1.0 / jnp.sqrt(bound)
    return product(zed_re * factor, zed_im * factor, unit_re, unit_im)


def body(res_re, res_im, basis_re, basis_im, lengths, pivots):
    wave_rows = res_re.shape[0]
    freq_cols = res_re.shape[1]
    bins = lax.axis_index("freq") * freq_cols + jnp.arange(freq_cols, dtype=jnp.int32)
    mask = (bins[None, :] < BIN_BLOCK * lengths[:, None]).astype(jnp.float32)
    live_re = res_re * mask
    live_im = res_im * mask
    owned = lax.axis_index("wave") * wave_rows + jnp.arange(wave_rows, dtype=jnp.int32)
    select = (pivots[:, None] == owned[None, :]).astype(jnp.float32)
    picked_re = plain(select, live_re)
    picked_im = plain(select, live_im)
    pivot_re, pivot_im = lax.psum((picked_re, picked_im), "wave")
    cross_re, cross_im = inner(pivot_re, pivot_im, basis_re, basis_im)
    basis_gram_re, basis_gram_im = inner(basis_re, basis_im, basis_re, basis_im)
    cross_re, cross_im, basis_gram_re, basis_gram_im = lax.psum(
        (cross_re, cross_im, basis_gram_re, basis_gram_im), "freq"
    )
    twist_re, twist_im = product(cross_re, cross_im, basis_gram_re, basis_gram_im)
    total_re = 2.0 * cross_re - twist_re
    total_im = 2.0 * cross_im - twist_im
    back_re, back_im = product(total_re, total_im, basis_re, basis_im)
    pivot_re = pivot_re - back_re
    pivot_im = pivot_im - back_im
    gram_re, gram_im = inner(pivot_re, pivot_im, pivot_re, pivot_im)
    gram_re, gram_im = lax.psum((gram_re, gram_im), "freq")
    block_re, block_im = whiten(gram_re, gram_im, pivot_re, pivot_im)
    coef_re, coef_im = inner(live_re, live_im, block_re, block_im)
    coef_re, coef_im = lax.psum((coef_re, coef_im), "freq")
    back_re, back_im = product(coef_re, coef_im, block_re, block_im)
    new_re = (live_re - back_re) * mask
    new_im = (live_im - back_im) * mask
    partial_sq = jnp.sum(new_re * new_re + new_im * new_im, axis=1)
    summed_sq = lax.psum(partial_sq, "freq")
    errors = summed_sq / (BIN_BLOCK * lengths).astype(jnp.float32)
    return (coef_re, coef_im, new_re, new_im, errors)


def solution(mesh):
    placed = (
        P("wave", "freq"),
        P("wave", "freq"),
        P(None, "freq"),
        P(None, "freq"),
        P("wave"),
        P(),
    )
    return jax.shard_map(
        body,
        mesh=mesh,
        in_specs=placed,
        out_specs=(
            P("wave", None),
            P("wave", None),
            P("wave", "freq"),
            P("wave", "freq"),
            P("wave"),
        ),
        check_vma=False,
    )
```

profile of v0, /device:TPU:0, one launch (start us, length us, event | category | flops | bytes accessed | tf_op | source)
XLA Modules:
  0.0 292.6 jit_solution(6388612484896936666)
XLA Ops:
  8.1 3.8 %fusion.9 = f32[128,2048]{1,0:T(8,128)} fusion(f32[256,2048]{1,0:T(8,128)} %param.7, s32[2048]{0:T(1024)S(1)} %iota_add_fusion, s32[256]{0:T(256)S(1)} %get-tuple-element.20, s32[256]{0:T(256)S(1)} %get-tuple-element.19, s32[128]{0:T(128)} %param.11), kind=kOutput, calls=%fused_computation.21 | convolution fusion | flops 806387712 | bytes 3156480 | tf_op jit(solution)/shard_map/dot_general | solution.py:14
  11.9 2.0 fusion.6
  14.2 1.9 fusion.91
  16.1 1.9 fusion.94
  18.0 2.6 convolution_subtract_fusion.3
  20.6 2.6 convolution_add_fusion.3
  23.1 55.2 %all-reduce.9.cloned.1.call-done = (f32[128,2048]{1,0:T(8,128)}, f32[128,2048]{1,0:T(8,128)}) async-done(((f32[128,2048]{1,0:T(8,128)}, f32[128,2048]{1,0:T(8,128)}), (f32[128,2048]{1,0:T(8,128)}, f32[128,2048]{1,0:T(8,128)})) %all-reduce.9.cloned.1.call-update) | async-done | bytes 2097168 | tf_op jit(solution)/shard_map/psum | solution.py:75
  78.3 3.5 %fusion.90 = f32[128,256]{1,0:T(8,128)S(1)} fusion(f32[128,2048]{1,0:T(8,128)} %get-tuple-element.7, f32[256,2048]{1,0:T(8,128)S(1)} %copy-done), kind=kOutput, calls=%fused_computation.150 | convolution fusion | flops 805306368 | bytes 3276800 | tf_op jit(solution)/shard_map/dot_general | solution.py:18
  81.9 2.2 fusion.93
  84.1 3.3 %convolution_add_fusion.5 = f32[128,256]{1,0:T(8,128)} fusion(f32[128,256]{1,0:T(8,128)S(1)} %fusion.90, f32[128,2048]{1,0:T(8,128)S(1)} %copy-done.17, f32[256,2048]{1,0:T(8,128)S(1)} %copy-done.2), kind=kOutput, calls=%fused_computation.31 | convolution fusion | flops 805339136 | bytes 3407872 | tf_op jit(solution)/shard_map/dot_general | solution.py:18
  87.4 2.9 convolution_subtract_fusion.5
  90.4 44.0 %all-reduce.15.cloned.1.call-done = (f32[128,256]{1,0:T(8,128)}, f32[256,256]{1,0:T(8,128)}, f32[128,256]{1,0:T(8,128)}, f32[256,256]{1,0:T(8,128)}) async-done(((f32[128,256]{1,0:T(8,128)}, f32[256,256]{1,0:T(8,128)}, f32[128,256]{1,0:T(8,128)}, f32[256,256]{1,0:T(8,128)}), (f32[128,256]{1,0:T(8,128)}, f32[256,256]{1,0:T(8,128)}, f32[128,256]{1,0:T(8,128)}, ...) | async-done | bytes 786448 | tf_op jit(solution)/shard_map/psum | solution.py:78
  134.4 1.3 fusion.92
  135.7 1.3 fusion.96
  137.0 1.3 fusion.11
  138.3 2.8 fusion.98
  141.2 1.2 fusion.95
  142.8 1.3 fusion.2
  144.6 1.3 fusion.3
  145.9 1.0 fusion.97
  146.9 1.0 fusion.99
  147.9 1.6 convolution_subtract_fusion.23
  149.6 1.6 convolution_add_fusion.23
  151.5 33.6 %all-reduce.13.cloned.1.call-done = (f32[128,128]{1,0:T(8,128)}, f32[128,128]{1,0:T(8,128)}) async-done(((f32[128,128]{1,0:T(8,128)}, f32[128,128]{1,0:T(8,128)}), (f32[128,128]{1,0:T(8,128)}, f32[128,128]{1,0:T(8,128)})) %all-reduce.13.cloned.1.call-update) | async-done | bytes 131088 | tf_op jit(solution)/shard_map/psum | solution.py:88
  185.0 2.0 gather_fusion
  187.0 1.0 add_reduce_fusion.1
  189.4 1.6 multiply_reduce_fusion
  191.0 1.7 fusion.33
  192.9 1.7 fusion.87
  194.9 1.7 fusion.31
  196.6 1.7 fusion.85
  198.6 0.9 convolution_subtract_fusion.20
  199.5 0.9 convolution_add_fusion.20
  212.2 1.1 fusion.52
  213.3 1.1 fusion.56
  214.6 1.1 convolution_add_fusion.2
  215.7 1.1 convolution_subtract_fusion.2
  216.8 0.9 copy-done.7
  217.7 2.1 fusion.5
  219.8 1.9 fusion.4
  221.8 2.6 fusion.12
  224.3 2.6 fusion.13
  226.9 35.4 %all-reduce.11.cloned.1.call-done = (f32[256,128]{1,0:T(8,128)}, f32[256,128]{1,0:T(8,128)}) async-done(((f32[256,128]{1,0:T(8,128)}, f32[256,128]{1,0:T(8,128)}), (f32[256,128]{1,0:T(8,128)}, f32[256,128]{1,0:T(8,128)})) %all-reduce.11.cloned.1.call-update) | async-done | bytes 262160 | tf_op jit(solution)/shard_map/psum | solution.py:91
  262.3 3.1 %fusion.129 = f32[256,2048]{1,0:T(8,128)S(1)} fusion(f32[256,128]{1,0:T(8,128)} %get-tuple-element.21, f32[128,2048]{1,0:T(8,128)} %copy-done.13), kind=kOutput, calls=%fused_computation.189 | convolution fusion | flops 805306368 | bytes 3276800 | tf_op jit(solution)/shard_map/dot_general | solution.py:14
  265.5 1.8 fusion.128
  267.4 2.2 compare_select_fusion.1
  269.6 3.8 %add_reduce_fusion = (f32[256]{0:T(256)S(1)}, f32[256,2048]{1,0:T(8,128)}) fusion(f32[256,2048]{1,0:T(8,128)S(1)} %compare_select_fusion.1, f32[256,2048]{1,0:T(8,128)S(1)} %fusion.129, f32[256,128]{1,0:T(8,128)S(1)} %copy-done.20, f32[128,2048]{1,0:T(8,128)S(1)} %copy-done.12, f32[256,2048]{1,0:T(8,128)S(1)} %copy-done.10, s32[256]{0:T(256)S(1)} %get-tuple-element.20, ...), kind=kOutput, calls=%fused_computation.15 | convolution fusion | flops 810024704 | bytes 9578496 | tf_op jit(solution)/shard_map/dot_general | solution.py:14
  273.4 10.5 %psum.87 = f32[256]{0:T(256)S(1)} all-reduce(f32[256]{0:T(256)S(1)} %get-tuple-element.17), channel_id=1, replica_groups=mesh['wave'=8,'freq'=4] {'freq'}, use_global_device_ids=true, to_apply=%region_15.16 | all-reduce | flops 256 | bytes 2048 | tf_op jit(solution)/shard_map/psum | solution.py:96
  (130 shorter events, 17.0 us)
Async XLA Ops:
  7.2 7.0 %copy-start = (f32[256,2048]{1,0:T(8,128)S(1)}, f32[256,2048]{1,0:T(8,128)}, u32[]{:S(2)}) copy-start(f32[256,2048]{1,0:T(8,128)} %param.8) | copy-start | bytes 6291460
  7.2 4.7 %copy-start.26 = (s32[128]{0:T(128)S(1)}, s32[128]{0:T(128)}, u32[]{:S(2)}) copy-start(s32[128]{0:T(128)} %param.11) | copy-start | bytes 1540
  7.2 71.1 %all-reduce.9.cloned.1.call-start = ((), (), s32[]{:S(2)}) async-start(), calls=%async_computation | async-start | bytes 4194304 | tf_op jit(solution)/shard_map/psum | solution.py:75
  7.3 4.6 %copy-start.6 = (f32[256,2048]{1,0:T(8,128)S(1)}, f32[256,2048]{1,0:T(8,128)}, u32[]{:S(2)}) copy-start(f32[256,2048]{1,0:T(8,128)} %param.6) | copy-start | bytes 6291460
  13.9 120.4 %all-reduce.15.cloned.1.call-start = ((), (), s32[]{:S(2)}) async-start(), calls=%async_computation.3 | async-start | bytes 1572864 | tf_op jit(solution)/shard_map/psum | solution.py:78
  14.2 1.9 copy-start.1
  78.3 3.6 %copy-start.17 = (f32[128,2048]{1,0:T(8,128)S(1)}, f32[128,2048]{1,0:T(8,128)}, u32[]{:S(2)}) copy-start(f32[128,2048]{1,0:T(8,128)} %get-tuple-element.8) | copy-start | bytes 3145732
  81.9 2.3 copy-start.2
  84.1 3.3 %copy-start.15 = (f32[128,2048]{1,0:T(8,128)S(1)}, f32[128,2048]{1,0:T(8,128)}, u32[]{:S(2)}) copy-start(f32[128,2048]{1,0:T(8,128)} %get-tuple-element.7) | copy-start | bytes 3145732
  90.3 94.7 %all-reduce.13.cloned.1.call-start = ((), (), s32[]{:S(2)}) async-start(), calls=%async_computation.2 | async-start | bytes 262144 | tf_op jit(solution)/shard_map/psum | solution.py:88
  141.1 1.3 copy-start.22
  141.2 1.3 copy-start.23
  141.2 1.6 copy-start.18
  142.7 1.6 copy-start.3
  142.8 1.8 copy-start.16
  145.9 2.0 copy-start.4
  151.2 111.1 %all-reduce.11.cloned.1.call-start = ((), (), s32[]{:S(2)}) async-start(), calls=%async_computation.1 | async-start | bytes 524288 | tf_op jit(solution)/shard_map/psum | solution.py:91
  185.0 13.5 %copy-start.24 = (f32[128,128]{1,0:T(8,128)S(1)}, f32[128,128]{1,0:T(8,128)}, u32[]{:S(2)}) copy-start(f32[128,128]{1,0:T(8,128)} %get-tuple-element.12) | copy-start | bytes 196612
  210.3 3.0 %copy-start.5 = (f32[128,2048]{1,0:T(8,128)S(1)}, f32[128,2048]{1,0:T(8,128)}, u32[]{:S(2)}) copy-start(f32[128,2048]{1,0:T(8,128)} %copy-done.4) | copy-start | bytes 3145732
  215.7 6.0 %copy-start.13 = (f32[128,2048]{1,0:T(8,128)}, f32[128,2048]{1,0:T(8,128)S(1)}, u32[]{:S(2)}) copy-start(f32[128,2048]{1,0:T(8,128)S(1)} %convolution_add_fusion.2) | copy-start | bytes 3145732
  215.7 2.0 copy-start.7
  217.7 6.6 %copy-start.11 = (f32[128,2048]{1,0:T(8,128)}, f32[128,2048]{1,0:T(8,128)S(1)}, u32[]{:S(2)}) copy-start(f32[128,2048]{1,0:T(8,128)S(1)} %convolution_subtract_fusion.2) | copy-start | bytes 3145732
  219.8 1.9 copy-start.9
  226.9 38.6 %copy-start.12 = (f32[128,2048]{1,0:T(8,128)S(1)}, f32[128,2048]{1,0:T(8,128)}, u32[]{:S(2)}) copy-start(f32[128,2048]{1,0:T(8,128)} %copy-done.11) | copy-start | bytes 3145732
  262.3 3.2 %copy-start.21 = (f32[256,128]{1,0:T(8,128)S(1)}, f32[256,128]{1,0:T(8,128)}, u32[]{:S(2)}) copy-start(f32[256,128]{1,0:T(8,128)} %get-tuple-element.21) | copy-start | bytes 393220
  265.5 1.9 copy-start.8
  265.5 1.9 copy-start.14
  265.5 1.9 copy-start.20
  267.3 2.2 copy-start.10
  269.6 3.8 %copy-start.19 = (f32[256,2048]{1,0:T(8,128)}, f32[256,2048]{1,0:T(8,128)S(1)}, u32[]{:S(2)}) copy-start(f32[256,2048]{1,0:T(8,128)S(1)} %compare_select_fusion.1) | copy-start | bytes 6291460
  269.6 14.3 %copy-start.25 = (s32[256]{0:T(256)S(1)}, s32[256]{0:T(256)}, u32[]{:S(2)}) copy-start(s32[256]{0:T(256)} %param.10) | copy-start | bytes 3076
Sparse Core Ops, SparseCore 0:
  14.1 64.2 all-reduce.8
  90.4 43.8 all-reduce.14
  151.3 33.6 all-reduce.12
  227.0 35.2 all-reduce.10
where the time goes:
time: 296 us; the launch traced here: 293 us
  waiting for transfers between devices  168 us (57%)
  matrix products  88.1 us (30%)
  between operations  15.7 us (5%)
  blocking collectives  10.5 us (4%)
  local copies, waits for them, and re-layouts  4.84 us (2%)
  other arithmetic  4.7 us (2%)
    psum x1, waiting for transfers between devices, body(): pivot_re, pivot_im = lax.psum((picked_re, picked_im), 'wave')  55.2 us
    dot_general x84, matrix products, plain(): jnp.dot(left, right, precision=lax.Precision.HIGHEST, preferred_element_t...  52.8 us
    psum x1, waiting for transfers between devices, body(): lax.psum((cross_re, cross_im, basis_gram_re, basis_gram_im), 'freq')  44 us
    psum x1, waiting for transfers between devices, body(): coef_re, coef_im = lax.psum((coef_re, coef_im), 'freq')  35.4 us
    dot_general x16, matrix products, against(): lax.dot_general(left, right, (((1,), (1,)), ((), ())), precision=lax.Prec...  35.2 us
    psum x1, waiting for transfers between devices, body(): gram_re, gram_im = lax.psum((gram_re, gram_im), 'freq')  33.6 us
    psum x1, blocking collectives, body(): summed_sq = lax.psum(partial_sq, 'freq')  10.5 us
  transfers between devices with their start and end apart: 4, of which 4 were waited for; matrix products, arithmetic and copies ran while one was open for 3% of the time, Pallas kernels for 0%

commit v1 on v0

v1 whole, which is shorter than its diff:
```python
import functools
import math

import jax
import jax.numpy as jnp
from jax import lax
from jax.experimental import pallas as pl
from jax.experimental.pallas import tpu as pltpu
from jax.sharding import PartitionSpec as P

BIN_BLOCK = 128
NS_STEPS = 6
epsilon = 1e-06
F32 = jnp.float32
BF16 = jnp.bfloat16
VMEM_LIMIT = 56 * 1024 * 1024

ANY = pl.BlockSpec(memory_space=pl.ANY)
SMEM = pl.BlockSpec(memory_space=pltpu.SMEM)
VMEM = pl.BlockSpec(memory_space=pltpu.VMEM)


def params():
    return pltpu.CompilerParams(vmem_limit_bytes=VMEM_LIMIT)


def up(value, step):
    return -(-value // step) * step


def swap(array, axis, size, distance):
    return lax.ppermute(array, axis, [(i, i ^ distance) for i in range(size)])


def split(value):
    high = value.astype(BF16)
    low = (value - high.astype(F32)).astype(BF16)
    return high, low


def split3(value):
    high = value.astype(BF16)
    rest = value - high.astype(F32)
    middle = rest.astype(BF16)
    low = (rest - middle.astype(F32)).astype(BF16)
    return high, middle, low


def nn(left, right):
    return jnp.dot(left, right, preferred_element_type=F32)


def nt(left, right):
    return lax.dot_general(left, right, (((1,), (1,)), ((), ())), preferred_element_type=F32)


def nn3(left, right):
    return nn(left[0], right[0]) + (nn(left[0], right[1]) + nn(left[1], right[0]))


def nt3(left, right):
    return nt(left[0], right[0]) + (nt(left[0], right[1]) + nt(left[1], right[0]))


def pick_kernel(cap, piv, lens, meta, re, im, out, where, rows_re, rows_im, sem):
    wave_rows, cols = re.shape
    base = meta[0] * wave_rows
    first_bin = meta[1] * cols
    skip = meta[2]

    def clear(slot, carry):
        where[slot] = -1
        return carry

    lax.fori_loop(0, rows_re.shape[0], clear, 0)

    def look(i, seen):
        row = piv[i] - base
        own = (row >= 0) & (row < wave_rows)
        slot = seen - skip

        @pl.when(own & (slot >= 0) & (slot < cap))
        def _():
            where[slot] = row

        return seen + own.astype(jnp.int32)

    lax.fori_loop(0, piv.shape[0], look, 0)

    def copies(slot):
        row = jnp.maximum(where[slot], 0)
        return (
            pltpu.make_async_copy(re.at[pl.ds(row, 1)], rows_re.at[pl.ds(slot, 1)], sem.at[0]),
            pltpu.make_async_copy(im.at[pl.ds(row, 1)], rows_im.at[pl.ds(slot, 1)], sem.at[1]),
        )

    def start(slot, carry):
        for copy in copies(slot):
            copy.start()
        return carry

    slots = rows_re.shape[0]
    lax.fori_loop(0, slots, start, 0)
    pltpu.make_async_copy(re.at[pl.ds(0, slots)], rows_re, sem.at[0]).wait()
    pltpu.make_async_copy(im.at[pl.ds(0, slots)], rows_im, sem.at[1]).wait()
    bins = lax.broadcasted_iota(jnp.int32, (1, cols), 1) + first_bin

    for slot in range(cap):
        row = where[slot]
        live = jnp.where(row >= 0, lens[jnp.maximum(row, 0)], 0) * BIN_BLOCK
        keep = bins < live
        out[slot : slot + 1, :] = jnp.where(keep, rows_re[slot : slot + 1, :], 0.0)
        out[cap + slot : cap + slot + 1, :] = jnp.where(keep, rows_im[slot : slot + 1, :], 0.0)


def pick(cap, pivots, lengths, meta, res_re, res_im):
    cols = res_re.shape[1]
    return pl.pallas_call(
        functools.partial(pick_kernel, cap),
        out_shape=jax.ShapeDtypeStruct((2 * cap, cols), F32),
        in_specs=[SMEM, SMEM, SMEM, ANY, ANY],
        out_specs=VMEM,
        scratch_shapes=[
            pltpu.SMEM((up(cap, 8),), jnp.int32),
            pltpu.VMEM((up(cap, 8), cols), F32),
            pltpu.VMEM((up(cap, 8), cols), F32),
            pltpu.SemaphoreType.DMA((2,)),
        ],
        compiler_params=params(),
        name="pick",
    )(pivots, lengths, meta, res_re, res_im)


def cross_kernel(cap, meta, rows, b_re, b_im, out):
    nb, cols = b_re.shape
    mine = out.shape[0] - up(cap, 8)
    start = pl.multiple_of(meta[0] * mine, mine)
    chunk = min(cols, 512)
    total = jnp.zeros((2 * cap + 2 * mine, 2 * nb), F32)
    for at in range(0, cols, chunk):
        part = pl.ds(at, chunk)
        left = split(
            jnp.concatenate([rows[:, part], b_re[pl.ds(start, mine), part], b_im[pl.ds(start, mine), part]], axis=0)
        )
        right = split(jnp.concatenate([b_re[:, part], b_im[:, part]], axis=0))
        total += nt3(left, right)

    def join(at, size):
        real, imag = total[at : at + size], total[at + size : at + 2 * size]
        return jnp.concatenate([real[:, :nb] + imag[:, nb:], imag[:, :nb] - real[:, nb:]], axis=1)

    out[...] = jnp.zeros_like(out)
    out[0:cap, :] = join(0, cap)
    out[up(cap, 8) :, :] = join(2 * cap, mine)


def cross(cap, mine, meta, rows, basis_re, basis_im):
    nb = basis_re.shape[0]
    return pl.pallas_call(
        functools.partial(cross_kernel, cap),
        out_shape=jax.ShapeDtypeStruct((up(cap, 8) + mine, 2 * nb), F32),
        in_specs=[SMEM, VMEM, VMEM, VMEM],
        out_specs=VMEM,
        compiler_params=params(),
        name="cross",
    )(meta, rows, basis_re, basis_im)


def parts_kernel(re, im, lens, meta, high, low):
    cols = re.shape[1]
    rows = re.shape[0]
    bins = lax.broadcasted_iota(jnp.int32, (1, cols), 1) + meta[1] * cols
    keep = bins < lens[...] * BIN_BLOCK
    for at, ref in ((0, re), (rows, im)):
        high_part, low_part = split(jnp.where(keep, ref[...], 0.0))
        high[at : at + rows, :] = high_part
        low[at : at + rows, :] = low_part


def parts(res_re, res_im, lens, meta):
    rows, cols = res_re.shape
    shape = jax.ShapeDtypeStruct((2 * rows, cols), BF16)
    return pl.pallas_call(
        parts_kernel,
        out_shape=(shape, shape),
        in_specs=[VMEM, VMEM, VMEM, SMEM],
        out_specs=(VMEM, VMEM),
        compiler_params=params(),
        name="parts",
    )(res_re, res_im, lens, meta)


def ranks(pivots_col, pivots_row, wave_rows):
    count = pivots_col.shape[0]
    owner_col = pivots_col // wave_rows
    owner_row = pivots_row // wave_rows
    i = lax.broadcasted_iota(jnp.int32, (count, count), 0)
    j = lax.broadcasted_iota(jnp.int32, (count, count), 1)
    ahead = (owner_col == owner_row) & (j < i)
    return owner_col, jnp.sum(ahead.astype(jnp.int32), axis=1, keepdims=True)


def one_hot(index, width):
    return (lax.broadcasted_iota(jnp.int32, (index.shape[0], width), 1) == index).astype(F32).astype(BF16)


def project_kernel(cap, nw, nf, places, n_cross, meta, pc, pr, extra_p, extra_c, b_re, b_im, r_high, r_low, *refs):
    list_refs, refs = refs[: len(places)], refs[len(places) :]
    cross_refs, refs = refs[:n_cross], refs[n_cross:]
    p_out, g_out, refs = refs[0], refs[1], refs[2:]
    d_out, refs = refs[:nf], refs[nf:]
    gathered, crossed, gram_b, basis, left_high, left_low, more_p, more_c, d_all, sem_l, sem_c, sem_b, sem_x = refs
    count = pc.shape[0]
    nb, cols = b_re.shape
    waves = r_high.shape[0] // 2
    capp = up(cap, 8)
    mine = nb // nw
    me_w, me_f, over = meta[0], meta[1], meta[3]

    def move(source, target, sem):
        copy = pltpu.make_async_copy(source, target, sem)
        copy.start()
        return copy

    waits = []
    for k, ref in enumerate(cross_refs):
        waits.append(move(ref.at[pl.ds(0, capp)], crossed.at[pl.ds(k * capp, capp)], sem_c.at[2 * k]))
        place = pl.multiple_of((me_w ^ k) * mine, mine)
        waits.append(move(ref.at[pl.ds(capp, mine)], gram_b.at[pl.ds(place, mine)], sem_c.at[2 * k + 1]))
    list_waits = []
    for index, ((k, col), ref) in enumerate(zip(places, list_refs)):
        target = gathered.at[pl.ds(k * 2 * cap, 2 * cap), pl.ds(col, ref.shape[1])]
        list_waits.append(move(ref, target, sem_l.at[index]))
    basis_waits = [
        move(b_re, basis.at[pl.ds(0, nb)], sem_b.at[0]),
        move(b_im, basis.at[pl.ds(nb, nb)], sem_b.at[1]),
    ]
    left_waits = [
        move(r_high, left_high, sem_b.at[2]),
        move(r_low, left_low, sem_b.at[3]),
    ]

    @pl.when(over > 0)
    def _():
        first = pltpu.make_async_copy(extra_p, more_p, sem_x.at[0])
        second = pltpu.make_async_copy(extra_c, more_c, sem_x.at[1])
        first.start()
        second.start()
        first.wait()
        second.wait()

    owner, rank = ranks(pc[...], pr[...], waves)
    held = rank < cap
    group = jnp.bitwise_xor(owner, me_w)
    nowhere = jnp.full_like(rank, -1)
    at_re = jnp.where(held, group * (2 * cap) + rank, nowhere)
    at_im = jnp.where(held, group * (2 * cap) + cap + rank, nowhere)
    at_c = jnp.where(held, group * capp + rank, nowhere)
    select = one_hot(jnp.concatenate([at_re, at_im], axis=0), nw * 2 * cap)
    select_c = one_hot(at_c, nw * capp)

    for copy in waits:
        copy.wait()
    pieces = split3(crossed[...])
    cross_all = nn(select_c, pieces[0]) + (nn(select_c, pieces[1]) + nn(select_c, pieces[2]))
    cross_all = cross_all + jnp.where(over > 0, more_c[...], 0.0)
    stacked = jnp.concatenate([cross_all[:, :nb], cross_all[:, nb:]], axis=0)
    twist = nn3(split(stacked), split(gram_b[...]))
    total_re = 2.0 * cross_all[:, :nb] - (twist[:count, :nb] - twist[count:, nb:])
    total_im = 2.0 * cross_all[:, nb:] - (twist[:count, nb:] + twist[count:, :nb])
    take = split(
        jnp.concatenate(
            [jnp.concatenate([total_re, -total_im], axis=1), jnp.concatenate([total_im, total_re], axis=1)], axis=0
        )
    )

    for copy in list_waits:
        copy.wait()
    for copy in basis_waits:
        copy.wait()
    for copy in left_waits:
        copy.wait()
    chunk = min(cols, 512)
    inner_r = jnp.zeros((2 * waves, 2 * count), F32)
    inner_p = jnp.zeros((2 * count, 2 * count), F32)
    for begin in range(0, cols, chunk):
        part = pl.ds(begin, chunk)
        high, low = split(gathered[:, part])
        block = nn(select, high) + nn(select, low)
        block = block + jnp.where(over > 0, more_p[:, part], 0.0)
        block = block - nn3(take, split(basis[:, part]))
        p_out[:, part] = block
        right = split(block)
        inner_p += nt3(right, right)
        inner_r += nt3((left_high[:, part], left_low[:, part]), right)

    gram_re = inner_p[:count, :count] + inner_p[count:, count:]
    gram_im = inner_p[count:, :count] - inner_p[:count, count:]
    i = lax.broadcasted_iota(jnp.int32, (count, count), 0)
    j = lax.broadcasted_iota(jnp.int32, (count, count), 1)
    g_out[...] = jnp.where(i <= j, gram_re, gram_im)
    d_all[:, :count] = inner_r[:waves, :count] + inner_r[waves:, count:]
    d_all[:, count:] = inner_r[waves:, :count] - inner_r[:waves, count:]
    share = waves // nf
    for k in range(nf):
        d_out[k][...] = d_all[pl.ds(pl.multiple_of((me_f ^ k) * share, share), share), :]


def project(cap, nw, nf, places, meta, pivots, extra_p, extra_c, basis_re, basis_im, r_high, r_low, lists, crosses):
    count = pivots.shape[0]
    nb, cols = basis_re.shape
    waves = r_high.shape[0] // 2
    capp = up(cap, 8)
    shapes = [
        jax.ShapeDtypeStruct((2 * count, cols), F32),
        jax.ShapeDtypeStruct((count, count), F32),
    ] + [jax.ShapeDtypeStruct((waves // nf, 2 * count), F32)] * nf
    return pl.pallas_call(
        functools.partial(project_kernel, cap, nw, nf, places, len(crosses)),
        out_shape=shapes,
        in_specs=[SMEM, VMEM, VMEM] + [ANY] * (6 + len(lists) + len(crosses)),
        out_specs=[VMEM] * len(shapes),
        scratch_shapes=[
            pltpu.VMEM((nw * 2 * cap, cols), F32),
            pltpu.VMEM((nw * capp, 2 * nb), F32),
            pltpu.VMEM((nb, 2 * nb), F32),
            pltpu.VMEM((2 * nb, cols), F32),
            pltpu.VMEM((2 * waves, cols), BF16),
            pltpu.VMEM((2 * waves, cols), BF16),
            pltpu.VMEM((2 * count, cols), F32),
            pltpu.VMEM((count, 2 * nb), F32),
            pltpu.VMEM((waves, 2 * count), F32),
            pltpu.SemaphoreType.DMA((len(lists),)),
            pltpu.SemaphoreType.DMA((2 * len(crosses),)),
            pltpu.SemaphoreType.DMA((4,)),
            pltpu.SemaphoreType.DMA((2,)),
        ],
        compiler_params=params(),
        name="project",
    )(
        meta,
        pivots.reshape(count, 1),
        pivots.reshape(1, count),
        extra_p,
        extra_c,
        basis_re,
        basis_im,
        r_high,
        r_low,
        *lists,
        *crosses,
    )


def whiten_kernel(nf, *refs):
    packed = refs[0][...]
    for ref in refs[1:nf]:
        packed = packed + ref[...]
    out = refs[nf]
    count = packed.shape[0]
    i = lax.broadcasted_iota(jnp.int32, (count, count), 0)
    j = lax.broadcasted_iota(jnp.int32, (count, count), 1)
    upper = jnp.where(i <= j, packed, 0.0)
    lower = jnp.where(i > j, packed, 0.0)
    diagonal = jnp.where(i == j, packed, 0.0)
    gram_re = upper + upper.T - diagonal
    gram_im = lower - lower.T
    scale_row = 1.0 / jnp.sqrt(jnp.sum(diagonal, axis=0, keepdims=True) + epsilon)
    scale_col = 1.0 / jnp.sqrt(jnp.sum(diagonal, axis=1, keepdims=True) + epsilon)
    outer = scale_col * scale_row
    gram_re = gram_re * outer
    gram_im = gram_im * outer
    bound = jnp.max(jnp.sum(jnp.abs(gram_re) + jnp.abs(gram_im), axis=1, keepdims=True), axis=0, keepdims=True)
    gram_re = gram_re / bound
    gram_im = gram_im / bound
    mix = jnp.concatenate(
        [jnp.concatenate([gram_re, gram_im], axis=1), jnp.concatenate([-gram_im, gram_re], axis=1)], axis=0
    )
    i = lax.broadcasted_iota(jnp.int32, (2 * count, 2 * count), 0)
    j = lax.broadcasted_iota(jnp.int32, (2 * count, 2 * count), 1)
    ident = jnp.where(i == j, 1.0, 0.0).astype(F32)
    zed = None
    for step in range(NS_STEPS):
        turn = 1.5 * ident - 0.5 * mix
        turn_parts = split(turn)
        zed = turn if zed is None else nn3(turn_parts, split(zed))
        if step < NS_STEPS - 1:
            mix = nn3(split(nn3(split(mix), turn_parts)), turn_parts)
    out[...] = zed * (1.0 / jnp.sqrt(bound)) * jnp.concatenate([scale_row, scale_row], axis=1)


def whiten(grams):
    count = grams[0].shape[0]
    return pl.pallas_call(
        functools.partial(whiten_kernel, len(grams)),
        out_shape=jax.ShapeDtypeStruct((2 * count, 2 * count), F32),
        in_specs=[VMEM] * len(grams),
        out_specs=VMEM,
        compiler_params=params(),
        name="whiten",
    )(*grams)


def update_kernel(nf, meta, lens, whitener, p, re, im, *refs):
    pieces, refs = refs[:nf], refs[nf:]
    coef_re, coef_im, new_re, new_im, squares, d_all, back_high, back_low, sums = refs
    waves, chunk = re.shape
    count = coef_re.shape[1]
    step = pl.program_id(0)
    share = waves // nf

    @pl.when(step == 0)
    def _():
        for k in range(nf):
            place = pl.multiple_of((meta[1] ^ k) * share, share)
            d_all[pl.ds(place, share), :] = pieces[k][...]
        turn = split(whitener[...])
        coef = nt3(split(d_all[...]), turn)
        coef_re[...] = coef[:, :count]
        coef_im[...] = coef[:, count:]
        back = nn3(split(coef), turn)
        back_re, back_im = back[:, :count], back[:, count:]
        high, low = split(
            jnp.concatenate(
                [jnp.concatenate([back_re, -back_im], axis=1), jnp.concatenate([back_im, back_re], axis=1)], axis=0
            )
        )
        back_high[...] = high
        back_low[...] = low
        sums[...] = jnp.zeros_like(sums)

    change = nn3((back_high[...], back_low[...]), split(p[...]))
    first = meta[1] * (chunk * pl.num_programs(0)) + step * chunk
    bins = lax.broadcasted_iota(jnp.int32, (1, chunk), 1) + first
    keep = bins < lens[...] * BIN_BLOCK
    now_re = jnp.where(keep, re[...] - change[:waves], 0.0)
    now_im = jnp.where(keep, im[...] - change[waves:], 0.0)
    new_re[...] = now_re
    new_im[...] = now_im
    square = now_re * now_re + now_im * now_im
    total = square[:, :128]
    for at in range(128, chunk, 128):
        total = total + square[:, at : at + 128]
    sums[...] += total

    @pl.when(step == pl.num_programs(0) - 1)
    def _():
        squares[...] = jnp.sum(sums[...].T, axis=0, keepdims=True)


def update(nf, meta, lens, whitener, p, res_re, res_im, pieces):
    waves, cols = res_re.shape
    count = p.shape[0] // 2
    share = waves // nf
    chunk = min(cols, 512)
    whole = lambda *shape: pl.BlockSpec(shape, lambda s: (0,) * len(shape))
    block = pl.BlockSpec((waves, chunk), lambda s: (0, s))
    return pl.pallas_call(
        functools.partial(update_kernel, nf),
        grid=(cols // chunk,),
        out_shape=[
            jax.ShapeDtypeStruct((waves, count), F32),
            jax.ShapeDtypeStruct((waves, count), F32),
            jax.ShapeDtypeStruct((waves, cols), F32),
            jax.ShapeDtypeStruct((waves, cols), F32),
            jax.ShapeDtypeStruct((1, waves), F32),
        ],
        in_specs=[
            SMEM,
            whole(waves, 1),
            whole(2 * count, 2 * count),
            pl.BlockSpec((2 * count, chunk), lambda s: (0, s)),
            block,
            block,
        ]
        + [whole(share, 2 * count)] * nf,
        out_specs=[whole(waves, count), whole(waves, count), block, block, whole(1, waves)],
        scratch_shapes=[
            pltpu.VMEM((waves, 2 * count), F32),
            pltpu.VMEM((2 * waves, 2 * count), BF16),
            pltpu.VMEM((2 * waves, 2 * count), BF16),
            pltpu.VMEM((waves, 128), F32),
        ],
        compiler_params=params(),
        name="update",
    )(meta, lens, whitener, p, res_re, res_im, *pieces)


def spread(rows, nw):
    half = rows.shape[1] // 2
    found = [(0, 0, rows)]
    if nw == 8:
        by_two = swap(rows, "wave", nw, 2)
        by_four = swap(rows, "wave", nw, 4)
        found.append((2, 0, by_two))
        found.append((4, 0, by_four))
        found.append((6, 0, swap(by_two[:, :half], "wave", nw, 4)))
        found.append((6, half, swap(by_four[:, half:], "wave", nw, 2)))
    else:
        found += [(k, 0, swap(rows, "wave", nw, k)) for k in range(2, nw, 2)]
    return found + [(k + 1, col, swap(array, "wave", nw, 1)) for k, col, array in found]


def spread_small(rows, nw):
    found = [rows] + [swap(rows, "wave", nw, k) for k in range(2, nw, 2)]
    both = []
    for array in found:
        both += [array, swap(array, "wave", nw, 1)]
    return both


def sum_over_freq(array, nf):
    return sum([swap(array, "freq", nf, k) for k in range(1, nf)], array)


def capacity(count, nw, rows):
    mean = count / nw
    return min(up(math.ceil(mean + 3.0 * math.sqrt(mean)), 4), count, rows)


def body(nw, nf, res_re, res_im, basis_re, basis_im, lengths, pivots):
    waves, cols = res_re.shape
    nb = basis_re.shape[0]
    count = pivots.shape[0]
    cap = capacity(count, nw, waves)
    capp = up(cap, 8)
    mine = nb // nw
    me_w = lax.axis_index("wave").astype(jnp.int32)
    me_f = lax.axis_index("freq").astype(jnp.int32)
    zero = jnp.zeros((), jnp.int32)
    lens = lengths.reshape(waves, 1)
    owners = pivots // waves
    counts = jnp.sum((owners[:, None] == jnp.arange(nw, dtype=jnp.int32)[None, :]).astype(jnp.int32), axis=0)
    rounds = (jnp.max(counts) + cap - 1) // cap

    rows = pick(cap, pivots, lengths, jnp.stack([me_w, me_f, zero, zero]), res_re, res_im)
    found = spread(rows, nw)
    meta = jnp.stack([me_w, me_f, zero, (rounds > 1).astype(jnp.int32)])
    partial = cross(cap, mine, meta, rows, basis_re, basis_im)
    crosses = spread_small(sum_over_freq(partial, nf), nw)
    r_high, r_low = parts(res_re, res_im, lens, meta)

    def another(carry):
        turn, extra_p, extra_c = carry
        more = pick(cap, pivots, lengths, jnp.stack([me_w, me_f, turn * cap, zero]), res_re, res_im)
        more_c = lax.psum(cross(cap, mine, meta, more, basis_re, basis_im)[:cap], "freq")
        all_p = lax.all_gather(more, "wave")
        all_c = lax.all_gather(more_c, "wave")
        rank = jnp.sum(
            ((owners[:, None] == owners[None, :]) & (jnp.arange(count)[None, :] < jnp.arange(count)[:, None])).astype(
                jnp.int32
            ),
            axis=1,
        ) - turn * cap
        slot = jnp.where((rank >= 0) & (rank < cap), owners * cap + rank, -1)
        chosen = (slot[:, None] == jnp.arange(nw * cap)[None, :]).astype(F32)
        place = lambda table: jnp.dot(chosen, table, precision=lax.Precision.HIGHEST, preferred_element_type=F32)
        added = jnp.concatenate(
            [place(all_p[:, :cap].reshape(nw * cap, cols)), place(all_p[:, cap:].reshape(nw * cap, cols))], axis=0
        )
        return turn + 1, extra_p + added, extra_c + place(all_c.reshape(nw * cap, 2 * nb))

    _, extra_p, extra_c = lax.while_loop(
        lambda carry: carry[0] < rounds,
        another,
        (jnp.ones((), jnp.int32), jnp.zeros((2 * count, cols), F32), jnp.zeros((count, 2 * nb), F32)),
    )

    places = tuple((k, col) for k, col, _ in found)
    p, gram, *pieces = project(
        cap,
        nw,
        nf,
        places,
        meta,
        pivots,
        extra_p,
        extra_c,
        basis_re,
        basis_im,
        r_high,
        r_low,
        [array for _, _, array in found],
        crosses,
    )
    piece = sum([swap(pieces[k], "freq", nf, k) for k in range(1, nf)], pieces[0])
    grams = [gram] + [swap(gram, "freq", nf, k) for k in range(1, nf)]
    every = [piece] + [swap(piece, "freq", nf, k) for k in range(1, nf)]
    whitener = whiten(grams)
    coef_re, coef_im, new_re, new_im, squares = update(nf, meta, lens, whitener, p, res_re, res_im, every)
    errors = sum_over_freq(squares, nf).reshape(waves) / (BIN_BLOCK * lengths).astype(F32)
    return coef_re, coef_im, new_re, new_im, errors


def solution(mesh):
    nw, nf = mesh.shape["wave"], mesh.shape["freq"]
    return jax.shard_map(
        functools.partial(body, nw, nf),
        mesh=mesh,
        in_specs=(P("wave", "freq"), P("wave", "freq"), P(None, "freq"), P(None, "freq"), P("wave"), P()),
        out_specs=(P("wave", None), P("wave", None), P("wave", "freq"), P("wave", "freq"), P("wave")),
        check_vma=False,
    )
```

time: 296 us -> 120 us (0.41)
  waiting for transfers between devices: 168 us -> 14.1 us
  matrix products: 88.1 us -> 0 us
  Pallas kernels: 0 us -> 39.3 us
  starting transfers between devices: 0.51 us -> 38.4 us
  blocking collectives: 10.5 us -> 0 us
    psum x4 -> x0, waiting for transfers between devices: 168 us -> none  [the longest x1 55.2 us: body(): pivot_re, pivot_im = lax.psum((picked_re, picked_im), 'wave')]
    dot_general x100 -> x0, matrix products: 88.1 us -> none  [the longest x84 52.8 us: plain(): jnp.dot(left, right, precision=lax.Precision.HIGHEST, preferred_element_t...]
    pallas_call x0 -> x6, Pallas kernels: none -> 39.3 us  [the longest x1 13.5 us: project(): pl.pallas_call(functools.partial(project_kernel, cap, nw, nf, places, len...]
    ppermute x0 -> x31, starting transfers between devices: none -> 38.4 us  [swap(): return lax.ppermute(array, axis, [(i, i ^ distance) for i in range(size)])]
    ppermute x0 -> x31, waiting for transfers between devices: none -> 14.1 us  [swap(): return lax.ppermute(array, axis, [(i, i ^ distance) for i in range(size)])]
    psum x1 -> x0, blocking collectives: 10.5 us -> none  [body(): summed_sq = lax.psum(partial_sq, 'freq')]
  transfers between devices with their start and end apart: 4 -> 31, of which waited for: 4 -> 9; matrix products, arithmetic and copies ran while one was open for 3% -> 6% of each run, Pallas kernels for 0% -> 8%
where the time goes in v1:
time: 120 us; the launch traced here: 119 us
  Pallas kernels  39.3 us (33%)
  starting transfers between devices  38.4 us (32%)
  between operations  15 us (12%)
  waiting for transfers between devices  14.1 us (12%)
  local copies, waits for them, and re-layouts  6.97 us (6%)
  other arithmetic  5.3 us (4%)
    ppermute x31, starting transfers between devices, swap(): return lax.ppermute(array, axis, [(i, i ^ distance) for i in range(size)])  38.4 us
    ppermute x31, waiting for transfers between devices, swap(): return lax.ppermute(array, axis, [(i, i ^ distance) for i in range(size)])  14.1 us
    pallas_call x1, Pallas kernels, project(): pl.pallas_call(functools.partial(project_kernel, cap, nw, nf, places, len...  13.5 us
    pallas_call x1, Pallas kernels, update(): pl.pallas_call(functools.partial(update_kernel, nf), grid=(cols // chunk,...  6.58 us
    pallas_call x1, Pallas kernels, pick(): pl.pallas_call(functools.partial(pick_kernel, cap), out_shape=jax.ShapeDt...  5.12 us
    pallas_call x1, Pallas kernels, whiten(): pl.pallas_call(functools.partial(whiten_kernel, len(grams)), out_shape=ja...  5.08 us
    pallas_call x1, Pallas kernels, parts(): pl.pallas_call(parts_kernel, out_shape=(shape, shape), in_specs=[VMEM, VM...  4.98 us
    pallas_call x1, Pallas kernels, cross(): pl.pallas_call(functools.partial(cross_kernel, cap), out_shape=jax.ShapeD...  4.04 us
  transfers between devices with their start and end apart: 31, of which 9 were waited for; matrix products, arithmetic and copies ran while one was open for 6% of the time, Pallas kernels for 8%

profile of v1, /device:TPU:0, one launch (start us, length us, event | category | flops | bytes accessed | tf_op | source)
XLA Modules:
  0.0 119.2 jit_solution(17859450756150383323)
XLA Ops:
  7.2 0.7 and_select_fusion.1
  7.9 0.6 reduce_max.9
  9.3 0.6 pad_add_fusion.3.meta
  9.9 5.1 %pick.2.rows.refs_0_ = f32[56,2048]{1,0:T(8,128)} custom-call(s32[128]{0:T(128)} %piv.1, s32[256]{0:T(256)} %lens.1, s32[4]{0:T(128)} %pad_add_fusion.3.meta, f32[256,2048]{1,0:T(8,128)} %re.5, f32[256,2048]{1,0:T(8,128)} %im.5), custom_call_target="tpu_custom_call" | custom-call | tf_op jit(solution)/shard_map/pick/pallas_call | solution.py:118
  15.1 4.0 %cross.3 = f32[64,512]{1,0:T(8,128)} custom-call(s32[4]{0:T(128)S(1)} %pad_add_fusion.1.meta, f32[56,2048]{1,0:T(8,128)} %pick.2.rows.refs_0_, f32[256,2048]{1,0:T(8,128)S(1)} %copy-done.5, f32[256,2048]{1,0:T(8,128)S(1)} %copy-done.6), custom_call_target="tpu_custom_call" | custom-call | tf_op jit(solution)/shard_map/cross/pallas_call | solution.py:159
  19.2 4.0 %collective-permute-start.10 = (f32[64,512]{1,0:T(8,128)}, f32[64,512]{1,0:T(8,128)S(1)}, u32[]{:S(2)}, u32[]{:S(2)}) collective-permute-start(f32[64,512]{1,0:T(8,128)} %cross.3), channel_id=1, source_target_pairs={{0,2},{1,3},{2,0},{3,1},{4,6},{5,7},{6,4},{7,5},{8,10},{9,11},{10,... | collective-permute-start | bytes 393224 | tf_op jit(solution)/shard_map/ppermute | solution.py:32
  23.2 1.3 %collective-permute-start.11 = (f32[64,512]{1,0:T(8,128)}, f32[64,512]{1,0:T(8,128)S(1)}, u32[]{:S(2)}, u32[]{:S(2)}) collective-permute-start(f32[64,512]{1,0:T(8,128)} %cross.3), channel_id=1, source_target_pairs={{0,3},{1,2},{2,1},{3,0},{4,7},{5,6},{6,5},{7,4},{8,11},{9,10},{10,... | collective-permute-start | bytes 393224 | tf_op jit(solution)/shard_map/ppermute | solution.py:32
  24.8 1.4 %collective-permute-start = (f32[56,2048]{1,0:T(8,128)}, f32[56,2048]{1,0:T(8,128)}, u32[]{:S(2)}, u32[]{:S(2)}) collective-permute-start(f32[56,2048]{1,0:T(8,128)} %pick.2.rows.refs_0_), channel_id=1, source_target_pairs={{0,8},{4,12},{8,0},{12,4},{16,24},{20,28},{24,16},{28,20},{1,9},{5... | collective-permute-start | bytes 1376264 | tf_op jit(solution)/shard_map/ppermute | solution.py:32
  26.2 1.5 %collective-permute-start.1 = (f32[56,2048]{1,0:T(8,128)}, f32[56,2048]{1,0:T(8,128)}, u32[]{:S(2)}, u32[]{:S(2)}) collective-permute-start(f32[56,2048]{1,0:T(8,128)} %pick.2.rows.refs_0_), channel_id=1, source_target_pairs={{0,16},{4,20},{8,24},{12,28},{16,0},{20,4},{24,8},{28,12},{1,17},{... | collective-permute-start | bytes 1376264 | tf_op jit(solution)/shard_map/ppermute | solution.py:32
  27.6 5.7 %collective-permute-done.10 = f32[64,512]{1,0:T(8,128)S(1)} collective-permute-done((f32[64,512]{1,0:T(8,128)}, f32[64,512]{1,0:T(8,128)S(1)}, u32[]{:S(2)}, u32[]{:S(2)}) %collective-permute-start.10) | collective-permute-done | bytes 131104 | tf_op jit(solution)/shard_map/ppermute | solution.py:32
  33.4 0.4 collective-permute-done.9
  33.8 0.9 add_add_fusion.refs_10_
  34.7 1.7 %collective-permute-start.13 = (f32[64,512]{1,0:T(8,128)S(1)}, f32[64,512]{1,0:T(8,128)S(1)}, u32[]{:S(2)}, u32[]{:S(2)}) collective-permute-start(f32[64,512]{1,0:T(8,128)S(1)} %add_add_fusion.refs_10_), channel_id=1, source_target_pairs={{0,8},{4,12},{8,0},{12,4},{16,24},{20,28},{24,16},{28,20},{1,9},{5... | collective-permute-start | bytes 393224 | tf_op jit(solution)/shard_map/ppermute | solution.py:32
  36.4 1.4 %collective-permute-start.15 = (f32[64,512]{1,0:T(8,128)S(1)}, f32[64,512]{1,0:T(8,128)S(1)}, u32[]{:S(2)}, u32[]{:S(2)}) collective-permute-start(f32[64,512]{1,0:T(8,128)S(1)} %add_add_fusion.refs_10_), channel_id=1, source_target_pairs={{0,16},{4,20},{8,24},{12,28},{16,0},{20,4},{24,8},{28,12},{1,17},{... | collective-permute-start | bytes 393224 | tf_op jit(solution)/shard_map/ppermute | solution.py:32
  37.8 0.5 collective-permute-start.17
  38.3 1.0 slice.23
  39.2 0.7 collective-permute-done.1.refs_2_
  39.9 2.2 %collective-permute-start.2 = (f32[56,1024]{1,0:T(8,128)S(1)}, f32[56,1024]{1,0:T(8,128)}, u32[]{:S(2)}, u32[]{:S(2)}) collective-permute-start(f32[56,1024]{1,0:T(8,128)S(1)} %slice.23), channel_id=1, source_target_pairs={{0,16},{4,20},{8,24},{12,28},{16,0},{20,4},{24,8},{28,12},{1,17},{... | collective-permute-start | bytes 688136 | tf_op jit(solution)/shard_map/ppermute | solution.py:32
  42.2 1.0 slice.24
  44.3 0.8 copy.20.lens
  45.1 5.0 %parts.1 = (bf16[512,2048]{1,0:T(8,128)(2,1)}, bf16[512,2048]{1,0:T(8,128)(2,1)}) custom-call(f32[256,2048]{1,0:T(8,128)S(1)} %copy-done, f32[256,2048]{1,0:T(8,128)} %im.5, s32[256,1]{1,0:T(8,128)} %copy.20.lens, s32[4]{0:T(128)S(1)} %pad_add_fusion.1.meta), custom_call_target="tpu_custom_call" | custom-call | tf_op jit(solution)/shard_map/parts/pallas_call | solution.py:183
  50.1 0.7 copy.19.pc
  52.3 1.6 %broadcast_in_dim.7 = f32[256,2048]{1,0:T(8,128)} broadcast(f32[]{:T(128)} %constant.65.clone.1), dimensions={} | broadcast | bytes 2097156 | tf_op jit(solution)/shard_map/broadcast_in_dim | solution.py:566
  54.1 0.8 collective-permute-done.7.refs_8_
  55.3 13.5 %project.1 = (f32[256,2048]{1,0:T(8,128)}, f32[128,128]{1,0:T(8,128)}, f32[64,256]{1,0:T(8,128)}, f32[64,256]{1,0:T(8,128)}, f32[64,256]{1,0:T(8,128)}, /*index=5*/f32[64,256]{1,0:T(8,128)}) custom-call(s32[4]{0:T(128)S(1)} %get-tuple-element.357, s32[128,1]{1,0:T(8,128)} %copy.19.pc, s32[1,128]{1,0:T(1,128)S(1)} %bitcast.35, ...), custom_call_target="tpu_custom_call" | custom-call | tf_op jit(solution)/shard_map/project/pallas_call | solution.py:318
  68.7 3.1 %collective-permute-start.22 = (f32[64,256]{1,0:T(8,128)}, f32[64,256]{1,0:T(8,128)S(1)}, u32[]{:S(2)}, u32[]{:S(2)}) collective-permute-start(f32[64,256]{1,0:T(8,128)} %get-tuple-element.154), channel_id=1, source_target_pairs={{0,1},{1,0},{2,3},{3,2},{4,5},{5,4},{6,7},{7,6},{8,9},{9,8},{10,11... | collective-permute-start | bytes 196616 | tf_op jit(solution)/shard_map/ppermute | solution.py:32
  71.9 2.0 %collective-permute-start.23 = (f32[64,256]{1,0:T(8,128)}, f32[64,256]{1,0:T(8,128)S(1)}, u32[]{:S(2)}, u32[]{:S(2)}) collective-permute-start(f32[64,256]{1,0:T(8,128)} %get-tuple-element.155), channel_id=1, source_target_pairs={{0,2},{1,3},{2,0},{3,1},{4,6},{5,7},{6,4},{7,5},{8,10},{9,11},{10,... | collective-permute-start | bytes 196616 | tf_op jit(solution)/shard_map/ppermute | solution.py:32
  73.9 1.4 %collective-permute-start.24 = (f32[64,256]{1,0:T(8,128)}, f32[64,256]{1,0:T(8,128)S(1)}, u32[]{:S(2)}, u32[]{:S(2)}) collective-permute-start(f32[64,256]{1,0:T(8,128)} %get-tuple-element.156), channel_id=1, source_target_pairs={{0,3},{1,2},{2,1},{3,0},{4,7},{5,6},{6,5},{7,4},{8,11},{9,10},{10,... | collective-permute-start | bytes 196616 | tf_op jit(solution)/shard_map/ppermute | solution.py:32
  75.2 0.6 collective-permute-start.19
  75.8 2.4 %collective-permute-start.20 = (f32[128,128]{1,0:T(8,128)}, f32[128,128]{1,0:T(8,128)S(1)}, u32[]{:S(2)}, u32[]{:S(2)}) collective-permute-start(f32[128,128]{1,0:T(8,128)} %get-tuple-element.151.refs_0_), channel_id=1, source_target_pairs={{0,2},{1,3},{2,0},{3,1},{4,6},{5,7},{6,4},{7,5},{8,10},{9,11},{10,... | collective-permute-start | bytes 196616 | tf_op jit(solution)/shard_map/ppermute | solution.py:32
  78.2 1.4 %collective-permute-start.21 = (f32[128,128]{1,0:T(8,128)}, f32[128,128]{1,0:T(8,128)S(1)}, u32[]{:S(2)}, u32[]{:S(2)}) collective-permute-start(f32[128,128]{1,0:T(8,128)} %get-tuple-element.151.refs_0_), channel_id=1, source_target_pairs={{0,3},{1,2},{2,1},{3,0},{4,7},{5,6},{6,5},{7,4},{8,11},{9,10},{10,... | collective-permute-start | bytes 196616 | tf_op jit(solution)/shard_map/ppermute | solution.py:32
  79.6 1.5 %collective-permute-done.24 = f32[64,256]{1,0:T(8,128)S(1)} collective-permute-done((f32[64,256]{1,0:T(8,128)}, f32[64,256]{1,0:T(8,128)S(1)}, u32[]{:S(2)}, u32[]{:S(2)}) %collective-permute-start.24) | collective-permute-done | bytes 65568 | tf_op jit(solution)/shard_map/ppermute | solution.py:32
  81.2 0.9 add_add_fusion.1.refs_0_
  82.1 4.3 %collective-permute-start.25 = (f32[64,256]{1,0:T(8,128)S(1)}, f32[64,256]{1,0:T(8,128)S(1)}, u32[]{:S(2)}, u32[]{:S(2)}) collective-permute-start(f32[64,256]{1,0:T(8,128)S(1)} %add_add_fusion.1.refs_0_), channel_id=1, source_target_pairs={{0,1},{1,0},{2,3},{3,2},{4,5},{5,4},{6,7},{7,6},{8,9},{9,8},{10,11... | collective-permute-start | bytes 196616 | tf_op jit(solution)/shard_map/ppermute | solution.py:32
  86.4 1.1 collective-permute-start.26
  87.5 1.5 %collective-permute-start.27 = (f32[64,256]{1,0:T(8,128)S(1)}, f32[64,256]{1,0:T(8,128)S(1)}, u32[]{:S(2)}, u32[]{:S(2)}) collective-permute-start(f32[64,256]{1,0:T(8,128)S(1)} %add_add_fusion.1.refs_0_), channel_id=1, source_target_pairs={{0,3},{1,2},{2,1},{3,0},{4,7},{5,6},{6,5},{7,4},{8,11},{9,10},{10,... | collective-permute-start | bytes 196616 | tf_op jit(solution)/shard_map/ppermute | solution.py:32
  89.0 0.6 copy-done.19
  89.6 0.6 copy-done.20
  90.2 5.1 %whiten.1.whitener = f32[256,256]{1,0:T(8,128)} custom-call(f32[128,128]{1,0:T(8,128)} %get-tuple-element.151.refs_0_, f32[128,128]{1,0:T(8,128)} %copy-done.18, f32[128,128]{1,0:T(8,128)} %copy-done.19, f32[128,128]{1,0:T(8,128)} %copy-done.20), custom_call_target="tpu_custom_call" | custom-call | tf_op jit(solution)/shard_map/whiten/pallas_call | solution.py:394
  95.3 0.6 copy-done.15
  96.0 6.6 %update.1 = (f32[256,128]{1,0:T(8,128)}, f32[256,128]{1,0:T(8,128)}, f32[256,2048]{1,0:T(8,128)}, f32[256,2048]{1,0:T(8,128)}, f32[1,256]{1,0:T(1,128)}) custom-call(s32[4]{0:T(128)S(1)} %get-tuple-element.357, s32[256,1]{1,0:T(8,128)} %copy.20.lens, f32[256,256]{1,0:T(8,128)} %whiten.1.whitener, f32[256,2048]{1,0:T(8,128)} %get-tuple-element.152.p, ...), custom_call_target="tpu_custom_call" | custom-call | tf_op jit(solution)/shard_map/update/pallas_call | solution.py:458
  102.5 1.0 collective-permute-start.28
  103.5 2.0 %collective-permute-start.29 = (f32[1,256]{1,0:T(1,128)}, f32[1,256]{1,0:T(1,128)S(1)}, u32[]{:S(2)}, u32[]{:S(2)}) collective-permute-start(f32[1,256]{1,0:T(1,128)} %get-tuple-element.161), channel_id=1, source_target_pairs={{0,2},{1,3},{2,0},{3,1},{4,6},{5,7},{6,4},{7,5},{8,10},{9,11},{10,... | collective-permute-start | bytes 3080 | tf_op jit(solution)/shard_map/ppermute | solution.py:32
  105.5 1.4 %collective-permute-start.30 = (f32[1,256]{1,0:T(1,128)}, f32[1,256]{1,0:T(1,128)S(1)}, u32[]{:S(2)}, u32[]{:S(2)}) collective-permute-start(f32[1,256]{1,0:T(1,128)} %get-tuple-element.161), channel_id=1, source_target_pairs={{0,3},{1,2},{2,1},{3,0},{4,7},{5,6},{6,5},{7,4},{8,11},{9,10},{10,... | collective-permute-start | bytes 3080 | tf_op jit(solution)/shard_map/ppermute | solution.py:32
  107.0 1.2 %collective-permute-done.29 = f32[1,256]{1,0:T(1,128)S(1)} collective-permute-done((f32[1,256]{1,0:T(1,128)}, f32[1,256]{1,0:T(1,128)S(1)}, u32[]{:S(2)}, u32[]{:S(2)}) %collective-permute-start.29) | collective-permute-done | bytes 1056 | tf_op jit(solution)/shard_map/ppermute | solution.py:32
  108.2 2.9 %collective-permute-done.30 = f32[1,256]{1,0:T(1,128)S(1)} collective-permute-done((f32[1,256]{1,0:T(1,128)}, f32[1,256]{1,0:T(1,128)S(1)}, u32[]{:S(2)}, u32[]{:S(2)}) %collective-permute-start.30) | collective-permute-done | bytes 1056 | tf_op jit(solution)/shard_map/ppermute | solution.py:32
  111.1 0.7 add_add_fusion.2
  111.8 0.6 convert_divide_fusion
  (78 shorter events, 3.7 us)
Async XLA Ops:
  9.9 5.1 %copy-start.5 = (f32[256,2048]{1,0:T(8,128)S(1)}, f32[256,2048]{1,0:T(8,128)}, u32[]{:S(2)}) copy-start(f32[256,2048]{1,0:T(8,128)} %b_re.3) | copy-start | bytes 6291460
  9.9 5.1 %copy-start.6 = (f32[256,2048]{1,0:T(8,128)S(1)}, f32[256,2048]{1,0:T(8,128)}, u32[]{:S(2)}) copy-start(f32[256,2048]{1,0:T(8,128)} %b_im.3) | copy-start | bytes 6291460
  15.1 29.2 %copy-start.21 = (s32[256]{0:T(256)S(1)}, s32[256]{0:T(256)}, u32[]{:S(2)}) copy-start(s32[256]{0:T(256)} %lens.1) | copy-start | bytes 3076
  15.1 30.0 %copy-start = (f32[256,2048]{1,0:T(8,128)S(1)}, f32[256,2048]{1,0:T(8,128)}, u32[]{:S(2)}) copy-start(f32[256,2048]{1,0:T(8,128)} %re.5) | copy-start | bytes 6291460
  19.2 14.2 %collective-permute-start.10 = (f32[64,512]{1,0:T(8,128)}, f32[64,512]{1,0:T(8,128)S(1)}, u32[]{:S(2)}, u32[]{:S(2)}) collective-permute-start(f32[64,512]{1,0:T(8,128)} %cross.3), channel_id=1, source_target_pairs={{0,2},{1,3},{2,0},{3,1},{4,6},{5,7},{6,4},{7,5},{8,10},{9,11},{10,... | collective-permute-start | bytes 393224 | tf_op jit(solution)/shard_map/ppermute | solution.py:32
  23.2 10.2 %collective-permute-start.11 = (f32[64,512]{1,0:T(8,128)}, f32[64,512]{1,0:T(8,128)S(1)}, u32[]{:S(2)}, u32[]{:S(2)}) collective-permute-start(f32[64,512]{1,0:T(8,128)} %cross.3), channel_id=1, source_target_pairs={{0,3},{1,2},{2,1},{3,0},{4,7},{5,6},{6,5},{7,4},{8,11},{9,10},{10,... | collective-permute-start | bytes 393224 | tf_op jit(solution)/shard_map/ppermute | solution.py:32
  24.5 9.2 %collective-permute-start.9 = (f32[64,512]{1,0:T(8,128)}, f32[64,512]{1,0:T(8,128)S(1)}, u32[]{:S(2)}, u32[]{:S(2)}) collective-permute-start(f32[64,512]{1,0:T(8,128)} %cross.3), channel_id=1, source_target_pairs={{0,1},{1,0},{2,3},{3,2},{4,5},{5,4},{6,7},{7,6},{8,9},{9,8},{10,11... | collective-permute-start | bytes 393224 | tf_op jit(solution)/shard_map/ppermute | solution.py:32
  24.8 13.5 %collective-permute-start = (f32[56,2048]{1,0:T(8,128)}, f32[56,2048]{1,0:T(8,128)}, u32[]{:S(2)}, u32[]{:S(2)}) collective-permute-start(f32[56,2048]{1,0:T(8,128)} %pick.2.rows.refs_0_), channel_id=1, source_target_pairs={{0,8},{4,12},{8,0},{12,4},{16,24},{20,28},{24,16},{28,20},{1,9},{5... | collective-permute-start | bytes 1376264 | tf_op jit(solution)/shard_map/ppermute | solution.py:32
  26.2 13.8 %collective-permute-start.1 = (f32[56,2048]{1,0:T(8,128)}, f32[56,2048]{1,0:T(8,128)}, u32[]{:S(2)}, u32[]{:S(2)}) collective-permute-start(f32[56,2048]{1,0:T(8,128)} %pick.2.rows.refs_0_), channel_id=1, source_target_pairs={{0,16},{4,20},{8,24},{12,28},{16,0},{20,4},{24,8},{28,12},{1,17},{... | collective-permute-start | bytes 1376264 | tf_op jit(solution)/shard_map/ppermute | solution.py:32
  34.7 15.4 %copy-start.7 = (f32[64,512]{1,0:T(8,128)}, f32[64,512]{1,0:T(8,128)S(1)}, u32[]{:S(2)}) copy-start(f32[64,512]{1,0:T(8,128)S(1)} %add_add_fusion.refs_10_) | copy-start | bytes 393220
  34.7 8.4 %collective-permute-start.13 = (f32[64,512]{1,0:T(8,128)S(1)}, f32[64,512]{1,0:T(8,128)S(1)}, u32[]{:S(2)}, u32[]{:S(2)}) collective-permute-start(f32[64,512]{1,0:T(8,128)S(1)} %add_add_fusion.refs_10_), channel_id=1, source_target_pairs={{0,8},{4,12},{8,0},{12,4},{16,24},{20,28},{24,16},{28,20},{1,9},{5... | collective-permute-start | bytes 393224 | tf_op jit(solution)/shard_map/ppermute | solution.py:32
  36.4 7.0 %collective-permute-start.15 = (f32[64,512]{1,0:T(8,128)S(1)}, f32[64,512]{1,0:T(8,128)S(1)}, u32[]{:S(2)}, u32[]{:S(2)}) collective-permute-start(f32[64,512]{1,0:T(8,128)S(1)} %add_add_fusion.refs_10_), channel_id=1, source_target_pairs={{0,16},{4,20},{8,24},{12,28},{16,0},{20,4},{24,8},{28,12},{1,17},{... | collective-permute-start | bytes 393224 | tf_op jit(solution)/shard_map/ppermute | solution.py:32
  37.8 6.0 %collective-permute-start.17 = (f32[64,512]{1,0:T(8,128)S(1)}, f32[64,512]{1,0:T(8,128)S(1)}, u32[]{:S(2)}, u32[]{:S(2)}) collective-permute-start(f32[64,512]{1,0:T(8,128)S(1)} %add_add_fusion.refs_10_), channel_id=1, source_target_pairs={{0,24},{4,28},{8,16},{12,20},{16,8},{20,12},{24,0},{28,4},{1,25},{... | collective-permute-start | bytes 393224 | tf_op jit(solution)/shard_map/ppermute | solution.py:32
  38.3 5.6 %collective-permute-start.12 = (f32[64,512]{1,0:T(8,128)S(1)}, f32[64,512]{1,0:T(8,128)S(1)}, u32[]{:S(2)}, u32[]{:S(2)}) collective-permute-start(f32[64,512]{1,0:T(8,128)S(1)} %add_add_fusion.refs_10_), channel_id=1, source_target_pairs={{0,4},{4,0},{8,12},{12,8},{16,20},{20,16},{24,28},{28,24},{1,5},{5... | collective-permute-start | bytes 393224 | tf_op jit(solution)/shard_map/ppermute | solution.py:32
  39.9 11.8 %collective-permute-start.2 = (f32[56,1024]{1,0:T(8,128)S(1)}, f32[56,1024]{1,0:T(8,128)}, u32[]{:S(2)}, u32[]{:S(2)}) collective-permute-start(f32[56,1024]{1,0:T(8,128)S(1)} %slice.23), channel_id=1, source_target_pairs={{0,16},{4,20},{8,24},{12,28},{16,0},{20,4},{24,8},{28,12},{1,17},{... | collective-permute-start | bytes 688136 | tf_op jit(solution)/shard_map/ppermute | solution.py:32
  43.1 7.0 %copy-start.9 = (f32[64,512]{1,0:T(8,128)}, f32[64,512]{1,0:T(8,128)S(1)}, u32[]{:S(2)}) copy-start(f32[64,512]{1,0:T(8,128)S(1)} %collective-permute-done.13.refs_12_) | copy-start | bytes 393220
  43.1 9.0 %collective-permute-start.3 = (f32[56,1024]{1,0:T(8,128)S(1)}, f32[56,1024]{1,0:T(8,128)}, u32[]{:S(2)}, u32[]{:S(2)}) collective-permute-start(f32[56,1024]{1,0:T(8,128)S(1)} %slice.24), channel_id=1, source_target_pairs={{0,8},{4,12},{8,0},{12,4},{16,24},{20,28},{24,16},{28,20},{1,9},{5... | collective-permute-start | bytes 688136 | tf_op jit(solution)/shard_map/ppermute | solution.py:32
  43.4 6.7 %copy-start.10 = (f32[64,512]{1,0:T(8,128)}, f32[64,512]{1,0:T(8,128)S(1)}, u32[]{:S(2)}) copy-start(f32[64,512]{1,0:T(8,128)S(1)} %collective-permute-done.15.refs_14_) | copy-start | bytes 393220
  43.4 7.7 %collective-permute-start.14 = (f32[64,512]{1,0:T(8,128)S(1)}, f32[64,512]{1,0:T(8,128)S(1)}, u32[]{:S(2)}, u32[]{:S(2)}) collective-permute-start(f32[64,512]{1,0:T(8,128)S(1)} %collective-permute-done.13.refs_12_), channel_id=1, source_target_pairs={{0,4},{4,0},{8,12},{12,8},{16,20},{20,16},{24,28},{28,24},{1,5},{5... | collective-permute-start | bytes 393224 | tf_op jit(solution)/shard_map/ppermute | solution.py:32
  43.8 6.3 %copy-start.11 = (f32[64,512]{1,0:T(8,128)}, f32[64,512]{1,0:T(8,128)S(1)}, u32[]{:S(2)}) copy-start(f32[64,512]{1,0:T(8,128)S(1)} %collective-permute-done.17.refs_16_) | copy-start | bytes 393220
  43.8 7.5 %collective-permute-start.16 = (f32[64,512]{1,0:T(8,128)S(1)}, f32[64,512]{1,0:T(8,128)S(1)}, u32[]{:S(2)}, u32[]{:S(2)}) collective-permute-start(f32[64,512]{1,0:T(8,128)S(1)} %collective-permute-done.15.refs_14_), channel_id=1, source_target_pairs={{0,4},{4,0},{8,12},{12,8},{16,20},{20,16},{24,28},{28,24},{1,5},{5... | collective-permute-start | bytes 393224 | tf_op jit(solution)/shard_map/ppermute | solution.py:32
  43.9 6.2 %copy-start.12 = (f32[64,512]{1,0:T(8,128)}, f32[64,512]{1,0:T(8,128)S(1)}, u32[]{:S(2)}) copy-start(f32[64,512]{1,0:T(8,128)S(1)} %collective-permute-done.12.refs_11_) | copy-start | bytes 393220
  43.9 7.7 %collective-permute-start.18 = (f32[64,512]{1,0:T(8,128)S(1)}, f32[64,512]{1,0:T(8,128)}, u32[]{:S(2)}, u32[]{:S(2)}) collective-permute-start(f32[64,512]{1,0:T(8,128)S(1)} %collective-permute-done.17.refs_16_), channel_id=1, source_target_pairs={{0,4},{4,0},{8,12},{12,8},{16,20},{20,16},{24,28},{28,24},{1,5},{5... | collective-permute-start | bytes 393224 | tf_op jit(solution)/shard_map/ppermute | solution.py:32
  45.1 5.0 %copy-start.22 = (s32[128]{0:T(128)S(1)}, s32[128]{0:T(128)}, u32[]{:S(2)}) copy-start(s32[128]{0:T(128)} %piv.1) | copy-start | bytes 1540
  51.0 1.2 %copy-start.13 = (f32[64,512]{1,0:T(8,128)}, f32[64,512]{1,0:T(8,128)S(1)}, u32[]{:S(2)}) copy-start(f32[64,512]{1,0:T(8,128)S(1)} %collective-permute-done.14.refs_13_) | copy-start | bytes 393220
  51.1 3.0 %collective-permute-start.4 = (f32[56,2048]{1,0:T(8,128)}, f32[56,2048]{1,0:T(8,128)}, u32[]{:S(2)}, u32[]{:S(2)}) collective-permute-start(f32[56,2048]{1,0:T(8,128)} %pick.2.rows.refs_0_), channel_id=1, source_target_pairs={{0,4},{4,0},{8,12},{12,8},{16,20},{20,16},{24,28},{28,24},{1,5},{5... | collective-permute-start | bytes 1376264 | tf_op jit(solution)/shard_map/ppermute | solution.py:32
  51.2 1.0 copy-start.14
  51.2 4.0 %collective-permute-start.5 = (f32[56,2048]{1,0:T(8,128)}, f32[56,2048]{1,0:T(8,128)}, u32[]{:S(2)}, u32[]{:S(2)}) collective-permute-start(f32[56,2048]{1,0:T(8,128)} %collective-permute-done.refs_1_), channel_id=1, source_target_pairs={{0,4},{4,0},{8,12},{12,8},{16,20},{20,16},{24,28},{28,24},{1,5},{5... | collective-permute-start | bytes 1376264 | tf_op jit(solution)/shard_map/ppermute | solution.py:32
  51.6 3.6 %collective-permute-start.6 = (f32[56,2048]{1,0:T(8,128)}, f32[56,2048]{1,0:T(8,128)}, u32[]{:S(2)}, u32[]{:S(2)}) collective-permute-start(f32[56,2048]{1,0:T(8,128)} %collective-permute-done.1.refs_2_), channel_id=1, source_target_pairs={{0,4},{4,0},{8,12},{12,8},{16,20},{20,16},{24,28},{28,24},{1,5},{5... | collective-permute-start | bytes 1376264 | tf_op jit(solution)/shard_map/ppermute | solution.py:32
  51.8 3.2 %collective-permute-start.7 = (f32[56,1024]{1,0:T(8,128)}, f32[56,1024]{1,0:T(8,128)}, u32[]{:S(2)}, u32[]{:S(2)}) collective-permute-start(f32[56,1024]{1,0:T(8,128)} %collective-permute-done.2.refs_3_), channel_id=1, source_target_pairs={{0,4},{4,0},{8,12},{12,8},{16,20},{20,16},{24,28},{28,24},{1,5},{5... | collective-permute-start | bytes 688136 | tf_op jit(solution)/shard_map/ppermute | solution.py:32
  52.2 3.1 %collective-permute-start.8 = (f32[56,1024]{1,0:T(8,128)}, f32[56,1024]{1,0:T(8,128)}, u32[]{:S(2)}, u32[]{:S(2)}) collective-permute-start(f32[56,1024]{1,0:T(8,128)} %collective-permute-done.3.refs_4_), channel_id=1, source_target_pairs={{0,4},{4,0},{8,12},{12,8},{16,20},{20,16},{24,28},{28,24},{1,5},{5... | collective-permute-start | bytes 688136 | tf_op jit(solution)/shard_map/ppermute | solution.py:32
  55.3 40.7 %copy-start.2 = (f32[256,2048]{1,0:T(8,128)S(1)}, f32[256,2048]{1,0:T(8,128)}, u32[]{:S(2)}) copy-start(f32[256,2048]{1,0:T(8,128)} %get-tuple-element.356) | copy-start | bytes 6291460
  68.7 9.5 %collective-permute-start.22 = (f32[64,256]{1,0:T(8,128)}, f32[64,256]{1,0:T(8,128)S(1)}, u32[]{:S(2)}, u32[]{:S(2)}) collective-permute-start(f32[64,256]{1,0:T(8,128)} %get-tuple-element.154), channel_id=1, source_target_pairs={{0,1},{1,0},{2,3},{3,2},{4,5},{5,4},{6,7},{7,6},{8,9},{9,8},{10,11... | collective-permute-start | bytes 196616 | tf_op jit(solution)/shard_map/ppermute | solution.py:32
  71.9 7.8 %collective-permute-start.23 = (f32[64,256]{1,0:T(8,128)}, f32[64,256]{1,0:T(8,128)S(1)}, u32[]{:S(2)}, u32[]{:S(2)}) collective-permute-start(f32[64,256]{1,0:T(8,128)} %get-tuple-element.155), channel_id=1, source_target_pairs={{0,2},{1,3},{2,0},{3,1},{4,6},{5,7},{6,4},{7,5},{8,10},{9,11},{10,... | collective-permute-start | bytes 196616 | tf_op jit(solution)/shard_map/ppermute | solution.py:32
  73.9 7.3 %collective-permute-start.24 = (f32[64,256]{1,0:T(8,128)}, f32[64,256]{1,0:T(8,128)S(1)}, u32[]{:S(2)}, u32[]{:S(2)}) collective-permute-start(f32[64,256]{1,0:T(8,128)} %get-tuple-element.156), channel_id=1, source_target_pairs={{0,3},{1,2},{2,1},{3,0},{4,7},{5,6},{6,5},{7,4},{8,11},{9,10},{10,... | collective-permute-start | bytes 196616 | tf_op jit(solution)/shard_map/ppermute | solution.py:32
  75.2 12.2 %collective-permute-start.19 = (f32[128,128]{1,0:T(8,128)}, f32[128,128]{1,0:T(8,128)S(1)}, u32[]{:S(2)}, u32[]{:S(2)}) collective-permute-start(f32[128,128]{1,0:T(8,128)} %get-tuple-element.151.refs_0_), channel_id=1, source_target_pairs={{0,1},{1,0},{2,3},{3,2},{4,5},{5,4},{6,7},{7,6},{8,9},{9,8},{10,11... | collective-permute-start | bytes 196616 | tf_op jit(solution)/shard_map/ppermute | solution.py:32
  75.8 13.1 %collective-permute-start.20 = (f32[128,128]{1,0:T(8,128)}, f32[128,128]{1,0:T(8,128)S(1)}, u32[]{:S(2)}, u32[]{:S(2)}) collective-permute-start(f32[128,128]{1,0:T(8,128)} %get-tuple-element.151.refs_0_), channel_id=1, source_target_pairs={{0,2},{1,3},{2,0},{3,1},{4,6},{5,7},{6,4},{7,5},{8,10},{9,11},{10,... | collective-permute-start | bytes 196616 | tf_op jit(solution)/shard_map/ppermute | solution.py:32
  78.2 10.7 %collective-permute-start.21 = (f32[128,128]{1,0:T(8,128)}, f32[128,128]{1,0:T(8,128)S(1)}, u32[]{:S(2)}, u32[]{:S(2)}) collective-permute-start(f32[128,128]{1,0:T(8,128)} %get-tuple-element.151.refs_0_), channel_id=1, source_target_pairs={{0,3},{1,2},{2,1},{3,0},{4,7},{5,6},{6,5},{7,4},{8,11},{9,10},{10,... | collective-permute-start | bytes 196616 | tf_op jit(solution)/shard_map/ppermute | solution.py:32
  82.0 13.3 %copy-start.8 = (f32[64,256]{1,0:T(8,128)}, f32[64,256]{1,0:T(8,128)S(1)}, u32[]{:S(2)}) copy-start(f32[64,256]{1,0:T(8,128)S(1)} %add_add_fusion.1.refs_0_) | copy-start | bytes 196612
  82.1 13.2 %collective-permute-start.25 = (f32[64,256]{1,0:T(8,128)S(1)}, f32[64,256]{1,0:T(8,128)S(1)}, u32[]{:S(2)}, u32[]{:S(2)}) collective-permute-start(f32[64,256]{1,0:T(8,128)S(1)} %add_add_fusion.1.refs_0_), channel_id=1, source_target_pairs={{0,1},{1,0},{2,3},{3,2},{4,5},{5,4},{6,7},{7,6},{8,9},{9,8},{10,11... | collective-permute-start | bytes 196616 | tf_op jit(solution)/shard_map/ppermute | solution.py:32
  86.4 8.9 %collective-permute-start.26 = (f32[64,256]{1,0:T(8,128)S(1)}, f32[64,256]{1,0:T(8,128)S(1)}, u32[]{:S(2)}, u32[]{:S(2)}) collective-permute-start(f32[64,256]{1,0:T(8,128)S(1)} %add_add_fusion.1.refs_0_), channel_id=1, source_target_pairs={{0,2},{1,3},{2,0},{3,1},{4,6},{5,7},{6,4},{7,5},{8,10},{9,11},{10,... | collective-permute-start | bytes 196616 | tf_op jit(solution)/shard_map/ppermute | solution.py:32
  87.5 1.5 %copy-start.18 = (f32[128,128]{1,0:T(8,128)}, f32[128,128]{1,0:T(8,128)S(1)}, u32[]{:S(2)}) copy-start(f32[128,128]{1,0:T(8,128)S(1)} %collective-permute-done.19.refs_1_) | copy-start | bytes 196612
  87.5 7.8 %collective-permute-start.27 = (f32[64,256]{1,0:T(8,128)S(1)}, f32[64,256]{1,0:T(8,128)S(1)}, u32[]{:S(2)}, u32[]{:S(2)}) collective-permute-start(f32[64,256]{1,0:T(8,128)S(1)} %add_add_fusion.1.refs_0_), channel_id=1, source_target_pairs={{0,3},{1,2},{2,1},{3,0},{4,7},{5,6},{6,5},{7,4},{8,11},{9,10},{10,... | collective-permute-start | bytes 196616 | tf_op jit(solution)/shard_map/ppermute | solution.py:32
  95.3 0.6 copy-start.16
  95.3 0.6 copy-start.17
  102.5 4.4 %collective-permute-start.28 = (f32[1,256]{1,0:T(1,128)}, f32[1,256]{1,0:T(1,128)S(1)}, u32[]{:S(2)}, u32[]{:S(2)}) collective-permute-start(f32[1,256]{1,0:T(1,128)} %get-tuple-element.161), channel_id=1, source_target_pairs={{0,1},{1,0},{2,3},{3,2},{4,5},{5,4},{6,7},{7,6},{8,9},{9,8},{10,11... | collective-permute-start | bytes 3080 | tf_op jit(solution)/shard_map/ppermute | solution.py:32
  103.5 4.7 %collective-permute-start.29 = (f32[1,256]{1,0:T(1,128)}, f32[1,256]{1,0:T(1,128)S(1)}, u32[]{:S(2)}, u32[]{:S(2)}) collective-permute-start(f32[1,256]{1,0:T(1,128)} %get-tuple-element.161), channel_id=1, source_target_pairs={{0,2},{1,3},{2,0},{3,1},{4,6},{5,7},{6,4},{7,5},{8,10},{9,11},{10,... | collective-permute-start | bytes 3080 | tf_op jit(solution)/shard_map/ppermute | solution.py:32
  105.5 5.6 %collective-permute-start.30 = (f32[1,256]{1,0:T(1,128)}, f32[1,256]{1,0:T(1,128)S(1)}, u32[]{:S(2)}, u32[]{:S(2)}) collective-permute-start(f32[1,256]{1,0:T(1,128)} %get-tuple-element.161), channel_id=1, source_target_pairs={{0,3},{1,2},{2,1},{3,0},{4,7},{5,6},{6,5},{7,4},{8,11},{9,10},{10,... | collective-permute-start | bytes 3080 | tf_op jit(solution)/shard_map/ppermute | solution.py:32
  (3 other events, 1.9 us)

commit v2 on v1

v2 whole, which is shorter than its diff:
```python
import functools
import math

import jax
import jax.numpy as jnp
from jax import lax
from jax.experimental import pallas as pl
from jax.experimental.pallas import tpu as pltpu
from jax.sharding import PartitionSpec as P

BIN_BLOCK = 128
NS_STEPS = 6
epsilon = 1e-06
F32 = jnp.float32
BF16 = jnp.bfloat16
MIB = 1024 * 1024

ANY = pl.BlockSpec(memory_space=pl.ANY)
SMEM = pl.BlockSpec(memory_space=pltpu.SMEM)
VMEM = pl.BlockSpec(memory_space=pltpu.VMEM)
HBM = pl.BlockSpec(memory_space=pltpu.HBM)


def params(mib):
    return pltpu.CompilerParams(vmem_limit_bytes=mib * MIB)


def light():
    return pl.CostEstimate(flops=1000, bytes_accessed=1000, transcendentals=0)


def column(row):
    wide = jnp.broadcast_to(row.astype(F32), (8, row.shape[1]))
    return wide.T[:, 0:1].astype(jnp.int32)


def up(value, step):
    return -(-value // step) * step


def swap(array, axis, size, distance):
    return lax.ppermute(array, axis, [(i, i ^ distance) for i in range(size)])


def split(value):
    high = value.astype(BF16)
    low = (value - high.astype(F32)).astype(BF16)
    return high, low


def split3(value):
    high = value.astype(BF16)
    rest = value - high.astype(F32)
    middle = rest.astype(BF16)
    low = (rest - middle.astype(F32)).astype(BF16)
    return high, middle, low


def nn(left, right):
    return jnp.dot(left, right, preferred_element_type=F32)


def nt(left, right):
    return lax.dot_general(left, right, (((1,), (1,)), ((), ())), preferred_element_type=F32)


def nn3(left, right):
    return nn(left[0], right[0]) + (nn(left[0], right[1]) + nn(left[1], right[0]))


def nt3(left, right):
    return nt(left[0], right[0]) + (nt(left[0], right[1]) + nt(left[1], right[0]))


def pick_kernel(cap, piv, lens, skip_ref, re, im, out, where, rows_re, rows_im, sem):
    wave_rows, cols = re.shape
    slots = rows_re.shape[0]
    base = lax.axis_index("wave") * wave_rows
    first_bin = lax.axis_index("freq") * cols
    skip = skip_ref[0]

    def fetch(row, slot):
        pltpu.make_async_copy(re.at[pl.ds(row, 1)], rows_re.at[pl.ds(slot, 1)], sem.at[0]).start()
        pltpu.make_async_copy(im.at[pl.ds(row, 1)], rows_im.at[pl.ds(slot, 1)], sem.at[1]).start()

    def look(i, seen):
        row = piv[i] - base
        own = (row >= 0) & (row < wave_rows)
        slot = seen - skip

        @pl.when(own & (slot >= 0) & (slot < cap))
        def _():
            where[slot] = lens[row]
            fetch(row, slot)

        return seen + own.astype(jnp.int32)

    found = lax.fori_loop(0, piv.shape[0], look, 0, unroll=8) - skip

    def fill(slot, carry):
        where[slot] = 0
        fetch(0, slot)
        return carry

    lax.fori_loop(jnp.clip(found, 0, cap), slots, fill, 0)
    at = lax.broadcasted_iota(jnp.int32, (slots, 1), 0)
    live = jnp.zeros((slots, 1), jnp.int32)
    for slot in range(slots):
        live = jnp.where(at == slot, where[slot] * BIN_BLOCK, live)
    bins = lax.broadcasted_iota(jnp.int32, (slots, cols), 1) + first_bin
    keep = bins < live
    pltpu.make_async_copy(re.at[pl.ds(0, slots)], rows_re, sem.at[0]).wait()
    pltpu.make_async_copy(im.at[pl.ds(0, slots)], rows_im, sem.at[1]).wait()
    out[0:cap, :] = jnp.where(keep, rows_re[...], 0.0)[0:cap]
    out[cap : 2 * cap, :] = jnp.where(keep, rows_im[...], 0.0)[0:cap]


def pick(cap, pivots, lengths, skip, res_re, res_im):
    cols = res_re.shape[1]
    return pl.pallas_call(
        functools.partial(pick_kernel, cap),
        out_shape=jax.ShapeDtypeStruct((2 * cap, cols), F32),
        in_specs=[SMEM, SMEM, SMEM, HBM, HBM],
        out_specs=VMEM,
        scratch_shapes=[
            pltpu.SMEM((up(cap, 8),), jnp.int32),
            pltpu.VMEM((up(cap, 8), cols), F32),
            pltpu.VMEM((up(cap, 8), cols), F32),
            pltpu.SemaphoreType.DMA((2,)),
        ],
        compiler_params=params(8),
        name="pick",
    )(pivots, lengths, skip, res_re, res_im)


def cross_kernel(cap, rows, b_re, b_im, out):
    nb, cols = b_re.shape
    mine = out.shape[0] - up(cap, 8)
    start = pl.multiple_of(lax.axis_index("wave") * mine, mine)
    chunk = min(cols, 512)
    total = jnp.zeros((2 * cap + 2 * mine, 2 * nb), F32)
    for at in range(0, cols, chunk):
        part = pl.ds(at, chunk)
        left = split(
            jnp.concatenate([rows[:, part], b_re[pl.ds(start, mine), part], b_im[pl.ds(start, mine), part]], axis=0)
        )
        right = split(jnp.concatenate([b_re[:, part], b_im[:, part]], axis=0))
        total += nt3(left, right)

    def join(at, size):
        real, imag = total[at : at + size], total[at + size : at + 2 * size]
        return jnp.concatenate([real[:, :nb] + imag[:, nb:], imag[:, :nb] - real[:, nb:]], axis=1)

    out[...] = jnp.zeros_like(out)
    out[0:cap, :] = join(0, cap)
    out[up(cap, 8) :, :] = join(2 * cap, mine)
def cross(cap, nw, rows, basis_re, basis_im):
    nb = basis_re.shape[0]
    return pl.pallas_call(
        functools.partial(cross_kernel, cap),
        out_shape=jax.ShapeDtypeStruct((up(cap, 8) + nb // nw, 2 * nb), F32),
        in_specs=[VMEM, VMEM, VMEM],
        out_specs=VMEM,
        compiler_params=params(16),
        cost_estimate=light(),
        name="cross",
    )(rows, basis_re, basis_im)


def ranks(pivots_col, pivots_row, wave_rows):
    count = pivots_col.shape[0]
    owner_col = pivots_col // wave_rows
    owner_row = pivots_row // wave_rows
    i = lax.broadcasted_iota(jnp.int32, (count, count), 0)
    j = lax.broadcasted_iota(jnp.int32, (count, count), 1)
    ahead = (owner_col == owner_row) & (j < i)
    return owner_col, jnp.sum(ahead.astype(jnp.int32), axis=1, keepdims=True)


def one_hot(index, width):
    return (lax.broadcasted_iota(jnp.int32, (index.shape[0], width), 1) == index).astype(F32).astype(BF16)


def move(source, target, sem):
    copy = pltpu.make_async_copy(source, target, sem)
    copy.start()
    return copy


def orders_kernel(cap, nw, waves, pr, listed, crossed, rounds, blank_p, blank_c):
    owner, rank = ranks(column(pr[...]), pr[...], waves)
    group = jnp.bitwise_xor(owner, lax.axis_index("wave"))
    rounds[0] = jnp.max(rank) // cap + 1
    at = jnp.where(rank < cap, group * (2 * cap) + rank, -nw * 2 * cap)
    both = jnp.concatenate([at, at + cap], axis=0)
    listed[...] = one_hot(both, listed.shape[1])
    capp = crossed.shape[1] // nw
    crossed[...] = one_hot(jnp.where(rank < cap, group * capp + rank, -1), crossed.shape[1])


def orders(cap, nw, waves, nb, cols, pivots):
    count = pivots.shape[0]
    return pl.pallas_call(
        functools.partial(orders_kernel, cap, nw, waves),
        out_shape=(
            jax.ShapeDtypeStruct((2 * count, nw * 2 * cap), BF16),
            jax.ShapeDtypeStruct((count, nw * up(cap, 8)), BF16),
            jax.ShapeDtypeStruct((1,), jnp.int32),
            jax.ShapeDtypeStruct((2 * count, cols), F32),
            jax.ShapeDtypeStruct((count, 2 * nb), F32),
        ),
        in_specs=[VMEM],
        out_specs=(VMEM, VMEM, SMEM, HBM, HBM),
        compiler_params=params(8),
        cost_estimate=light(),
        name="orders",
    )(pivots.reshape(1, count))


def fetch_lists(refs, places, cap, gathered, sem):
    waits = []
    for index, ((k, col), ref) in enumerate(zip(places, refs)):
        target = gathered.at[pl.ds(k * 2 * cap, 2 * cap), pl.ds(col, ref.shape[1])]
        waits.append(move(ref, target, sem.at[index]))
    return waits


def packed(gram_re, gram_im):
    i = lax.broadcasted_iota(jnp.int32, gram_re.shape, 0)
    j = lax.broadcasted_iota(jnp.int32, gram_re.shape, 1)
    return jnp.where(i <= j, gram_re, gram_im)


def joined(total, rows, cols):
    real = total[:rows, :cols] + total[rows:, cols:]
    imag = total[rows:, :cols] - total[:rows, cols:]
    return real, imag


def stack_columns(pair_re, pair_im, target, chunk, sem):
    rows, cols = pair_re.shape
    waits = []
    for step in range(cols // chunk):
        part = pl.ds(step * chunk, chunk)
        waits.append(
            [
                move(pair_re.at[:, part], target.at[pl.ds(0, rows), part], sem.at[step, 0]),
                move(pair_im.at[:, part], target.at[pl.ds(rows, rows), part], sem.at[step, 1]),
            ]
        )
    return waits


def project_kernel(cap, nw, nf, places, rounds, select, select_c, lens, b_re, b_im, re, im, *refs):
    extra_p, extra_c, refs = refs[0], refs[1], refs[2:]
    list_refs, refs = refs[: len(places)], refs[len(places) :]
    cross_refs, refs = refs[:nw], refs[nw:]
    p_out, g_out, refs = refs[0], refs[1], refs[2:]
    out, refs = refs[:nf], refs[nf:]
    gathered, crossed, gram_b, basis, live, placed, more_p, more_c, d_all, sem_l, sem_c, sem_b, sem_x = refs
    count = select_c.shape[0]
    nb, cols = b_re.shape
    waves = re.shape[0]
    capp = up(cap, 8)
    mine = nb // nw
    me_w, me_f, over = lax.axis_index("wave"), lax.axis_index("freq"), rounds[0] > 1
    waits = []
    for k, ref in enumerate(cross_refs):
        at = (k ^ 1) * capp
        waits.append(move(ref.at[pl.ds(0, capp)], crossed.at[pl.ds(at, capp)], sem_c.at[2 * k]))
        at = pl.multiple_of((me_w ^ k) * mine, mine)
        waits.append(move(ref.at[pl.ds(capp, mine)], gram_b.at[pl.ds(at, mine)], sem_c.at[2 * k + 1]))
    list_waits = fetch_lists(list_refs, places, cap, gathered, sem_l)
    chunk = min(cols, 1024)

    @pl.when(over)
    def _():
        first = pltpu.make_async_copy(extra_p, more_p, sem_x.at[0])
        second = pltpu.make_async_copy(extra_c, more_c, sem_x.at[1])
        first.start()
        second.start()
        first.wait()
        second.wait()

    for copy in list_waits:
        copy.wait()
    basis_waits = stack_columns(b_re, b_im, basis, chunk, sem_b)
    for step in range(cols // chunk):
        part = pl.ds(step * chunk, chunk)
        high, low = split(gathered[:, part])
        block = nn(select[...], high) + nn(select[...], low)
        placed[:, part] = block + jnp.where(over, more_p[:, part], 0.0)
    for copy in waits:
        copy.wait()
    pieces = split3(crossed[...])
    cross_all = nn(select_c[...], pieces[0]) + (nn(select_c[...], pieces[1]) + nn(select_c[...], pieces[2]))
    cross_all = cross_all + jnp.where(over, more_c[...], 0.0)
    stacked = jnp.concatenate([cross_all[:, :nb], cross_all[:, nb:]], axis=0)
    twist = nn3(split(stacked), split(gram_b[...]))
    total_re = 2.0 * cross_all[:, :nb] - (twist[:count, :nb] - twist[count:, nb:])
    total_im = 2.0 * cross_all[:, nb:] - (twist[:count, nb:] + twist[count:, :nb])
    take = split(
        jnp.concatenate(
            [jnp.concatenate([total_re, -total_im], axis=1), jnp.concatenate([total_im, total_re], axis=1)], axis=0
        )
    )
    live_waits = [
        move(re, live.at[pl.ds(0, waves)], sem_x.at[2]),
        move(im, live.at[pl.ds(waves, waves)], sem_x.at[3]),
    ]
    for step in range(cols // chunk):
        part = pl.ds(step * chunk, chunk)
        for copy in basis_waits[step]:
            copy.wait()
        placed[:, part] = placed[:, part] - nn3(take, split(basis[:, part]))
    p_wait = move(placed, p_out, sem_x.at[4])
    right = split(placed[...])
    inner_p = nt(right[0], right[0])
    inner_q = nt(right[0], right[1])
    for copy in live_waits:
        copy.wait()
    end = column(lens[...]) * BIN_BLOCK
    keep = lax.broadcasted_iota(jnp.int32, (1, cols), 1) + me_f * cols < end
    inner_re = nt3(split(jnp.where(keep, live[0:waves, :], 0.0)), right)
    inner_im = nt3(split(jnp.where(keep, live[waves : 2 * waves, :], 0.0)), right)
    inner_r = jnp.concatenate([inner_re, inner_im], axis=0)
    g_out[...] = packed(*joined(inner_p + (inner_q + inner_q.T), count, count))
    d_all[:, :count], d_all[:, count:] = joined(inner_r, waves, count)
    share = waves // nf
    for k in range(nf):
        out[k][...] = d_all[pl.ds(pl.multiple_of((me_f ^ k) * share, share), share), :]
    p_wait.wait()


def project(cap, nw, nf, places, rounds, select, select_c, lens, *rest):
    basis_re, res_re = rest[0], rest[2]
    count = select_c.shape[0]
    nb, cols = basis_re.shape
    waves = res_re.shape[0]
    shapes = [jax.ShapeDtypeStruct((2 * count, cols), F32), jax.ShapeDtypeStruct((count, count), F32)]
    shapes += [jax.ShapeDtypeStruct((waves // nf, 2 * count), F32)] * nf
    return pl.pallas_call(
        functools.partial(project_kernel, cap, nw, nf, places),
        out_shape=shapes,
        in_specs=[SMEM] + [VMEM] * 3 + [HBM] * len(rest),
        out_specs=[HBM] + [VMEM] * (len(shapes) - 1),
        scratch_shapes=[
            pltpu.VMEM((select.shape[1], cols), F32),
            pltpu.VMEM((nw * up(cap, 8), 2 * nb), F32),
            pltpu.VMEM((nb, 2 * nb), F32),
            pltpu.VMEM((2 * nb, cols), F32),
            pltpu.VMEM((2 * waves, cols), F32),
            pltpu.VMEM((2 * count, cols), F32),
            pltpu.VMEM((2 * count, cols), F32),
            pltpu.VMEM((count, 2 * nb), F32),
            pltpu.VMEM((waves, 2 * count), F32),
            pltpu.SemaphoreType.DMA((len(places),)),
            pltpu.SemaphoreType.DMA((2 * nw,)),
            pltpu.SemaphoreType.DMA((cols // min(cols, 1024), 2)),
            pltpu.SemaphoreType.DMA((5,)),
        ],
        compiler_params=params(61),
        name="project",
    )(rounds, select, select_c, lens, *rest)


def whiten_kernel(nf, *refs):
    gram = refs[0][...]
    for ref in refs[1:nf]:
        gram = gram + ref[...]
    out = refs[nf]
    count = gram.shape[0]
    i = lax.broadcasted_iota(jnp.int32, (count, count), 0)
    j = lax.broadcasted_iota(jnp.int32, (count, count), 1)
    upper = jnp.where(i <= j, gram, 0.0)
    lower = jnp.where(i > j, gram, 0.0)
    diagonal = jnp.where(i == j, gram, 0.0)
    gram_re = upper + upper.T - diagonal
    gram_im = lower - lower.T
    scale_row = 1.0 / jnp.sqrt(jnp.sum(diagonal, axis=0, keepdims=True) + epsilon)
    scale_col = 1.0 / jnp.sqrt(jnp.sum(diagonal, axis=1, keepdims=True) + epsilon)
    outer = scale_col * scale_row
    gram_re = gram_re * outer
    gram_im = gram_im * outer
    bound = jnp.max(jnp.sum(jnp.abs(gram_re) + jnp.abs(gram_im), axis=1, keepdims=True), axis=0, keepdims=True)
    gram_re = gram_re / bound
    gram_im = gram_im / bound
    mix = jnp.concatenate(
        [jnp.concatenate([gram_re, gram_im], axis=1), jnp.concatenate([-gram_im, gram_re], axis=1)], axis=0
    )
    i = lax.broadcasted_iota(jnp.int32, (2 * count, 2 * count), 0)
    j = lax.broadcasted_iota(jnp.int32, (2 * count, 2 * count), 1)
    ident = jnp.where(i == j, 1.0, 0.0).astype(F32)
    zed = None
    for step in range(NS_STEPS):
        turn = 1.5 * ident - 0.5 * mix
        turn_parts = split(turn)
        zed = turn if zed is None else nn3(turn_parts, split(zed))
        if step < NS_STEPS - 1:
            mix = nn3(split(nn3(split(mix), turn_parts)), turn_parts)
    out[...] = zed * (1.0 / jnp.sqrt(bound)) * jnp.concatenate([scale_row, scale_row], axis=1)


def whiten(grams):
    count = grams[0].shape[0]
    return pl.pallas_call(
        functools.partial(whiten_kernel, len(grams)),
        out_shape=jax.ShapeDtypeStruct((2 * count, 2 * count), F32),
        in_specs=[VMEM] * len(grams),
        out_specs=VMEM,
        compiler_params=params(8),
        name="whiten",
    )(*grams)


def update_kernel(nf, lens, whitener, p, re, im, *refs):
    pieces, refs = refs[:nf], refs[nf:]
    coef_re, coef_im, new_re, new_im, squares, d_all = refs
    waves, cols = re.shape
    count = coef_re.shape[1]
    share = waves // nf
    me_f = lax.axis_index("freq")
    for k in range(nf):
        d_all[pl.ds(pl.multiple_of((me_f ^ k) * share, share), share), :] = pieces[k][...]
    turn = split(whitener[...])
    coef = nt3(split(d_all[...]), turn)
    coef_re[...] = coef[:, :count]
    coef_im[...] = coef[:, count:]
    back = nn3(split(coef), turn)
    back_re, back_im = back[:, :count], back[:, count:]
    left = split(
        jnp.concatenate(
            [jnp.concatenate([back_re, -back_im], axis=1), jnp.concatenate([back_im, back_re], axis=1)], axis=0
        )
    )
    live = column(lens[...]) * BIN_BLOCK
    sums = jnp.zeros((waves, 128), F32)
    chunk = min(cols, 512)
    for begin in range(0, cols, chunk):
        part = pl.ds(begin, chunk)
        change = nn3(left, split(p[:, part]))
        keep = lax.broadcasted_iota(jnp.int32, (1, chunk), 1) + (me_f * cols + begin) < live
        now_re = jnp.where(keep, re[:, part] - change[:waves], 0.0)
        now_im = jnp.where(keep, im[:, part] - change[waves:], 0.0)
        new_re[:, part] = now_re
        new_im[:, part] = now_im
        square = now_re * now_re + now_im * now_im
        for at in range(0, chunk, 128):
            sums += square[:, at : at + 128]
    squares[...] = jnp.sum(sums.T, axis=0, keepdims=True)


def update(nf, lens, whitener, p, res_re, res_im, pieces):
    waves, cols = res_re.shape
    count = p.shape[0] // 2
    return pl.pallas_call(
        functools.partial(update_kernel, nf),
        out_shape=[
            jax.ShapeDtypeStruct((waves, count), F32),
            jax.ShapeDtypeStruct((waves, count), F32),
            jax.ShapeDtypeStruct((waves, cols), F32),
            jax.ShapeDtypeStruct((waves, cols), F32),
            jax.ShapeDtypeStruct((1, waves), F32),
        ],
        in_specs=[VMEM] * (5 + nf),
        out_specs=[VMEM] * 5,
        scratch_shapes=[pltpu.VMEM((waves, 2 * count), F32)],
        compiler_params=params(24),
        name="update",
    )(lens, whitener, p, res_re, res_im, *pieces)


def spread(rows, nw, work):
    half = rows.shape[1] // 2
    found = [(0, 0, rows)]
    beside = swap(rows, "wave", nw, 1)
    if nw == 8:
        by_two = swap(rows, "wave", nw, 2)
        by_four = swap(rows, "wave", nw, 4)
        done = work(beside)
        by_two, by_four, _ = lax.optimization_barrier((by_two, by_four, done))
        found.append((2, 0, by_two))
        found.append((4, 0, by_four))
        found.append((6, 0, swap(by_two[:, :half], "wave", nw, 4)))
        found.append((6, half, swap(by_four[:, half:], "wave", nw, 2)))
    else:
        found += [(k, 0, swap(rows, "wave", nw, k)) for k in range(2, nw, 2)]
        done = work(beside)
    return found + [(1, 0, beside)] + [(k + 1, col, swap(array, "wave", nw, 1)) for k, col, array in found[1:]], done


def spread_small(rows, nw):
    found = [rows] + [swap(rows, "wave", nw, k) for k in range(2, nw, 2)]
    both = []
    for array in found:
        both += [array, swap(array, "wave", nw, 1)]
    return both


def sum_pieces(pieces, nf):
    return sum([swap(pieces[k], "freq", nf, k) for k in range(1, nf)], pieces[0])


def sum_over_freq(array, nf):
    return sum([swap(array, "freq", nf, k) for k in range(1, nf)], array)


def capacity(count, nw, rows):
    mean = count / nw
    return min(up(math.ceil(mean + 3.0 * math.sqrt(mean)), 4), count, rows)


def body(nw, nf, res_re, res_im, basis_re, basis_im, lengths, pivots):
    waves, cols = res_re.shape
    nb = basis_re.shape[0]
    count = pivots.shape[0]
    cap = capacity(count, nw, waves)
    lens = lengths.reshape(1, waves)
    zero = jnp.zeros((1,), jnp.int32)
    rows = pick(cap, pivots, lengths, zero, res_re, res_im)
    work = lambda beside: (cross(cap, nw, beside, basis_re, basis_im), orders(cap, nw, waves, nb, cols, pivots))
    found, (partial, ordered) = spread(rows, nw, work)
    select, select_c, rounds, blank_p, blank_c = ordered
    crosses = spread_small(sum_over_freq(partial, nf), nw)
    lists = [array for _, _, array in found]
    places = tuple((k, col) for k, col, _ in found)
    blank_p, blank_c, lists, crosses = lax.optimization_barrier((blank_p, blank_c, lists, crosses))

    def another(carry):
        turn, extra_p, extra_c = carry
        turn, owners = lax.optimization_barrier((turn, pivots // waves))
        more = pick(cap, pivots, lengths, (turn * cap).reshape(1), res_re, res_im)
        more_c = sum_over_freq(cross(cap, nw, more, basis_re, basis_im), nf)[:cap]
        everyone = lambda rows: [rows] + [swap(rows, "wave", nw, k) for k in range(1, nw)]
        earlier = jnp.arange(count)[None, :] < jnp.arange(count)[:, None]
        rank = jnp.sum(((owners[:, None] == owners[None, :]) & earlier).astype(jnp.int32), axis=1) - turn * cap
        group = jnp.bitwise_xor(owners, lax.axis_index("wave").astype(jnp.int32))
        slot = jnp.where((rank >= 0) & (rank < cap), group * cap + rank, -1)
        chosen = (slot[:, None] == jnp.arange(nw * cap)[None, :]).astype(F32)

        def arrange(tables):
            table = jnp.concatenate(tables, axis=0)
            return jnp.dot(chosen, table, precision=lax.Precision.HIGHEST, preferred_element_type=F32)

        all_p = everyone(more)
        added = jnp.concatenate([arrange([p[:cap] for p in all_p]), arrange([p[cap:] for p in all_p])], axis=0)
        first = turn == 1
        extra_p = jnp.where(first, 0.0, extra_p) + added
        extra_c = jnp.where(first, 0.0, extra_c) + arrange(everyone(more_c))
        return turn + 1, extra_p, extra_c

    _, extra_p, extra_c = lax.while_loop(
        lambda carry: carry[0] < rounds[0],
        another,
        (jnp.ones((), jnp.int32), blank_p, blank_c),
    )

    rest = [basis_re, basis_im, res_re, res_im, extra_p, extra_c, *lists, *crosses]
    p, gram, *pieces = project(cap, nw, nf, places, rounds, select, select_c, lens, *rest)
    piece = sum_pieces(pieces, nf)
    grams = [gram] + [swap(gram, "freq", nf, k) for k in range(1, nf)]
    every = [piece] + [swap(piece, "freq", nf, k) for k in range(1, nf)]
    whitener = whiten(grams)
    coef_re, coef_im, new_re, new_im, squares = update(nf, lens, whitener, p, res_re, res_im, every)
    errors = sum_over_freq(squares, nf).reshape(waves) / (BIN_BLOCK * lengths).astype(F32)
    return coef_re, coef_im, new_re, new_im, errors


def solution(mesh):
    nw, nf = mesh.shape["wave"], mesh.shape["freq"]
    return jax.shard_map(
        functools.partial(body, nw, nf),
        mesh=mesh,
        in_specs=(P("wave", "freq"), P("wave", "freq"), P(None, "freq"), P(None, "freq"), P("wave"), P()),
        out_specs=(P("wave", None), P("wave", None), P("wave", "freq"), P("wave", "freq"), P("wave")),
        check_vma=False,
    )
```

time: 120 us -> 91.8 us (0.77)
  between operations: 15 us -> 0.94 us
  Pallas kernels: 39.3 us -> 29.6 us
  waiting for transfers between devices: 14.1 us -> 18.4 us
  other arithmetic: 5.3 us -> 1.49 us
  starting transfers between devices: 38.4 us -> 35.1 us
  local copies, waits for them, and re-layouts: 6.97 us -> 5.15 us
    pallas_call x3, Pallas kernels: 25 us -> 20.4 us  [the longest x1 13.3 us: project(): pl.pallas_call(functools.partial(project_kernel, cap, nw, nf, places), ou...]
    ppermute x31, waiting for transfers between devices: 14.1 us -> 18.4 us  [swap(): return lax.ppermute(array, axis, [(i, i ^ distance) for i in range(size)])]
    ppermute x31, starting transfers between devices: 38.4 us -> 35.1 us  [swap(): return lax.ppermute(array, axis, [(i, i ^ distance) for i in range(size)])]
    unnamed x40 -> x42, local copies, waits for them, and re-layouts: 1.94 us -> 5.12 us
    pallas_call x1, Pallas kernels: 4.04 us -> 2.2 us  [cross(): pl.pallas_call(functools.partial(cross_kernel, cap), out_shape=jax.ShapeD...]
    pallas_call x1, Pallas kernels: 5.08 us -> 3.43 us  [whiten(): pl.pallas_call(functools.partial(whiten_kernel, len(grams)), out_shape=ja...]
    broadcast_in_dim x2 -> x0, local copies, waits for them, and re-layouts: 1.58 us -> none  [the longest x1 1.56 us: body(): jnp.zeros((2 * count, cols), F32)]
    add x2, other arithmetic: 1.62 us -> 0.05 us  [sum_over_freq(): return sum([swap(array, 'freq', nf, k) for k in range(1, nf)], array)]
  transfers between devices with their start and end apart: 31 -> 31, of which waited for: 9 -> 10; matrix products, arithmetic and copies ran while one was open for 6% -> 1% of each run, Pallas kernels for 8% -> 7%
where the time goes in v2:
time: 91.8 us; the launch traced here: 91.5 us
  starting transfers between devices  35.1 us (38%)
  Pallas kernels  29.6 us (32%)
  waiting for transfers between devices  18.4 us (20%)
  local copies, waits for them, and re-layouts  5.15 us (6%)
  other arithmetic  1.49 us (2%)
  between operations  0.94 us (1%)
    ppermute x31, starting transfers between devices, swap(): return lax.ppermute(array, axis, [(i, i ^ distance) for i in range(size)])  35.1 us
    ppermute x31, waiting for transfers between devices, swap(): return lax.ppermute(array, axis, [(i, i ^ distance) for i in range(size)])  18.4 us
    pallas_call x1, Pallas kernels, project(): pl.pallas_call(functools.partial(project_kernel, cap, nw, nf, places), ou...  13.3 us
    pallas_call x1, Pallas kernels, update(): pl.pallas_call(functools.partial(update_kernel, nf), out_shape=[jax.Shape...  6.23 us
    unnamed x42, local copies, waits for them, and re-layouts  5.12 us
    pallas_call x1, Pallas kernels, pick(): pl.pallas_call(functools.partial(pick_kernel, cap), out_shape=jax.ShapeDt...  3.56 us
    pallas_call x1, Pallas kernels, whiten(): pl.pallas_call(functools.partial(whiten_kernel, len(grams)), out_shape=ja...  3.43 us
    pallas_call x1, Pallas kernels, cross(): pl.pallas_call(functools.partial(cross_kernel, cap), out_shape=jax.ShapeD...  2.2 us
  transfers between devices with their start and end apart: 31, of which 10 were waited for; matrix products, arithmetic and copies ran while one was open for 1% of the time, Pallas kernels for 7%

profile of v2, /device:TPU:0, one launch (start us, length us, event | category | flops | bytes accessed | tf_op | source)
XLA Modules:
  0.0 91.5 jit_solution(15001176948112494050)
XLA Ops:
  0.7 3.6 %pick.2.refs_2_ = f32[56,2048]{1,0:T(8,128)S(1)} custom-call(s32[128]{0:T(128)} %piv.1, s32[256]{0:T(256)} %lens.1, s32[1]{0:T(128)} %constant.77.clone.1.skip_ref, f32[256,2048]{1,0:T(8,128)} %re.5, f32[256,2048]{1,0:T(8,128)} %im.5), custom_call_target="tpu_custom_call" | custom-call | tf_op jit(solution)/shard_map/pick/pallas_call | solution.py:120
  4.3 0.9 collective-permute-start.19
  5.2 2.3 %collective-permute-start.18 = (f32[56,2048]{1,0:T(8,128)S(1)}, f32[56,2048]{1,0:T(8,128)S(1)}, u32[]{:S(2)}, u32[]{:S(2)}) collective-permute-start(f32[56,2048]{1,0:T(8,128)S(1)} %pick.2.refs_2_), channel_id=1, source_target_pairs={{0,16},{4,20},{8,24},{12,28},{16,0},{20,4},{24,8},{28,12},{1,17},{... | collective-permute-start | bytes 1376264 | tf_op jit(solution)/shard_map/ppermute | solution.py:42
  7.5 1.6 %collective-permute-start.17 = (f32[56,2048]{1,0:T(8,128)S(1)}, f32[56,2048]{1,0:T(8,128)S(1)}, u32[]{:S(2)}, u32[]{:S(2)}) collective-permute-start(f32[56,2048]{1,0:T(8,128)S(1)} %pick.2.refs_2_), channel_id=1, source_target_pairs={{0,8},{4,12},{8,0},{12,4},{16,24},{20,28},{24,16},{28,20},{1,9},{5... | collective-permute-start | bytes 1376264 | tf_op jit(solution)/shard_map/ppermute | solution.py:42
  9.1 2.2 %cross.6 = f32[64,512]{1,0:T(8,128)S(1)} custom-call(f32[56,2048]{1,0:T(8,128)S(1)} %collective-permute-done.19.rows.refs_7_, f32[256,2048]{1,0:T(8,128)S(1)} %copy-done.9, f32[256,2048]{1,0:T(8,128)S(1)} %copy-done.11), custom_call_target="tpu_custom_call" | custom-call | flops 1000 | bytes 1000 | tf_op jit(solution)/shard_map/cross/pallas_call | solution.py:159
  11.3 3.7 %collective-permute-start.28 = (f32[64,512]{1,0:T(8,128)S(1)}, f32[64,512]{1,0:T(8,128)S(1)}, u32[]{:S(2)}, u32[]{:S(2)}) collective-permute-start(f32[64,512]{1,0:T(8,128)S(1)} %cross.6), channel_id=1, source_target_pairs={{0,3},{1,2},{2,1},{3,0},{4,7},{5,6},{6,5},{7,4},{8,11},{9,10},{10,... | collective-permute-start | bytes 393224 | tf_op jit(solution)/shard_map/ppermute | solution.py:42
  15.0 0.8 collective-permute-start.26
  15.8 0.8 orders.1
  16.7 0.7 copy-done.3
  17.4 0.6 copy-done.4
  18.0 0.6 collective-permute-done.18.refs_4_
  18.6 1.5 %collective-permute-done.17.refs_3_ = f32[56,2048]{1,0:T(8,128)S(1)} collective-permute-done((f32[56,2048]{1,0:T(8,128)S(1)}, f32[56,2048]{1,0:T(8,128)S(1)}, u32[]{:S(2)}, u32[]{:S(2)}) %collective-permute-start.17) | collective-permute-done | bytes 458784 | tf_op jit(solution)/shard_map/ppermute | solution.py:42
  20.2 1.6 %collective-permute-start.21 = (f32[56,1024]{1,0:T(8,128)S(1)}, f32[56,1024]{1,0:T(8,128)S(1)}, u32[]{:S(2)}, u32[]{:S(2)}) collective-permute-start(f32[56,1024]{1,0:T(8,128)S(1)} %slice.126), channel_id=1, source_target_pairs={{0,8},{4,12},{8,0},{12,4},{16,24},{20,28},{24,16},{28,20},{1,9},{5... | collective-permute-start | bytes 688136 | tf_op jit(solution)/shard_map/ppermute | solution.py:42
  21.8 0.7 collective-permute-start.20
  22.5 3.6 %collective-permute-done.27 = f32[64,512]{1,0:T(8,128)S(1)} collective-permute-done((f32[64,512]{1,0:T(8,128)S(1)}, f32[64,512]{1,0:T(8,128)S(1)}, u32[]{:S(2)}, u32[]{:S(2)}) %collective-permute-start.27) | collective-permute-done | bytes 131104 | tf_op jit(solution)/shard_map/ppermute | solution.py:42
  26.2 1.5 %collective-permute-start.34 = (f32[64,512]{1,0:T(8,128)S(1)}, f32[64,512]{1,0:T(8,128)S(1)}, u32[]{:S(2)}, u32[]{:S(2)}) collective-permute-start(f32[64,512]{1,0:T(8,128)S(1)} %add_add_fusion.refs_12_), channel_id=1, source_target_pairs={{0,24},{4,28},{8,16},{12,20},{16,8},{20,12},{24,0},{28,4},{1,25},{... | collective-permute-start | bytes 393224 | tf_op jit(solution)/shard_map/ppermute | solution.py:42
  27.7 0.7 collective-permute-start.32
  28.3 1.4 %collective-permute-start.30 = (f32[64,512]{1,0:T(8,128)S(1)}, f32[64,512]{1,0:T(8,128)S(1)}, u32[]{:S(2)}, u32[]{:S(2)}) collective-permute-start(f32[64,512]{1,0:T(8,128)S(1)} %add_add_fusion.refs_12_), channel_id=1, source_target_pairs={{0,8},{4,12},{8,0},{12,4},{16,24},{20,28},{24,16},{28,20},{1,9},{5... | collective-permute-start | bytes 393224 | tf_op jit(solution)/shard_map/ppermute | solution.py:42
  29.8 0.5 collective-permute-start.23
  30.3 3.0 %collective-permute-done.34.refs_18_ = f32[64,512]{1,0:T(8,128)S(1)} collective-permute-done((f32[64,512]{1,0:T(8,128)S(1)}, f32[64,512]{1,0:T(8,128)S(1)}, u32[]{:S(2)}, u32[]{:S(2)}) %collective-permute-start.34) | collective-permute-done | bytes 131104 | tf_op jit(solution)/shard_map/ppermute | solution.py:42
  33.3 1.3 %collective-permute-done.32.refs_16_ = f32[64,512]{1,0:T(8,128)} collective-permute-done((f32[64,512]{1,0:T(8,128)S(1)}, f32[64,512]{1,0:T(8,128)}, u32[]{:S(2)}, u32[]{:S(2)}) %collective-permute-start.32) | collective-permute-done | bytes 131104 | tf_op jit(solution)/shard_map/ppermute | solution.py:42
  34.6 0.5 collective-permute-start.33
  35.2 0.7 collective-permute-done.35.refs_19_
  36.0 0.7 copy-done.22
  36.8 0.4 collective-permute-start.31
  37.1 1.4 %collective-permute-done.31.refs_15_ = f32[64,512]{1,0:T(8,128)S(1)} collective-permute-done((f32[64,512]{1,0:T(8,128)}, f32[64,512]{1,0:T(8,128)S(1)}, u32[]{:S(2)}, u32[]{:S(2)}) %collective-permute-start.31) | collective-permute-done | bytes 131104 | tf_op jit(solution)/shard_map/ppermute | solution.py:42
  38.5 0.6 copy-done.23
  39.2 0.9 while.15
  40.1 13.3 %project.1 = (f32[256,2048]{1,0:T(8,128)}, f32[128,128]{1,0:T(8,128)}, f32[64,256]{1,0:T(8,128)}, f32[64,256]{1,0:T(8,128)}, f32[64,256]{1,0:T(8,128)}, /*index=5*/f32[64,256]{1,0:T(8,128)}) custom-call(s32[1]{0:T(128)} %get-tuple-element.407.rounds, bf16[256,448]{1,0:T(8,128)(2,1)} %copy-done.3, bf16[128,256]{1,0:T(8,128)(2,1)} %copy-done.4, ...), custom_call_target="tpu_custom_call" | custom-call | tf_op jit(solution)/shard_map/project/pallas_call | solution.py:342
  53.5 1.1 %collective-permute-start.39 = (f32[64,256]{1,0:T(8,128)}, f32[64,256]{1,0:T(8,128)S(1)}, u32[]{:S(2)}, u32[]{:S(2)}) collective-permute-start(f32[64,256]{1,0:T(8,128)} %get-tuple-element.244), channel_id=1, source_target_pairs={{0,1},{1,0},{2,3},{3,2},{4,5},{5,4},{6,7},{7,6},{8,9},{9,8},{10,11... | collective-permute-start | bytes 196616 | tf_op jit(solution)/shard_map/ppermute | solution.py:42
  54.6 2.6 %collective-permute-start.40 = (f32[64,256]{1,0:T(8,128)}, f32[64,256]{1,0:T(8,128)S(1)}, u32[]{:S(2)}, u32[]{:S(2)}) collective-permute-start(f32[64,256]{1,0:T(8,128)} %get-tuple-element.245), channel_id=1, source_target_pairs={{0,2},{1,3},{2,0},{3,1},{4,6},{5,7},{6,4},{7,5},{8,10},{9,11},{10,... | collective-permute-start | bytes 196616 | tf_op jit(solution)/shard_map/ppermute | solution.py:42
  57.2 0.8 collective-permute-start.41
  57.9 3.1 %collective-permute-start.38 = (f32[128,128]{1,0:T(8,128)}, f32[128,128]{1,0:T(8,128)S(1)}, u32[]{:S(2)}, u32[]{:S(2)}) collective-permute-start(f32[128,128]{1,0:T(8,128)} %get-tuple-element.241.refs_0_), channel_id=1, source_target_pairs={{0,3},{1,2},{2,1},{3,0},{4,7},{5,6},{6,5},{7,4},{8,11},{9,10},{10,... | collective-permute-start | bytes 196616 | tf_op jit(solution)/shard_map/ppermute | solution.py:42
  61.0 1.3 %collective-permute-start.36 = (f32[128,128]{1,0:T(8,128)}, f32[128,128]{1,0:T(8,128)S(1)}, u32[]{:S(2)}, u32[]{:S(2)}) collective-permute-start(f32[128,128]{1,0:T(8,128)} %get-tuple-element.241.refs_0_), channel_id=1, source_target_pairs={{0,1},{1,0},{2,3},{3,2},{4,5},{5,4},{6,7},{7,6},{8,9},{9,8},{10,11... | collective-permute-start | bytes 196616 | tf_op jit(solution)/shard_map/ppermute | solution.py:42
  62.3 3.1 %collective-permute-done.40 = f32[64,256]{1,0:T(8,128)S(1)} collective-permute-done((f32[64,256]{1,0:T(8,128)}, f32[64,256]{1,0:T(8,128)S(1)}, u32[]{:S(2)}, u32[]{:S(2)}) %collective-permute-start.40) | collective-permute-done | bytes 65568 | tf_op jit(solution)/shard_map/ppermute | solution.py:42
  65.4 0.9 add_add_fusion.1.refs_0_
  66.3 3.4 %collective-permute-start.44 = (f32[64,256]{1,0:T(8,128)S(1)}, f32[64,256]{1,0:T(8,128)S(1)}, u32[]{:S(2)}, u32[]{:S(2)}) collective-permute-start(f32[64,256]{1,0:T(8,128)S(1)} %add_add_fusion.1.refs_0_), channel_id=1, source_target_pairs={{0,3},{1,2},{2,1},{3,0},{4,7},{5,6},{6,5},{7,4},{8,11},{9,10},{10,... | collective-permute-start | bytes 196616 | tf_op jit(solution)/shard_map/ppermute | solution.py:42
  69.6 1.3 %collective-permute-start.43 = (f32[64,256]{1,0:T(8,128)S(1)}, f32[64,256]{1,0:T(8,128)S(1)}, u32[]{:S(2)}, u32[]{:S(2)}) collective-permute-start(f32[64,256]{1,0:T(8,128)S(1)} %add_add_fusion.1.refs_0_), channel_id=1, source_target_pairs={{0,2},{1,3},{2,0},{3,1},{4,6},{5,7},{6,4},{7,5},{8,10},{9,11},{10,... | collective-permute-start | bytes 196616 | tf_op jit(solution)/shard_map/ppermute | solution.py:42
  70.9 0.5 collective-permute-start.42
  71.5 0.8 copy-done.5
  72.3 3.4 %whiten.1.whitener = f32[256,256]{1,0:T(8,128)S(1)} custom-call(f32[128,128]{1,0:T(8,128)S(1)} %copy-done.5, f32[128,128]{1,0:T(8,128)S(1)} %collective-permute-done.36.refs_1_, f32[128,128]{1,0:T(8,128)S(1)} %collective-permute-done.37.refs_2_, f32[128,128]{1,0:T(8,128)S(1)} %collective-permute-done.38.refs_3_), custom_call_target="tpu_custom_call" | custom-call | tf_op jit(solution)/shard_map/whiten/pallas_call | solution.py:406
  75.8 1.6 %copy-done = f32[256,2048]{1,0:T(8,128)S(1)} copy-done((f32[256,2048]{1,0:T(8,128)S(1)}, f32[256,2048]{1,0:T(8,128)}, u32[]{:S(2)}) %copy-start) | copy-done | bytes 2097176
  77.4 6.2 %update.1 = (f32[256,128]{1,0:T(8,128)}, f32[256,128]{1,0:T(8,128)}, f32[256,2048]{1,0:T(8,128)}, f32[256,2048]{1,0:T(8,128)}, f32[1,256]{1,0:T(1,128)S(1)}) custom-call(s32[1,256]{1,0:T(1,128)S(1)} %bitcast.18, f32[256,256]{1,0:T(8,128)S(1)} %whiten.1.whitener, f32[256,2048]{1,0:T(8,128)S(1)} %copy-done, f32[256,2048]{1,0:T(8,128)S(1)} %copy-done.8, ...), custom_call_target="tpu_custom_call" | custom-call | tf_op jit(solution)/shard_map/update/pallas_call | solution.py:456
  83.6 2.9 %collective-permute-start.47 = (f32[1,256]{1,0:T(1,128)S(1)}, f32[1,256]{1,0:T(1,128)S(1)}, u32[]{:S(2)}, u32[]{:S(2)}) collective-permute-start(f32[1,256]{1,0:T(1,128)S(1)} %get-tuple-element.251), channel_id=1, source_target_pairs={{0,3},{1,2},{2,1},{3,0},{4,7},{5,6},{6,5},{7,4},{8,11},{9,10},{10,... | collective-permute-start | bytes 3080 | tf_op jit(solution)/shard_map/ppermute | solution.py:42
  86.6 1.4 %collective-permute-start.45 = (f32[1,256]{1,0:T(1,128)S(1)}, f32[1,256]{1,0:T(1,128)S(1)}, u32[]{:S(2)}, u32[]{:S(2)}) collective-permute-start(f32[1,256]{1,0:T(1,128)S(1)} %get-tuple-element.251), channel_id=1, source_target_pairs={{0,1},{1,0},{2,3},{3,2},{4,5},{5,4},{6,7},{7,6},{8,9},{9,8},{10,11... | collective-permute-start | bytes 3080 | tf_op jit(solution)/shard_map/ppermute | solution.py:42
  88.0 1.0 %collective-permute-done.47 = f32[1,256]{1,0:T(1,128)S(1)} collective-permute-done((f32[1,256]{1,0:T(1,128)S(1)}, f32[1,256]{1,0:T(1,128)S(1)}, u32[]{:S(2)}, u32[]{:S(2)}) %collective-permute-start.47) | collective-permute-done | bytes 1056 | tf_op jit(solution)/shard_map/ppermute | solution.py:42
  89.0 2.0 %collective-permute-done.46 = f32[1,256]{1,0:T(1,128)S(1)} collective-permute-done((f32[1,256]{1,0:T(1,128)S(1)}, f32[1,256]{1,0:T(1,128)S(1)}, u32[]{:S(2)}, u32[]{:S(2)}) %collective-permute-start.46) | collective-permute-done | bytes 1056 | tf_op jit(solution)/shard_map/ppermute | solution.py:42
  91.0 0.6 convert_divide_fusion
  (70 shorter events, 0.6 us)
Async XLA Ops:
  0.6 8.5 %copy-start.11 = (f32[256,2048]{1,0:T(8,128)S(1)}, f32[256,2048]{1,0:T(8,128)}, u32[]{:S(2)}) copy-start(f32[256,2048]{1,0:T(8,128)} %b_im.3) | copy-start | bytes 6291460
  0.6 8.5 %copy-start.9 = (f32[256,2048]{1,0:T(8,128)S(1)}, f32[256,2048]{1,0:T(8,128)}, u32[]{:S(2)}) copy-start(f32[256,2048]{1,0:T(8,128)} %b_re.3) | copy-start | bytes 6291460
  4.2 7.1 %copy-start.1 = (f32[56,2048]{1,0:T(8,128)}, f32[56,2048]{1,0:T(8,128)S(1)}, u32[]{:S(2)}) copy-start(f32[56,2048]{1,0:T(8,128)S(1)} %pick.2.refs_2_) | copy-start | bytes 1376260
  4.2 11.6 %copy-start.25 = (s32[128]{0:T(128)S(1)}, s32[128]{0:T(128)}, u32[]{:S(2)}) copy-start(s32[128]{0:T(128)} %piv.1) | copy-start | bytes 1540
  4.2 34.9 %copy-start.6 = (f32[256,2048]{1,0:T(8,128)S(1)}, f32[256,2048]{1,0:T(8,128)}, u32[]{:S(2)}) copy-start(f32[256,2048]{1,0:T(8,128)} %re.5) | copy-start | bytes 6291460
  4.3 34.9 %copy-start.24 = (s32[256]{0:T(256)S(1)}, s32[256]{0:T(256)}, u32[]{:S(2)}) copy-start(s32[256]{0:T(256)} %lens.1) | copy-start | bytes 3076
  4.3 4.8 %collective-permute-start.19 = (f32[56,2048]{1,0:T(8,128)S(1)}, f32[56,2048]{1,0:T(8,128)S(1)}, u32[]{:S(2)}, u32[]{:S(2)}) collective-permute-start(f32[56,2048]{1,0:T(8,128)S(1)} %pick.2.refs_2_), channel_id=1, source_target_pairs={{0,4},{4,0},{8,12},{12,8},{16,20},{20,16},{24,28},{28,24},{1,5},{5... | collective-permute-start | bytes 1376264 | tf_op jit(solution)/shard_map/ppermute | solution.py:42
  5.2 13.5 %collective-permute-start.18 = (f32[56,2048]{1,0:T(8,128)S(1)}, f32[56,2048]{1,0:T(8,128)S(1)}, u32[]{:S(2)}, u32[]{:S(2)}) collective-permute-start(f32[56,2048]{1,0:T(8,128)S(1)} %pick.2.refs_2_), channel_id=1, source_target_pairs={{0,16},{4,20},{8,24},{12,28},{16,0},{20,4},{24,8},{28,12},{1,17},{... | collective-permute-start | bytes 1376264 | tf_op jit(solution)/shard_map/ppermute | solution.py:42
  7.5 12.6 %collective-permute-start.17 = (f32[56,2048]{1,0:T(8,128)S(1)}, f32[56,2048]{1,0:T(8,128)S(1)}, u32[]{:S(2)}, u32[]{:S(2)}) collective-permute-start(f32[56,2048]{1,0:T(8,128)S(1)} %pick.2.refs_2_), channel_id=1, source_target_pairs={{0,8},{4,12},{8,0},{12,4},{16,24},{20,28},{24,16},{28,20},{1,9},{5... | collective-permute-start | bytes 1376264 | tf_op jit(solution)/shard_map/ppermute | solution.py:42
  9.1 2.2 %copy-start.2 = (f32[56,2048]{1,0:T(8,128)}, f32[56,2048]{1,0:T(8,128)S(1)}, u32[]{:S(2)}) copy-start(f32[56,2048]{1,0:T(8,128)S(1)} %collective-permute-done.19.rows.refs_7_) | copy-start | bytes 1376260
  11.3 11.1 %collective-permute-start.28 = (f32[64,512]{1,0:T(8,128)S(1)}, f32[64,512]{1,0:T(8,128)S(1)}, u32[]{:S(2)}, u32[]{:S(2)}) collective-permute-start(f32[64,512]{1,0:T(8,128)S(1)} %cross.6), channel_id=1, source_target_pairs={{0,3},{1,2},{2,1},{3,0},{4,7},{5,6},{6,5},{7,4},{8,11},{9,10},{10,... | collective-permute-start | bytes 393224 | tf_op jit(solution)/shard_map/ppermute | solution.py:42
  15.0 11.1 %collective-permute-start.27 = (f32[64,512]{1,0:T(8,128)S(1)}, f32[64,512]{1,0:T(8,128)S(1)}, u32[]{:S(2)}, u32[]{:S(2)}) collective-permute-start(f32[64,512]{1,0:T(8,128)S(1)} %cross.6), channel_id=1, source_target_pairs={{0,2},{1,3},{2,0},{3,1},{4,6},{5,7},{6,4},{7,5},{8,10},{9,11},{10,... | collective-permute-start | bytes 393224 | tf_op jit(solution)/shard_map/ppermute | solution.py:42
  15.0 11.1 %collective-permute-start.26 = (f32[64,512]{1,0:T(8,128)S(1)}, f32[64,512]{1,0:T(8,128)S(1)}, u32[]{:S(2)}, u32[]{:S(2)}) collective-permute-start(f32[64,512]{1,0:T(8,128)S(1)} %cross.6), channel_id=1, source_target_pairs={{0,1},{1,0},{2,3},{3,2},{4,5},{5,4},{6,7},{7,6},{8,9},{9,8},{10,11... | collective-permute-start | bytes 393224 | tf_op jit(solution)/shard_map/ppermute | solution.py:42
  18.6 20.5 %copy-start.15 = (f32[56,2048]{1,0:T(8,128)}, f32[56,2048]{1,0:T(8,128)S(1)}, u32[]{:S(2)}) copy-start(f32[56,2048]{1,0:T(8,128)S(1)} %collective-permute-done.18.refs_4_) | copy-start | bytes 1376260
  20.1 19.1 %copy-start.16 = (f32[56,2048]{1,0:T(8,128)}, f32[56,2048]{1,0:T(8,128)S(1)}, u32[]{:S(2)}) copy-start(f32[56,2048]{1,0:T(8,128)S(1)} %collective-permute-done.17.refs_3_) | copy-start | bytes 1376260
  20.2 9.6 %collective-permute-start.21 = (f32[56,1024]{1,0:T(8,128)S(1)}, f32[56,1024]{1,0:T(8,128)S(1)}, u32[]{:S(2)}, u32[]{:S(2)}) collective-permute-start(f32[56,1024]{1,0:T(8,128)S(1)} %slice.126), channel_id=1, source_target_pairs={{0,8},{4,12},{8,0},{12,4},{16,24},{20,28},{24,16},{28,20},{1,9},{5... | collective-permute-start | bytes 688136 | tf_op jit(solution)/shard_map/ppermute | solution.py:42
  21.8 8.0 %collective-permute-start.20 = (f32[56,1024]{1,0:T(8,128)S(1)}, f32[56,1024]{1,0:T(8,128)}, u32[]{:S(2)}, u32[]{:S(2)}) collective-permute-start(f32[56,1024]{1,0:T(8,128)S(1)} %slice.125), channel_id=1, source_target_pairs={{0,16},{4,20},{8,24},{12,28},{16,0},{20,4},{24,8},{28,12},{1,17},{... | collective-permute-start | bytes 688136 | tf_op jit(solution)/shard_map/ppermute | solution.py:42
  26.2 13.0 %copy-start.17 = (f32[64,512]{1,0:T(8,128)}, f32[64,512]{1,0:T(8,128)S(1)}, u32[]{:S(2)}) copy-start(f32[64,512]{1,0:T(8,128)S(1)} %add_add_fusion.refs_12_) | copy-start | bytes 393220
  26.2 7.1 %collective-permute-start.34 = (f32[64,512]{1,0:T(8,128)S(1)}, f32[64,512]{1,0:T(8,128)S(1)}, u32[]{:S(2)}, u32[]{:S(2)}) collective-permute-start(f32[64,512]{1,0:T(8,128)S(1)} %add_add_fusion.refs_12_), channel_id=1, source_target_pairs={{0,24},{4,28},{8,16},{12,20},{16,8},{20,12},{24,0},{28,4},{1,25},{... | collective-permute-start | bytes 393224 | tf_op jit(solution)/shard_map/ppermute | solution.py:42
  27.7 6.9 %collective-permute-start.32 = (f32[64,512]{1,0:T(8,128)S(1)}, f32[64,512]{1,0:T(8,128)}, u32[]{:S(2)}, u32[]{:S(2)}) collective-permute-start(f32[64,512]{1,0:T(8,128)S(1)} %add_add_fusion.refs_12_), channel_id=1, source_target_pairs={{0,16},{4,20},{8,24},{12,28},{16,0},{20,4},{24,8},{28,12},{1,17},{... | collective-permute-start | bytes 393224 | tf_op jit(solution)/shard_map/ppermute | solution.py:42
  28.3 6.3 %collective-permute-start.30 = (f32[64,512]{1,0:T(8,128)S(1)}, f32[64,512]{1,0:T(8,128)S(1)}, u32[]{:S(2)}, u32[]{:S(2)}) collective-permute-start(f32[64,512]{1,0:T(8,128)S(1)} %add_add_fusion.refs_12_), channel_id=1, source_target_pairs={{0,8},{4,12},{8,0},{12,4},{16,24},{20,28},{24,16},{28,20},{1,9},{5... | collective-permute-start | bytes 393224 | tf_op jit(solution)/shard_map/ppermute | solution.py:42
  29.7 9.5 %copy-start.18 = (f32[56,1024]{1,0:T(8,128)}, f32[56,1024]{1,0:T(8,128)S(1)}, u32[]{:S(2)}) copy-start(f32[56,1024]{1,0:T(8,128)S(1)} %collective-permute-done.21.refs_6_) | copy-start | bytes 688132
  29.7 8.8 %collective-permute-start.22 = (f32[56,2048]{1,0:T(8,128)S(1)}, f32[56,2048]{1,0:T(8,128)}, u32[]{:S(2)}, u32[]{:S(2)}) collective-permute-start(f32[56,2048]{1,0:T(8,128)S(1)} %collective-permute-done.17.refs_3_), channel_id=1, source_target_pairs={{0,4},{4,0},{8,12},{12,8},{16,20},{20,16},{24,28},{28,24},{1,5},{5... | collective-permute-start | bytes 1376264 | tf_op jit(solution)/shard_map/ppermute | solution.py:42
  29.8 8.8 %collective-permute-start.23 = (f32[56,2048]{1,0:T(8,128)S(1)}, f32[56,2048]{1,0:T(8,128)}, u32[]{:S(2)}, u32[]{:S(2)}) collective-permute-start(f32[56,2048]{1,0:T(8,128)S(1)} %collective-permute-done.18.refs_4_), channel_id=1, source_target_pairs={{0,4},{4,0},{8,12},{12,8},{16,20},{20,16},{24,28},{28,24},{1,5},{5... | collective-permute-start | bytes 1376264 | tf_op jit(solution)/shard_map/ppermute | solution.py:42
  33.3 5.9 %copy-start.19 = (f32[64,512]{1,0:T(8,128)}, f32[64,512]{1,0:T(8,128)S(1)}, u32[]{:S(2)}) copy-start(f32[64,512]{1,0:T(8,128)S(1)} %collective-permute-done.34.refs_18_) | copy-start | bytes 393220
  33.3 1.8 %collective-permute-start.29 = (f32[64,512]{1,0:T(8,128)S(1)}, f32[64,512]{1,0:T(8,128)S(1)}, u32[]{:S(2)}, u32[]{:S(2)}) collective-permute-start(f32[64,512]{1,0:T(8,128)S(1)} %add_add_fusion.refs_12_), channel_id=1, source_target_pairs={{0,4},{4,0},{8,12},{12,8},{16,20},{20,16},{24,28},{28,24},{1,5},{5... | collective-permute-start | bytes 393224 | tf_op jit(solution)/shard_map/ppermute | solution.py:42
  34.6 1.3 %collective-permute-start.35 = (f32[64,512]{1,0:T(8,128)S(1)}, f32[64,512]{1,0:T(8,128)S(1)}, u32[]{:S(2)}, u32[]{:S(2)}) collective-permute-start(f32[64,512]{1,0:T(8,128)S(1)} %collective-permute-done.34.refs_18_), channel_id=1, source_target_pairs={{0,4},{4,0},{8,12},{12,8},{16,20},{20,16},{24,28},{28,24},{1,5},{5... | collective-permute-start | bytes 393224 | tf_op jit(solution)/shard_map/ppermute | solution.py:42
  34.6 1.3 %copy-start.20 = (f32[64,512]{1,0:T(8,128)}, f32[64,512]{1,0:T(8,128)S(1)}, u32[]{:S(2)}) copy-start(f32[64,512]{1,0:T(8,128)S(1)} %collective-permute-done.30.refs_14_) | copy-start | bytes 393220
  34.6 2.2 %collective-permute-start.33 = (f32[64,512]{1,0:T(8,128)}, f32[64,512]{1,0:T(8,128)}, u32[]{:S(2)}, u32[]{:S(2)}) collective-permute-start(f32[64,512]{1,0:T(8,128)} %collective-permute-done.32.refs_16_), channel_id=1, source_target_pairs={{0,4},{4,0},{8,12},{12,8},{16,20},{20,16},{24,28},{28,24},{1,5},{5... | collective-permute-start | bytes 393224 | tf_op jit(solution)/shard_map/ppermute | solution.py:42
  35.1 0.8 copy-start.21
  35.1 3.4 %collective-permute-start.25 = (f32[56,1024]{1,0:T(8,128)S(1)}, f32[56,1024]{1,0:T(8,128)}, u32[]{:S(2)}, u32[]{:S(2)}) collective-permute-start(f32[56,1024]{1,0:T(8,128)S(1)} %collective-permute-done.21.refs_6_), channel_id=1, source_target_pairs={{0,4},{4,0},{8,12},{12,8},{16,20},{20,16},{24,28},{28,24},{1,5},{5... | collective-permute-start | bytes 688136 | tf_op jit(solution)/shard_map/ppermute | solution.py:42
  36.6 1.9 %collective-permute-start.24 = (f32[56,1024]{1,0:T(8,128)}, f32[56,1024]{1,0:T(8,128)}, u32[]{:S(2)}, u32[]{:S(2)}) collective-permute-start(f32[56,1024]{1,0:T(8,128)} %collective-permute-done.20.refs_5_), channel_id=1, source_target_pairs={{0,4},{4,0},{8,12},{12,8},{16,20},{20,16},{24,28},{28,24},{1,5},{5... | collective-permute-start | bytes 688136 | tf_op jit(solution)/shard_map/ppermute | solution.py:42
  36.8 1.7 %collective-permute-start.31 = (f32[64,512]{1,0:T(8,128)}, f32[64,512]{1,0:T(8,128)S(1)}, u32[]{:S(2)}, u32[]{:S(2)}) collective-permute-start(f32[64,512]{1,0:T(8,128)} %copy-done.20), channel_id=1, source_target_pairs={{0,4},{4,0},{8,12},{12,8},{16,20},{20,16},{24,28},{28,24},{1,5},{5... | collective-permute-start | bytes 393224 | tf_op jit(solution)/shard_map/ppermute | solution.py:42
  40.1 35.7 %copy-start.8 = (f32[256,2048]{1,0:T(8,128)S(1)}, f32[256,2048]{1,0:T(8,128)}, u32[]{:S(2)}) copy-start(f32[256,2048]{1,0:T(8,128)} %re.5) | copy-start | bytes 6291460
  53.5 7.5 %collective-permute-start.39 = (f32[64,256]{1,0:T(8,128)}, f32[64,256]{1,0:T(8,128)S(1)}, u32[]{:S(2)}, u32[]{:S(2)}) collective-permute-start(f32[64,256]{1,0:T(8,128)} %get-tuple-element.244), channel_id=1, source_target_pairs={{0,1},{1,0},{2,3},{3,2},{4,5},{5,4},{6,7},{7,6},{8,9},{9,8},{10,11... | collective-permute-start | bytes 196616 | tf_op jit(solution)/shard_map/ppermute | solution.py:42
  54.6 10.8 %collective-permute-start.40 = (f32[64,256]{1,0:T(8,128)}, f32[64,256]{1,0:T(8,128)S(1)}, u32[]{:S(2)}, u32[]{:S(2)}) collective-permute-start(f32[64,256]{1,0:T(8,128)} %get-tuple-element.245), channel_id=1, source_target_pairs={{0,2},{1,3},{2,0},{3,1},{4,6},{5,7},{6,4},{7,5},{8,10},{9,11},{10,... | collective-permute-start | bytes 196616 | tf_op jit(solution)/shard_map/ppermute | solution.py:42
  57.2 8.2 %collective-permute-start.41 = (f32[64,256]{1,0:T(8,128)}, f32[64,256]{1,0:T(8,128)S(1)}, u32[]{:S(2)}, u32[]{:S(2)}) collective-permute-start(f32[64,256]{1,0:T(8,128)} %get-tuple-element.246), channel_id=1, source_target_pairs={{0,3},{1,2},{2,1},{3,0},{4,7},{5,6},{6,5},{7,4},{8,11},{9,10},{10,... | collective-permute-start | bytes 196616 | tf_op jit(solution)/shard_map/ppermute | solution.py:42
  57.9 13.0 %collective-permute-start.38 = (f32[128,128]{1,0:T(8,128)}, f32[128,128]{1,0:T(8,128)S(1)}, u32[]{:S(2)}, u32[]{:S(2)}) collective-permute-start(f32[128,128]{1,0:T(8,128)} %get-tuple-element.241.refs_0_), channel_id=1, source_target_pairs={{0,3},{1,2},{2,1},{3,0},{4,7},{5,6},{6,5},{7,4},{8,11},{9,10},{10,... | collective-permute-start | bytes 196616 | tf_op jit(solution)/shard_map/ppermute | solution.py:42
  61.0 10.5 %collective-permute-start.37 = (f32[128,128]{1,0:T(8,128)}, f32[128,128]{1,0:T(8,128)S(1)}, u32[]{:S(2)}, u32[]{:S(2)}) collective-permute-start(f32[128,128]{1,0:T(8,128)} %get-tuple-element.241.refs_0_), channel_id=1, source_target_pairs={{0,2},{1,3},{2,0},{3,1},{4,6},{5,7},{6,4},{7,5},{8,10},{9,11},{10,... | collective-permute-start | bytes 196616 | tf_op jit(solution)/shard_map/ppermute | solution.py:42
  61.0 10.5 %collective-permute-start.36 = (f32[128,128]{1,0:T(8,128)}, f32[128,128]{1,0:T(8,128)S(1)}, u32[]{:S(2)}, u32[]{:S(2)}) collective-permute-start(f32[128,128]{1,0:T(8,128)} %get-tuple-element.241.refs_0_), channel_id=1, source_target_pairs={{0,1},{1,0},{2,3},{3,2},{4,5},{5,4},{6,7},{7,6},{8,9},{9,8},{10,11... | collective-permute-start | bytes 196616 | tf_op jit(solution)/shard_map/ppermute | solution.py:42
  66.3 9.5 %collective-permute-start.44 = (f32[64,256]{1,0:T(8,128)S(1)}, f32[64,256]{1,0:T(8,128)S(1)}, u32[]{:S(2)}, u32[]{:S(2)}) collective-permute-start(f32[64,256]{1,0:T(8,128)S(1)} %add_add_fusion.1.refs_0_), channel_id=1, source_target_pairs={{0,3},{1,2},{2,1},{3,0},{4,7},{5,6},{6,5},{7,4},{8,11},{9,10},{10,... | collective-permute-start | bytes 196616 | tf_op jit(solution)/shard_map/ppermute | solution.py:42
  69.6 6.1 %collective-permute-start.43 = (f32[64,256]{1,0:T(8,128)S(1)}, f32[64,256]{1,0:T(8,128)S(1)}, u32[]{:S(2)}, u32[]{:S(2)}) collective-permute-start(f32[64,256]{1,0:T(8,128)S(1)} %add_add_fusion.1.refs_0_), channel_id=1, source_target_pairs={{0,2},{1,3},{2,0},{3,1},{4,6},{5,7},{6,4},{7,5},{8,10},{9,11},{10,... | collective-permute-start | bytes 196616 | tf_op jit(solution)/shard_map/ppermute | solution.py:42
  70.9 4.8 %collective-permute-start.42 = (f32[64,256]{1,0:T(8,128)S(1)}, f32[64,256]{1,0:T(8,128)S(1)}, u32[]{:S(2)}, u32[]{:S(2)}) collective-permute-start(f32[64,256]{1,0:T(8,128)S(1)} %add_add_fusion.1.refs_0_), channel_id=1, source_target_pairs={{0,1},{1,0},{2,3},{3,2},{4,5},{5,4},{6,7},{7,6},{8,9},{9,8},{10,11... | collective-permute-start | bytes 196616 | tf_op jit(solution)/shard_map/ppermute | solution.py:42
  71.5 0.8 copy-start.5
  75.8 1.6 %copy-start = (f32[256,2048]{1,0:T(8,128)S(1)}, f32[256,2048]{1,0:T(8,128)}, u32[]{:S(2)}) copy-start(f32[256,2048]{1,0:T(8,128)} %get-tuple-element.242.p) | copy-start | bytes 6291460
  83.6 5.4 %collective-permute-start.47 = (f32[1,256]{1,0:T(1,128)S(1)}, f32[1,256]{1,0:T(1,128)S(1)}, u32[]{:S(2)}, u32[]{:S(2)}) collective-permute-start(f32[1,256]{1,0:T(1,128)S(1)} %get-tuple-element.251), channel_id=1, source_target_pairs={{0,3},{1,2},{2,1},{3,0},{4,7},{5,6},{6,5},{7,4},{8,11},{9,10},{10,... | collective-permute-start | bytes 3080 | tf_op jit(solution)/shard_map/ppermute | solution.py:42
  86.5 4.5 %collective-permute-start.46 = (f32[1,256]{1,0:T(1,128)S(1)}, f32[1,256]{1,0:T(1,128)S(1)}, u32[]{:S(2)}, u32[]{:S(2)}) collective-permute-start(f32[1,256]{1,0:T(1,128)S(1)} %get-tuple-element.251), channel_id=1, source_target_pairs={{0,2},{1,3},{2,0},{3,1},{4,6},{5,7},{6,4},{7,5},{8,10},{9,11},{10,... | collective-permute-start | bytes 3080 | tf_op jit(solution)/shard_map/ppermute | solution.py:42
  86.6 4.4 %collective-permute-start.45 = (f32[1,256]{1,0:T(1,128)S(1)}, f32[1,256]{1,0:T(1,128)S(1)}, u32[]{:S(2)}, u32[]{:S(2)}) collective-permute-start(f32[1,256]{1,0:T(1,128)S(1)} %get-tuple-element.251), channel_id=1, source_target_pairs={{0,1},{1,0},{2,3},{3,2},{4,5},{5,4},{6,7},{7,6},{8,9},{9,8},{10,11... | collective-permute-start | bytes 3080 | tf_op jit(solution)/shard_map/ppermute | solution.py:42
  (4 other events, 2.7 us)

commit v3 on v2

--- a/solution.py
+++ b/solution.py
@@ -187,7 +187,7 @@
     return copy
 
 
-def orders_kernel(cap, nw, waves, pr, listed, crossed, rounds, blank_p, blank_c):
+def orders_kernel(cap, nw, waves, pr, listed, crossed, rounds):
     owner, rank = ranks(column(pr[...]), pr[...], waves)
     group = jnp.bitwise_xor(owner, lax.axis_index("wave"))
     rounds[0] = jnp.max(rank) // cap + 1
@@ -198,7 +198,7 @@
     crossed[...] = one_hot(jnp.where(rank < cap, group * capp + rank, -1), crossed.shape[1])
 
 
-def orders(cap, nw, waves, nb, cols, pivots):
+def orders(cap, nw, waves, pivots):
     count = pivots.shape[0]
     return pl.pallas_call(
         functools.partial(orders_kernel, cap, nw, waves),
@@ -206,11 +206,9 @@
             jax.ShapeDtypeStruct((2 * count, nw * 2 * cap), BF16),
             jax.ShapeDtypeStruct((count, nw * up(cap, 8)), BF16),
             jax.ShapeDtypeStruct((1,), jnp.int32),
-            jax.ShapeDtypeStruct((2 * count, cols), F32),
-            jax.ShapeDtypeStruct((count, 2 * nb), F32),
         ),
         in_specs=[VMEM],
-        out_specs=(VMEM, VMEM, SMEM, HBM, HBM),
+        out_specs=(VMEM, VMEM, SMEM),
         compiler_params=params(8),
         cost_estimate=light(),
         name="orders",
@@ -237,33 +235,18 @@
     return real, imag
 
 
-def stack_columns(pair_re, pair_im, target, chunk, sem):
-    rows, cols = pair_re.shape
-    waits = []
-    for step in range(cols // chunk):
-        part = pl.ds(step * chunk, chunk)
-        waits.append(
-            [
-                move(pair_re.at[:, part], target.at[pl.ds(0, rows), part], sem.at[step, 0]),
-                move(pair_im.at[:, part], target.at[pl.ds(rows, rows), part], sem.at[step, 1]),
-            ]
-        )
-    return waits
-
-
-def project_kernel(cap, nw, nf, places, rounds, select, select_c, lens, b_re, b_im, re, im, *refs):
-    extra_p, extra_c, refs = refs[0], refs[1], refs[2:]
+def project_kernel(cap, nw, nf, places, select, select_c, lens, b_re, b_im, re, im, *refs):
     list_refs, refs = refs[: len(places)], refs[len(places) :]
     cross_refs, refs = refs[:nw], refs[nw:]
     p_out, g_out, refs = refs[0], refs[1], refs[2:]
     out, refs = refs[:nf], refs[nf:]
-    gathered, crossed, gram_b, basis, live, placed, more_p, more_c, d_all, sem_l, sem_c, sem_b, sem_x = refs
+    gathered, crossed, gram_b, d_all, sem_l, sem_c = refs
     count = select_c.shape[0]
     nb, cols = b_re.shape
     waves = re.shape[0]
     capp = up(cap, 8)
     mine = nb // nw
-    me_w, me_f, over = lax.axis_index("wave"), lax.axis_index("freq"), rounds[0] > 1
+    me_w, me_f = lax.axis_index("wave"), lax.axis_index("freq")
     waits = []
     for k, ref in enumerate(cross_refs):
         at = (k ^ 1) * capp
@@ -273,28 +256,17 @@
     list_waits = fetch_lists(list_refs, places, cap, gathered, sem_l)
     chunk = min(cols, 1024)
 
-    @pl.when(over)
-    def _():
-        first = pltpu.make_async_copy(extra_p, more_p, sem_x.at[0])
-        second = pltpu.make_async_copy(extra_c, more_c, sem_x.at[1])
-        first.start()
-        second.start()
-        first.wait()
-        second.wait()
-
     for copy in list_waits:
         copy.wait()
-    basis_waits = stack_columns(b_re, b_im, basis, chunk, sem_b)
     for step in range(cols // chunk):
         part = pl.ds(step * chunk, chunk)
         high, low = split(gathered[:, part])
         block = nn(select[...], high) + nn(select[...], low)
-        placed[:, part] = block + jnp.where(over, more_p[:, part], 0.0)
+        p_out[:, part] = block
     for copy in waits:
         copy.wait()
     pieces = split3(crossed[...])
     cross_all = nn(select_c[...], pieces[0]) + (nn(select_c[...], pieces[1]) + nn(select_c[...], pieces[2]))
-    cross_all = cross_all + jnp.where(over, more_c[...], 0.0)
     stacked = jnp.concatenate([cross_all[:, :nb], cross_all[:, nb:]], axis=0)
     twist = nn3(split(stacked), split(gram_b[...]))
     total_re = 2.0 * cross_all[:, :nb] - (twist[:count, :nb] - twist[count:, nb:])
@@ -304,35 +276,26 @@
             [jnp.concatenate([total_re, -total_im], axis=1), jnp.concatenate([total_im, total_re], axis=1)], axis=0
         )
     )
-    live_waits = [
-        move(re, live.at[pl.ds(0, waves)], sem_x.at[2]),
-        move(im, live.at[pl.ds(waves, waves)], sem_x.at[3]),
-    ]
     for step in range(cols // chunk):
         part = pl.ds(step * chunk, chunk)
-        for copy in basis_waits[step]:
-            copy.wait()
-        placed[:, part] = placed[:, part] - nn3(take, split(basis[:, part]))
-    p_wait = move(placed, p_out, sem_x.at[4])
-    right = split(placed[...])
+        basis = jnp.concatenate([b_re[:, part], b_im[:, part]], axis=0)
+        p_out[:, part] = p_out[:, part] - nn3(take, split(basis))
+    right = split(p_out[...])
     inner_p = nt(right[0], right[0])
     inner_q = nt(right[0], right[1])
-    for copy in live_waits:
-        copy.wait()
     end = column(lens[...]) * BIN_BLOCK
     keep = lax.broadcasted_iota(jnp.int32, (1, cols), 1) + me_f * cols < end
-    inner_re = nt3(split(jnp.where(keep, live[0:waves, :], 0.0)), right)
-    inner_im = nt3(split(jnp.where(keep, live[waves : 2 * waves, :], 0.0)), right)
+    inner_re = nt3(split(jnp.where(keep, re[...], 0.0)), right)
+    inner_im = nt3(split(jnp.where(keep, im[...], 0.0)), right)
     inner_r = jnp.concatenate([inner_re, inner_im], axis=0)
     g_out[...] = packed(*joined(inner_p + (inner_q + inner_q.T), count, count))
     d_all[:, :count], d_all[:, count:] = joined(inner_r, waves, count)
     share = waves // nf
     for k in range(nf):
         out[k][...] = d_all[pl.ds(pl.multiple_of((me_f ^ k) * share, share), share), :]
-    p_wait.wait()
-
-
-def project(cap, nw, nf, places, rounds, select, select_c, lens, *rest):
+
+
+def project(cap, nw, nf, places, select, select_c, lens, *rest):
     basis_re, res_re = rest[0], rest[2]
     count = select_c.shape[0]
     nb, cols = basis_re.shape
@@ -342,26 +305,19 @@
     return pl.pallas_call(
         functools.partial(project_kernel, cap, nw, nf, places),
         out_shape=shapes,
-        in_specs=[SMEM] + [VMEM] * 3 + [HBM] * len(rest),
-        out_specs=[HBM] + [VMEM] * (len(shapes) - 1),
+        in_specs=[VMEM] * 7 + [HBM] * (len(rest) - 4),
+        out_specs=[VMEM] * len(shapes),
         scratch_shapes=[
             pltpu.VMEM((select.shape[1], cols), F32),
             pltpu.VMEM((nw * up(cap, 8), 2 * nb), F32),
             pltpu.VMEM((nb, 2 * nb), F32),
-            pltpu.VMEM((2 * nb, cols), F32),
-            pltpu.VMEM((2 * waves, cols), F32),
-            pltpu.VMEM((2 * count, cols), F32),
-            pltpu.VMEM((2 * count, cols), F32),
-            pltpu.VMEM((count, 2 * nb), F32),
             pltpu.VMEM((waves, 2 * count), F32),
             pltpu.SemaphoreType.DMA((len(places),)),
             pltpu.SemaphoreType.DMA((2 * nw,)),
-            pltpu.SemaphoreType.DMA((cols // min(cols, 1024), 2)),
-            pltpu.SemaphoreType.DMA((5,)),
         ],
-        compiler_params=params(61),
+        compiler_params=params(36),
         name="project",
-    )(rounds, select, select_c, lens, *rest)
+    )(select, select_c, lens, *rest)
 
 
 def whiten_kernel(nf, *refs):
@@ -518,52 +474,70 @@
     lens = lengths.reshape(1, waves)
     zero = jnp.zeros((1,), jnp.int32)
     rows = pick(cap, pivots, lengths, zero, res_re, res_im)
-    work = lambda beside: (cross(cap, nw, beside, basis_re, basis_im), orders(cap, nw, waves, nb, cols, pivots))
+    work = lambda beside: (cross(cap, nw, beside, basis_re, basis_im), orders(cap, nw, waves, pivots))
     found, (partial, ordered) = spread(rows, nw, work)
-    select, select_c, rounds, blank_p, blank_c = ordered
+    select, select_c, rounds = ordered
     crosses = spread_small(sum_over_freq(partial, nf), nw)
     lists = [array for _, _, array in found]
     places = tuple((k, col) for k, col, _ in found)
-    blank_p, blank_c, lists, crosses = lax.optimization_barrier((blank_p, blank_c, lists, crosses))
-
-    def another(carry):
-        turn, extra_p, extra_c = carry
-        turn, owners = lax.optimization_barrier((turn, pivots // waves))
-        more = pick(cap, pivots, lengths, (turn * cap).reshape(1), res_re, res_im)
-        more_c = sum_over_freq(cross(cap, nw, more, basis_re, basis_im), nf)[:cap]
-        everyone = lambda rows: [rows] + [swap(rows, "wave", nw, k) for k in range(1, nw)]
-        earlier = jnp.arange(count)[None, :] < jnp.arange(count)[:, None]
-        rank = jnp.sum(((owners[:, None] == owners[None, :]) & earlier).astype(jnp.int32), axis=1) - turn * cap
-        group = jnp.bitwise_xor(owners, lax.axis_index("wave").astype(jnp.int32))
-        slot = jnp.where((rank >= 0) & (rank < cap), group * cap + rank, -1)
-        chosen = (slot[:, None] == jnp.arange(nw * cap)[None, :]).astype(F32)
-
-        def arrange(tables):
-            table = jnp.concatenate(tables, axis=0)
-            return jnp.dot(chosen, table, precision=lax.Precision.HIGHEST, preferred_element_type=F32)
-
-        all_p = everyone(more)
-        added = jnp.concatenate([arrange([p[:cap] for p in all_p]), arrange([p[cap:] for p in all_p])], axis=0)
-        first = turn == 1
-        extra_p = jnp.where(first, 0.0, extra_p) + added
-        extra_c = jnp.where(first, 0.0, extra_c) + arrange(everyone(more_c))
-        return turn + 1, extra_p, extra_c
-
-    _, extra_p, extra_c = lax.while_loop(
-        lambda carry: carry[0] < rounds[0],
-        another,
-        (jnp.ones((), jnp.int32), blank_p, blank_c),
-    )
-
-    rest = [basis_re, basis_im, res_re, res_im, extra_p, extra_c, *lists, *crosses]
-    p, gram, *pieces = project(cap, nw, nf, places, rounds, select, select_c, lens, *rest)
+    rest = [basis_re, basis_im, res_re, res_im, *lists, *crosses]
+    p, gram, *pieces = project(cap, nw, nf, places, select, select_c, lens, *rest)
     piece = sum_pieces(pieces, nf)
     grams = [gram] + [swap(gram, "freq", nf, k) for k in range(1, nf)]
     every = [piece] + [swap(piece, "freq", nf, k) for k in range(1, nf)]
     whitener = whiten(grams)
     coef_re, coef_im, new_re, new_im, squares = update(nf, lens, whitener, p, res_re, res_im, every)
     errors = sum_over_freq(squares, nf).reshape(waves) / (BIN_BLOCK * lengths).astype(F32)
-    return coef_re, coef_im, new_re, new_im, errors
+    made = (coef_re, coef_im, new_re, new_im, errors)
+
+    def again(carry):
+        turn, given = lax.optimization_barrier((carry[0], (res_re, res_im, basis_re, basis_im, lengths, pivots)))
+        return turn + 1, plainly(nw, nf, *given)
+
+    _, made = lax.while_loop(lambda carry: carry[0] < rounds[0].clip(1, 2), again, (jnp.ones((), jnp.int32), made))
+    return made
+
+
+def plainly(nw, nf, res_re, res_im, basis_re, basis_im, lengths, pivots):
+    waves, cols = res_re.shape
+    count = pivots.shape[0]
+    nb = basis_re.shape[0]
+
+    def total(array, axis, size):
+        for bit in range(size.bit_length() - 1):
+            array = array + swap(array, axis, size, 1 << bit)
+        return array
+
+    exact = dict(precision=lax.Precision.HIGHEST, preferred_element_type=F32)
+    dot = functools.partial(jnp.dot, **exact)
+    dot_t = lambda left, right: lax.dot_general(left, right, (((1,), (1,)), ((), ())), **exact)
+    pair = lambda real, imag: jnp.concatenate([real, imag], axis=0)
+    bins = lax.axis_index("freq") * cols + jnp.arange(cols, dtype=jnp.int32)
+    mask = (bins[None, :] < BIN_BLOCK * lengths[:, None]).astype(F32)
+    live = pair(res_re * mask, res_im * mask)
+    owned = lax.axis_index("wave") * waves + jnp.arange(waves, dtype=jnp.int32)
+    select = (pivots[:, None] == owned[None, :]).astype(F32)
+    pivot = total(pair(dot(select, live[:waves]), dot(select, live[waves:])), "wave", nw)
+    basis = pair(basis_re, basis_im)
+
+    def inner(left, right, rows, columns):
+        return joined(total(dot_t(left, right), "freq", nf), rows, columns)
+
+    for _ in range(2):
+        take_re, take_im = inner(pivot, basis, count, nb)
+        pivot = pivot - pair(
+            dot(take_re, basis_re) - dot(take_im, basis_im), dot(take_re, basis_im) + dot(take_im, basis_re)
+        )
+    whitener = whiten([packed(*inner(pivot, pivot, count, count))])
+    pieces = jnp.concatenate(inner(live, pivot, waves, count), axis=1)
+    coef = dot_t(pieces, whitener)
+    back = dot(coef, whitener)
+    back_re, back_im = back[:, :count], back[:, count:]
+    new_re = (live[:waves] - dot(back_re, pivot[:count]) + dot(back_im, pivot[count:])) * mask
+    new_im = (live[waves:] - dot(back_re, pivot[count:]) - dot(back_im, pivot[:count])) * mask
+    squares = total(jnp.sum(new_re * new_re + new_im * new_im, axis=1), "freq", nf)
+    errors = squares / (BIN_BLOCK * lengths).astype(F32)
+    return coef[:, :count], coef[:, count:], new_re, new_im, errors
 
 
 def solution(mesh):

time: 91.8 us -> 86.4 us (0.941)
  local copies, waits for them, and re-layouts: 5.15 us -> 0.07 us
  Pallas kernels: 29.6 us -> 25.3 us
  waiting for transfers between devices: 18.4 us -> 21.9 us
  starting transfers between devices: 35.1 us -> 36.3 us
    unnamed x42 -> x12, local copies, waits for them, and re-layouts: 5.12 us -> 0.04 us
    ppermute x31, waiting for transfers between devices: 18.4 us -> 21.9 us  [swap(): return lax.ppermute(array, axis, [(i, i ^ distance) for i in range(size)])]
    pallas_call x1, Pallas kernels: 13.3 us -> 10.7 us  [project(): pl.pallas_call(functools.partial(project_kernel, cap, nw, nf, places), ou...]
    pallas_call x1, Pallas kernels: 6.23 us -> 4.69 us  [update(): pl.pallas_call(functools.partial(update_kernel, nf), out_shape=[jax.Shape...]
    ppermute x31, starting transfers between devices: 35.1 us -> 36.3 us  [swap(): return lax.ppermute(array, axis, [(i, i ^ distance) for i in range(size)])]
  transfers between devices with their start and end apart: 31 -> 31, of which waited for: 10 -> 14; matrix products, arithmetic and copies ran while one was open for 1% -> 0% of each run, Pallas kernels for 7% -> 7%
where the time goes in v3:
time: 86.4 us; the launch traced here: 86.2 us
  starting transfers between devices  36.3 us (42%)
  Pallas kernels  25.3 us (29%)
  waiting for transfers between devices  21.9 us (25%)
  between operations  1.02 us (1%)
  loops' own time  0.89 us (1%)
    ppermute x31, starting transfers between devices, swap(): return lax.ppermute(array, axis, [(i, i ^ distance) for i in range(size)])  36.3 us
    ppermute x31, waiting for transfers between devices, swap(): return lax.ppermute(array, axis, [(i, i ^ distance) for i in range(size)])  21.9 us
    pallas_call x1, Pallas kernels, project(): pl.pallas_call(functools.partial(project_kernel, cap, nw, nf, places), ou...  10.7 us
    pallas_call x1, Pallas kernels, update(): pl.pallas_call(functools.partial(update_kernel, nf), out_shape=[jax.Shape...  4.69 us
    pallas_call x1, Pallas kernels, pick(): pl.pallas_call(functools.partial(pick_kernel, cap), out_shape=jax.ShapeDt...  3.53 us
    pallas_call x1, Pallas kernels, whiten(): pl.pallas_call(functools.partial(whiten_kernel, len(grams)), out_shape=ja...  3.42 us
    pallas_call x1, Pallas kernels, cross(): pl.pallas_call(functools.partial(cross_kernel, cap), out_shape=jax.ShapeD...  2.2 us
  transfers between devices with their start and end apart: 31, of which 14 were waited for; matrix products, arithmetic and copies ran while one was open for 0% of the time, Pallas kernels for 7%

profile of v3, /device:TPU:0, one launch (start us, length us, event | category | flops | bytes accessed | tf_op | source)
XLA Modules:
  0.0 86.2 jit_solution(14822922881993119336)
XLA Ops:
  0.7 3.5 %pick.1.refs_0_ = f32[56,2048]{1,0:T(8,128)S(1)} custom-call(s32[128]{0:T(128)} %piv.1, s32[256]{0:T(256)} %lens.1, s32[1]{0:T(128)} %constant.34.clone.1.skip_ref, f32[256,2048]{1,0:T(8,128)} %re.5, f32[256,2048]{1,0:T(8,128)} %im.5), custom_call_target="tpu_custom_call" | custom-call | tf_op jit(solution)/shard_map/pick/pallas_call | solution.py:120
  4.2 0.0 copy-start.7
  4.2 1.1 %collective-permute-start.15 = (f32[56,2048]{1,0:T(8,128)S(1)}, f32[56,2048]{1,0:T(8,128)S(1)}, u32[]{:S(2)}, u32[]{:S(2)}) collective-permute-start(f32[56,2048]{1,0:T(8,128)S(1)} %pick.1.refs_0_), channel_id=1, source_target_pairs={{0,4},{4,0},{8,12},{12,8},{16,20},{20,16},{24,28},{28,24},{1,5},{5... | collective-permute-start | bytes 1376264 | tf_op jit(solution)/shard_map/ppermute | solution.py:42
  5.3 2.6 %collective-permute-start.13 = (f32[56,2048]{1,0:T(8,128)S(1)}, f32[56,2048]{1,0:T(8,128)S(1)}, u32[]{:S(2)}, u32[]{:S(2)}) collective-permute-start(f32[56,2048]{1,0:T(8,128)S(1)} %pick.1.refs_0_), channel_id=1, source_target_pairs={{0,8},{4,12},{8,0},{12,4},{16,24},{20,28},{24,16},{28,20},{1,9},{5... | collective-permute-start | bytes 1376264 | tf_op jit(solution)/shard_map/ppermute | solution.py:42
  7.9 1.2 %collective-permute-start.14 = (f32[56,2048]{1,0:T(8,128)S(1)}, f32[56,2048]{1,0:T(8,128)S(1)}, u32[]{:S(2)}, u32[]{:S(2)}) collective-permute-start(f32[56,2048]{1,0:T(8,128)S(1)} %pick.1.refs_0_), channel_id=1, source_target_pairs={{0,16},{4,20},{8,24},{12,28},{16,0},{20,4},{24,8},{28,12},{1,17},{... | collective-permute-start | bytes 1376264 | tf_op jit(solution)/shard_map/ppermute | solution.py:42
  9.1 2.2 %cross.1 = f32[64,512]{1,0:T(8,128)S(1)} custom-call(f32[56,2048]{1,0:T(8,128)S(1)} %collective-permute-done.15.rows.refs_5_, f32[256,2048]{1,0:T(8,128)S(1)} %copy-done, f32[256,2048]{1,0:T(8,128)S(1)} %copy-done.1), custom_call_target="tpu_custom_call" | custom-call | flops 1000 | bytes 1000 | tf_op jit(solution)/shard_map/cross/pallas_call | solution.py:159
  11.3 1.6 %collective-permute-start.22 = (f32[64,512]{1,0:T(8,128)S(1)}, f32[64,512]{1,0:T(8,128)S(1)}, u32[]{:S(2)}, u32[]{:S(2)}) collective-permute-start(f32[64,512]{1,0:T(8,128)S(1)} %cross.1), channel_id=1, source_target_pairs={{0,1},{1,0},{2,3},{3,2},{4,5},{5,4},{6,7},{7,6},{8,9},{9,8},{10,11... | collective-permute-start | bytes 393224 | tf_op jit(solution)/shard_map/ppermute | solution.py:42
  12.9 2.6 %collective-permute-start.23 = (f32[64,512]{1,0:T(8,128)S(1)}, f32[64,512]{1,0:T(8,128)S(1)}, u32[]{:S(2)}, u32[]{:S(2)}) collective-permute-start(f32[64,512]{1,0:T(8,128)S(1)} %cross.1), channel_id=1, source_target_pairs={{0,2},{1,3},{2,0},{3,1},{4,6},{5,7},{6,4},{7,5},{8,10},{9,11},{10,... | collective-permute-start | bytes 393224 | tf_op jit(solution)/shard_map/ppermute | solution.py:42
  15.5 0.2 collective-permute-start.24
  15.7 0.8 orders.1
  16.6 2.4 %collective-permute-done.13.refs_1_ = f32[56,2048]{1,0:T(8,128)S(1)} collective-permute-done((f32[56,2048]{1,0:T(8,128)S(1)}, f32[56,2048]{1,0:T(8,128)S(1)}, u32[]{:S(2)}, u32[]{:S(2)}) %collective-permute-start.13) | collective-permute-done | bytes 458784 | tf_op jit(solution)/shard_map/ppermute | solution.py:42
  19.0 1.5 %collective-permute-done.14.refs_2_ = f32[56,2048]{1,0:T(8,128)S(1)} collective-permute-done((f32[56,2048]{1,0:T(8,128)S(1)}, f32[56,2048]{1,0:T(8,128)S(1)}, u32[]{:S(2)}, u32[]{:S(2)}) %collective-permute-start.14) | collective-permute-done | bytes 458784 | tf_op jit(solution)/shard_map/ppermute | solution.py:42
  20.5 1.0 %collective-permute-start.16 = (f32[56,1024]{1,0:T(8,128)S(1)}, f32[56,1024]{1,0:T(8,128)S(1)}, u32[]{:S(2)}, u32[]{:S(2)}) collective-permute-start(f32[56,1024]{1,0:T(8,128)S(1)} %slice.74), channel_id=1, source_target_pairs={{0,16},{4,20},{8,24},{12,28},{16,0},{20,4},{24,8},{28,12},{1,17},{... | collective-permute-start | bytes 688136 | tf_op jit(solution)/shard_map/ppermute | solution.py:42
  21.5 0.9 %collective-permute-start.17 = (f32[56,1024]{1,0:T(8,128)S(1)}, f32[56,1024]{1,0:T(8,128)S(1)}, u32[]{:S(2)}, u32[]{:S(2)}) collective-permute-start(f32[56,1024]{1,0:T(8,128)S(1)} %slice.75), channel_id=1, source_target_pairs={{0,8},{4,12},{8,0},{12,4},{16,24},{20,28},{24,16},{28,20},{1,9},{5... | collective-permute-start | bytes 688136 | tf_op jit(solution)/shard_map/ppermute | solution.py:42
  22.4 3.2 %collective-permute-done.23 = f32[64,512]{1,0:T(8,128)S(1)} collective-permute-done((f32[64,512]{1,0:T(8,128)S(1)}, f32[64,512]{1,0:T(8,128)S(1)}, u32[]{:S(2)}, u32[]{:S(2)}) %collective-permute-start.23) | collective-permute-done | bytes 131104 | tf_op jit(solution)/shard_map/ppermute | solution.py:42
  25.7 0.9 collective-permute-start.26
  26.5 0.9 %collective-permute-start.28 = (f32[64,512]{1,0:T(8,128)S(1)}, f32[64,512]{1,0:T(8,128)S(1)}, u32[]{:S(2)}, u32[]{:S(2)}) collective-permute-start(f32[64,512]{1,0:T(8,128)S(1)} %add_add_fusion.refs_10_), channel_id=1, source_target_pairs={{0,16},{4,20},{8,24},{12,28},{16,0},{20,4},{24,8},{28,12},{1,17},{... | collective-permute-start | bytes 393224 | tf_op jit(solution)/shard_map/ppermute | solution.py:42
  27.4 0.5 collective-permute-done.16.refs_3_
  27.9 1.3 %collective-permute-done.17.refs_4_ = f32[56,1024]{1,0:T(8,128)S(1)} collective-permute-done((f32[56,1024]{1,0:T(8,128)S(1)}, f32[56,1024]{1,0:T(8,128)S(1)}, u32[]{:S(2)}, u32[]{:S(2)}) %collective-permute-start.17) | collective-permute-done | bytes 229408 | tf_op jit(solution)/shard_map/ppermute | solution.py:42
  29.2 1.4 %collective-permute-start.30 = (f32[64,512]{1,0:T(8,128)S(1)}, f32[64,512]{1,0:T(8,128)S(1)}, u32[]{:S(2)}, u32[]{:S(2)}) collective-permute-start(f32[64,512]{1,0:T(8,128)S(1)} %add_add_fusion.refs_10_), channel_id=1, source_target_pairs={{0,24},{4,28},{8,16},{12,20},{16,8},{20,12},{24,0},{28,4},{1,25},{... | collective-permute-start | bytes 393224 | tf_op jit(solution)/shard_map/ppermute | solution.py:42
  30.6 0.1 collective-permute-done.26.refs_12_
  30.7 0.8 collective-permute-done.28.refs_14_
  31.5 3.6 %collective-permute-done.30.refs_16_ = f32[64,512]{1,0:T(8,128)S(1)} collective-permute-done((f32[64,512]{1,0:T(8,128)S(1)}, f32[64,512]{1,0:T(8,128)S(1)}, u32[]{:S(2)}, u32[]{:S(2)}) %collective-permute-start.30) | collective-permute-done | bytes 131104 | tf_op jit(solution)/shard_map/ppermute | solution.py:42
  35.1 0.5 collective-permute-start.20
  35.6 0.1 collective-permute-start.21
  35.7 0.8 collective-permute-done.29.refs_15_
  36.4 0.1 collective-permute-start.31
  36.6 1.2 %collective-permute-done.31.refs_17_ = f32[64,512]{1,0:T(8,128)S(1)} collective-permute-done((f32[64,512]{1,0:T(8,128)S(1)}, f32[64,512]{1,0:T(8,128)S(1)}, u32[]{:S(2)}, u32[]{:S(2)}) %collective-permute-start.31) | collective-permute-done | bytes 131104 | tf_op jit(solution)/shard_map/ppermute | solution.py:42
  37.8 10.7 %project.1 = (f32[256,2048]{1,0:T(8,128)S(1)}, f32[128,128]{1,0:T(8,128)S(1)}, f32[64,256]{1,0:T(8,128)S(1)}, f32[64,256]{1,0:T(8,128)S(1)}, f32[64,256]{1,0:T(8,128)S(1)}, /*index=5*/f32[64,256]{1,0:T(8,128)S(1)}) custom-call(bf16[256,448]{1,0:T(8,128)(2,1)S(1)} %get-tuple-element.95.select, bf16[128,256]{1,0:T(8,128)(2,1)S(1)} %get-tuple-element.96.select_c, ...), custom_call_target="tpu_custom_call" | custom-call | tf_op jit(solution)/shard_map/project/pallas_call | solution.py:305
  48.5 1.8 %collective-permute-start.35 = (f32[64,256]{1,0:T(8,128)S(1)}, f32[64,256]{1,0:T(8,128)S(1)}, u32[]{:S(2)}, u32[]{:S(2)}) collective-permute-start(f32[64,256]{1,0:T(8,128)S(1)} %get-tuple-element.103), channel_id=1, source_target_pairs={{0,1},{1,0},{2,3},{3,2},{4,5},{5,4},{6,7},{7,6},{8,9},{9,8},{10,11... | collective-permute-start | bytes 196616 | tf_op jit(solution)/shard_map/ppermute | solution.py:42
  50.3 3.0 %collective-permute-start.36 = (f32[64,256]{1,0:T(8,128)S(1)}, f32[64,256]{1,0:T(8,128)S(1)}, u32[]{:S(2)}, u32[]{:S(2)}) collective-permute-start(f32[64,256]{1,0:T(8,128)S(1)} %get-tuple-element.104), channel_id=1, source_target_pairs={{0,2},{1,3},{2,0},{3,1},{4,6},{5,7},{6,4},{7,5},{8,10},{9,11},{10,... | collective-permute-start | bytes 196616 | tf_op jit(solution)/shard_map/ppermute | solution.py:42
  53.3 0.6 collective-permute-start.32
  53.9 3.8 %collective-permute-start.33 = (f32[128,128]{1,0:T(8,128)S(1)}, f32[128,128]{1,0:T(8,128)S(1)}, u32[]{:S(2)}, u32[]{:S(2)}) collective-permute-start(f32[128,128]{1,0:T(8,128)S(1)} %get-tuple-element.100.refs_0_), channel_id=1, source_target_pairs={{0,2},{1,3},{2,0},{3,1},{4,6},{5,7},{6,4},{7,5},{8,10},{9,11},{10,... | collective-permute-start | bytes 196616 | tf_op jit(solution)/shard_map/ppermute | solution.py:42
  57.7 0.2 collective-permute-start.34
  57.9 2.3 %collective-permute-done.37 = f32[64,256]{1,0:T(8,128)S(1)} collective-permute-done((f32[64,256]{1,0:T(8,128)S(1)}, f32[64,256]{1,0:T(8,128)S(1)}, u32[]{:S(2)}, u32[]{:S(2)}) %collective-permute-start.37) | collective-permute-done | bytes 65568 | tf_op jit(solution)/shard_map/ppermute | solution.py:42
  60.2 2.2 %collective-permute-start.38 = (f32[64,256]{1,0:T(8,128)S(1)}, f32[64,256]{1,0:T(8,128)S(1)}, u32[]{:S(2)}, u32[]{:S(2)}) collective-permute-start(f32[64,256]{1,0:T(8,128)S(1)} %add_add_fusion.1.refs_0_), channel_id=1, source_target_pairs={{0,1},{1,0},{2,3},{3,2},{4,5},{5,4},{6,7},{7,6},{8,9},{9,8},{10,11... | collective-permute-start | bytes 196616 | tf_op jit(solution)/shard_map/ppermute | solution.py:42
  62.4 3.9 %collective-permute-start.39 = (f32[64,256]{1,0:T(8,128)S(1)}, f32[64,256]{1,0:T(8,128)S(1)}, u32[]{:S(2)}, u32[]{:S(2)}) collective-permute-start(f32[64,256]{1,0:T(8,128)S(1)} %add_add_fusion.1.refs_0_), channel_id=1, source_target_pairs={{0,2},{1,3},{2,0},{3,1},{4,6},{5,7},{6,4},{7,5},{8,10},{9,11},{10,... | collective-permute-start | bytes 196616 | tf_op jit(solution)/shard_map/ppermute | solution.py:42
  66.3 1.4 %collective-permute-start.40 = (f32[64,256]{1,0:T(8,128)S(1)}, f32[64,256]{1,0:T(8,128)S(1)}, u32[]{:S(2)}, u32[]{:S(2)}) collective-permute-start(f32[64,256]{1,0:T(8,128)S(1)} %add_add_fusion.1.refs_0_), channel_id=1, source_target_pairs={{0,3},{1,2},{2,1},{3,0},{4,7},{5,6},{6,5},{7,4},{8,11},{9,10},{10,... | collective-permute-start | bytes 196616 | tf_op jit(solution)/shard_map/ppermute | solution.py:42
  67.7 3.4 %whiten.2.whitener = f32[256,256]{1,0:T(8,128)S(1)} custom-call(f32[128,128]{1,0:T(8,128)S(1)} %get-tuple-element.100.refs_0_, f32[128,128]{1,0:T(8,128)S(1)} %collective-permute-done.32.refs_1_, f32[128,128]{1,0:T(8,128)S(1)} %collective-permute-done.33.refs_2_, f32[128,128]{1,0:T(8,128)S(1)} %collective-permute-done.34.refs_3_), custom_call_target="tpu_custom_call" | custom-call | tf_op jit(solution)/shard_map/whiten/pallas_call | solution.py:362
  71.2 1.3 %collective-permute-done.40.refs_3_ = f32[64,256]{1,0:T(8,128)S(1)} collective-permute-done((f32[64,256]{1,0:T(8,128)S(1)}, f32[64,256]{1,0:T(8,128)S(1)}, u32[]{:S(2)}, u32[]{:S(2)}) %collective-permute-start.40) | collective-permute-done | bytes 65568 | tf_op jit(solution)/shard_map/ppermute | solution.py:42
  72.5 4.7 %update.1 = (f32[256,128]{1,0:T(8,128)}, f32[256,128]{1,0:T(8,128)}, f32[256,2048]{1,0:T(8,128)}, f32[256,2048]{1,0:T(8,128)}, f32[1,256]{1,0:T(1,128)S(1)}) custom-call(s32[1,256]{1,0:T(1,128)S(1)} %bitcast.63, f32[256,256]{1,0:T(8,128)S(1)} %whiten.2.whitener, f32[256,2048]{1,0:T(8,128)S(1)} %get-tuple-element.101.p, f32[256,2048]{1,0:T(8,128)S(1)} %copy-done.3, ...), custom_call_target="tpu_custom_call" | custom-call | tf_op jit(solution)/shard_map/update/pallas_call | solution.py:412
  77.2 0.7 collective-permute-start.41
  77.9 1.2 %collective-permute-start.42 = (f32[1,256]{1,0:T(1,128)S(1)}, f32[1,256]{1,0:T(1,128)S(1)}, u32[]{:S(2)}, u32[]{:S(2)}) collective-permute-start(f32[1,256]{1,0:T(1,128)S(1)} %get-tuple-element.110), channel_id=1, source_target_pairs={{0,2},{1,3},{2,0},{3,1},{4,6},{5,7},{6,4},{7,5},{8,10},{9,11},{10,... | collective-permute-start | bytes 3080 | tf_op jit(solution)/shard_map/ppermute | solution.py:42
  79.1 2.4 %collective-permute-start.43 = (f32[1,256]{1,0:T(1,128)S(1)}, f32[1,256]{1,0:T(1,128)S(1)}, u32[]{:S(2)}, u32[]{:S(2)}) collective-permute-start(f32[1,256]{1,0:T(1,128)S(1)} %get-tuple-element.110), channel_id=1, source_target_pairs={{0,3},{1,2},{2,1},{3,0},{4,7},{5,6},{6,5},{7,4},{8,11},{9,10},{10,... | collective-permute-start | bytes 3080 | tf_op jit(solution)/shard_map/ppermute | solution.py:42
  81.6 0.8 collective-permute-done.42
  82.4 2.1 %collective-permute-done.43 = f32[1,256]{1,0:T(1,128)S(1)} collective-permute-done((f32[1,256]{1,0:T(1,128)S(1)}, f32[1,256]{1,0:T(1,128)S(1)}, u32[]{:S(2)}, u32[]{:S(2)}) %collective-permute-start.43) | collective-permute-done | bytes 1056 | tf_op jit(solution)/shard_map/ppermute | solution.py:42
  84.5 0.6 convert_divide_fusion.1
  85.1 0.9 %while.18 = (s32[]{:T(128)}, f32[256,128]{1,0:T(8,128)}, f32[256,128]{1,0:T(8,128)}, f32[256,2048]{1,0:T(8,128)}, f32[256,2048]{1,0:T(8,128)}, /*index=5*/f32[25...) while((s32[]{:T(128)}, f32[256,128]{1,0:T(8,128)}, ...), condition=%wide.region_2.3_spmd, body=%wide.region_0.2_spmd.sunk | while | flops 22968406016 | bytes 205383488 | solution.py:497
  (39 shorter events, 0.2 us)
Async XLA Ops:
  0.6 8.4 %copy-start = (f32[256,2048]{1,0:T(8,128)S(1)}, f32[256,2048]{1,0:T(8,128)}, u32[]{:S(2)}) copy-start(f32[256,2048]{1,0:T(8,128)} %b_re.3) | copy-start | bytes 6291460
  0.6 8.4 %copy-start.1 = (f32[256,2048]{1,0:T(8,128)S(1)}, f32[256,2048]{1,0:T(8,128)}, u32[]{:S(2)}) copy-start(f32[256,2048]{1,0:T(8,128)} %b_im.3) | copy-start | bytes 6291460
  4.2 11.5 %copy-start.7 = (s32[128]{0:T(128)S(1)}, s32[128]{0:T(128)}, u32[]{:S(2)}) copy-start(s32[128]{0:T(128)} %piv.1) | copy-start | bytes 1540
  4.2 33.6 %copy-start.3 = (f32[256,2048]{1,0:T(8,128)S(1)}, f32[256,2048]{1,0:T(8,128)}, u32[]{:S(2)}) copy-start(f32[256,2048]{1,0:T(8,128)} %re.5) | copy-start | bytes 6291460
  4.2 33.6 %copy-start.4 = (f32[256,2048]{1,0:T(8,128)S(1)}, f32[256,2048]{1,0:T(8,128)}, u32[]{:S(2)}) copy-start(f32[256,2048]{1,0:T(8,128)} %im.5) | copy-start | bytes 6291460
  4.2 33.6 %copy-start.6 = (s32[256]{0:T(256)S(1)}, s32[256]{0:T(256)}, u32[]{:S(2)}) copy-start(s32[256]{0:T(256)} %lens.1) | copy-start | bytes 3076
  4.2 4.8 %collective-permute-start.15 = (f32[56,2048]{1,0:T(8,128)S(1)}, f32[56,2048]{1,0:T(8,128)S(1)}, u32[]{:S(2)}, u32[]{:S(2)}) collective-permute-start(f32[56,2048]{1,0:T(8,128)S(1)} %pick.1.refs_0_), channel_id=1, source_target_pairs={{0,4},{4,0},{8,12},{12,8},{16,20},{20,16},{24,28},{28,24},{1,5},{5... | collective-permute-start | bytes 1376264 | tf_op jit(solution)/shard_map/ppermute | solution.py:42
  5.3 13.7 %collective-permute-start.13 = (f32[56,2048]{1,0:T(8,128)S(1)}, f32[56,2048]{1,0:T(8,128)S(1)}, u32[]{:S(2)}, u32[]{:S(2)}) collective-permute-start(f32[56,2048]{1,0:T(8,128)S(1)} %pick.1.refs_0_), channel_id=1, source_target_pairs={{0,8},{4,12},{8,0},{12,4},{16,24},{20,28},{24,16},{28,20},{1,9},{5... | collective-permute-start | bytes 1376264 | tf_op jit(solution)/shard_map/ppermute | solution.py:42
  7.9 12.6 %collective-permute-start.14 = (f32[56,2048]{1,0:T(8,128)S(1)}, f32[56,2048]{1,0:T(8,128)S(1)}, u32[]{:S(2)}, u32[]{:S(2)}) collective-permute-start(f32[56,2048]{1,0:T(8,128)S(1)} %pick.1.refs_0_), channel_id=1, source_target_pairs={{0,16},{4,20},{8,24},{12,28},{16,0},{20,4},{24,8},{28,12},{1,17},{... | collective-permute-start | bytes 1376264 | tf_op jit(solution)/shard_map/ppermute | solution.py:42
  11.3 11.1 %collective-permute-start.22 = (f32[64,512]{1,0:T(8,128)S(1)}, f32[64,512]{1,0:T(8,128)S(1)}, u32[]{:S(2)}, u32[]{:S(2)}) collective-permute-start(f32[64,512]{1,0:T(8,128)S(1)} %cross.1), channel_id=1, source_target_pairs={{0,1},{1,0},{2,3},{3,2},{4,5},{5,4},{6,7},{7,6},{8,9},{9,8},{10,11... | collective-permute-start | bytes 393224 | tf_op jit(solution)/shard_map/ppermute | solution.py:42
  12.9 12.7 %collective-permute-start.23 = (f32[64,512]{1,0:T(8,128)S(1)}, f32[64,512]{1,0:T(8,128)S(1)}, u32[]{:S(2)}, u32[]{:S(2)}) collective-permute-start(f32[64,512]{1,0:T(8,128)S(1)} %cross.1), channel_id=1, source_target_pairs={{0,2},{1,3},{2,0},{3,1},{4,6},{5,7},{6,4},{7,5},{8,10},{9,11},{10,... | collective-permute-start | bytes 393224 | tf_op jit(solution)/shard_map/ppermute | solution.py:42
  15.5 10.1 %collective-permute-start.24 = (f32[64,512]{1,0:T(8,128)S(1)}, f32[64,512]{1,0:T(8,128)S(1)}, u32[]{:S(2)}, u32[]{:S(2)}) collective-permute-start(f32[64,512]{1,0:T(8,128)S(1)} %cross.1), channel_id=1, source_target_pairs={{0,3},{1,2},{2,1},{3,0},{4,7},{5,6},{6,5},{7,4},{8,11},{9,10},{10,... | collective-permute-start | bytes 393224 | tf_op jit(solution)/shard_map/ppermute | solution.py:42
  20.5 7.4 %collective-permute-start.16 = (f32[56,1024]{1,0:T(8,128)S(1)}, f32[56,1024]{1,0:T(8,128)S(1)}, u32[]{:S(2)}, u32[]{:S(2)}) collective-permute-start(f32[56,1024]{1,0:T(8,128)S(1)} %slice.74), channel_id=1, source_target_pairs={{0,16},{4,20},{8,24},{12,28},{16,0},{20,4},{24,8},{28,12},{1,17},{... | collective-permute-start | bytes 688136 | tf_op jit(solution)/shard_map/ppermute | solution.py:42
  21.5 7.7 %collective-permute-start.17 = (f32[56,1024]{1,0:T(8,128)S(1)}, f32[56,1024]{1,0:T(8,128)S(1)}, u32[]{:S(2)}, u32[]{:S(2)}) collective-permute-start(f32[56,1024]{1,0:T(8,128)S(1)} %slice.75), channel_id=1, source_target_pairs={{0,8},{4,12},{8,0},{12,4},{16,24},{20,28},{24,16},{28,20},{1,9},{5... | collective-permute-start | bytes 688136 | tf_op jit(solution)/shard_map/ppermute | solution.py:42
  25.7 5.0 %collective-permute-start.26 = (f32[64,512]{1,0:T(8,128)S(1)}, f32[64,512]{1,0:T(8,128)S(1)}, u32[]{:S(2)}, u32[]{:S(2)}) collective-permute-start(f32[64,512]{1,0:T(8,128)S(1)} %add_add_fusion.refs_10_), channel_id=1, source_target_pairs={{0,8},{4,12},{8,0},{12,4},{16,24},{20,28},{24,16},{28,20},{1,9},{5... | collective-permute-start | bytes 393224 | tf_op jit(solution)/shard_map/ppermute | solution.py:42
  26.5 5.0 %collective-permute-start.28 = (f32[64,512]{1,0:T(8,128)S(1)}, f32[64,512]{1,0:T(8,128)S(1)}, u32[]{:S(2)}, u32[]{:S(2)}) collective-permute-start(f32[64,512]{1,0:T(8,128)S(1)} %add_add_fusion.refs_10_), channel_id=1, source_target_pairs={{0,16},{4,20},{8,24},{12,28},{16,0},{20,4},{24,8},{28,12},{1,17},{... | collective-permute-start | bytes 393224 | tf_op jit(solution)/shard_map/ppermute | solution.py:42
  27.4 10.4 %collective-permute-start.18 = (f32[56,2048]{1,0:T(8,128)S(1)}, f32[56,2048]{1,0:T(8,128)S(1)}, u32[]{:S(2)}, u32[]{:S(2)}) collective-permute-start(f32[56,2048]{1,0:T(8,128)S(1)} %collective-permute-done.13.refs_1_), channel_id=1, source_target_pairs={{0,4},{4,0},{8,12},{12,8},{16,20},{20,16},{24,28},{28,24},{1,5},{5... | collective-permute-start | bytes 1376264 | tf_op jit(solution)/shard_map/ppermute | solution.py:42
  27.9 9.9 %collective-permute-start.19 = (f32[56,2048]{1,0:T(8,128)S(1)}, f32[56,2048]{1,0:T(8,128)S(1)}, u32[]{:S(2)}, u32[]{:S(2)}) collective-permute-start(f32[56,2048]{1,0:T(8,128)S(1)} %collective-permute-done.14.refs_2_), channel_id=1, source_target_pairs={{0,4},{4,0},{8,12},{12,8},{16,20},{20,16},{24,28},{28,24},{1,5},{5... | collective-permute-start | bytes 1376264 | tf_op jit(solution)/shard_map/ppermute | solution.py:42
  29.2 5.9 %collective-permute-start.30 = (f32[64,512]{1,0:T(8,128)S(1)}, f32[64,512]{1,0:T(8,128)S(1)}, u32[]{:S(2)}, u32[]{:S(2)}) collective-permute-start(f32[64,512]{1,0:T(8,128)S(1)} %add_add_fusion.refs_10_), channel_id=1, source_target_pairs={{0,24},{4,28},{8,16},{12,20},{16,8},{20,12},{24,0},{28,4},{1,25},{... | collective-permute-start | bytes 393224 | tf_op jit(solution)/shard_map/ppermute | solution.py:42
  30.7 4.4 %collective-permute-start.25 = (f32[64,512]{1,0:T(8,128)S(1)}, f32[64,512]{1,0:T(8,128)S(1)}, u32[]{:S(2)}, u32[]{:S(2)}) collective-permute-start(f32[64,512]{1,0:T(8,128)S(1)} %add_add_fusion.refs_10_), channel_id=1, source_target_pairs={{0,4},{4,0},{8,12},{12,8},{16,20},{20,16},{24,28},{28,24},{1,5},{5... | collective-permute-start | bytes 393224 | tf_op jit(solution)/shard_map/ppermute | solution.py:42
  31.5 4.1 %collective-permute-start.27 = (f32[64,512]{1,0:T(8,128)S(1)}, f32[64,512]{1,0:T(8,128)S(1)}, u32[]{:S(2)}, u32[]{:S(2)}) collective-permute-start(f32[64,512]{1,0:T(8,128)S(1)} %collective-permute-done.26.refs_12_), channel_id=1, source_target_pairs={{0,4},{4,0},{8,12},{12,8},{16,20},{20,16},{24,28},{28,24},{1,5},{5... | collective-permute-start | bytes 393224 | tf_op jit(solution)/shard_map/ppermute | solution.py:42
  35.1 1.3 %collective-permute-start.29 = (f32[64,512]{1,0:T(8,128)S(1)}, f32[64,512]{1,0:T(8,128)S(1)}, u32[]{:S(2)}, u32[]{:S(2)}) collective-permute-start(f32[64,512]{1,0:T(8,128)S(1)} %collective-permute-done.28.refs_14_), channel_id=1, source_target_pairs={{0,4},{4,0},{8,12},{12,8},{16,20},{20,16},{24,28},{28,24},{1,5},{5... | collective-permute-start | bytes 393224 | tf_op jit(solution)/shard_map/ppermute | solution.py:42
  35.1 2.7 %collective-permute-start.20 = (f32[56,1024]{1,0:T(8,128)S(1)}, f32[56,1024]{1,0:T(8,128)S(1)}, u32[]{:S(2)}, u32[]{:S(2)}) collective-permute-start(f32[56,1024]{1,0:T(8,128)S(1)} %collective-permute-done.16.refs_3_), channel_id=1, source_target_pairs={{0,4},{4,0},{8,12},{12,8},{16,20},{20,16},{24,28},{28,24},{1,5},{5... | collective-permute-start | bytes 688136 | tf_op jit(solution)/shard_map/ppermute | solution.py:42
  35.6 2.2 %collective-permute-start.21 = (f32[56,1024]{1,0:T(8,128)S(1)}, f32[56,1024]{1,0:T(8,128)S(1)}, u32[]{:S(2)}, u32[]{:S(2)}) collective-permute-start(f32[56,1024]{1,0:T(8,128)S(1)} %collective-permute-done.17.refs_4_), channel_id=1, source_target_pairs={{0,4},{4,0},{8,12},{12,8},{16,20},{20,16},{24,28},{28,24},{1,5},{5... | collective-permute-start | bytes 688136 | tf_op jit(solution)/shard_map/ppermute | solution.py:42
  36.4 1.3 %collective-permute-start.31 = (f32[64,512]{1,0:T(8,128)S(1)}, f32[64,512]{1,0:T(8,128)S(1)}, u32[]{:S(2)}, u32[]{:S(2)}) collective-permute-start(f32[64,512]{1,0:T(8,128)S(1)} %collective-permute-done.30.refs_16_), channel_id=1, source_target_pairs={{0,4},{4,0},{8,12},{12,8},{16,20},{20,16},{24,28},{28,24},{1,5},{5... | collective-permute-start | bytes 393224 | tf_op jit(solution)/shard_map/ppermute | solution.py:42
  48.5 9.2 %collective-permute-start.35 = (f32[64,256]{1,0:T(8,128)S(1)}, f32[64,256]{1,0:T(8,128)S(1)}, u32[]{:S(2)}, u32[]{:S(2)}) collective-permute-start(f32[64,256]{1,0:T(8,128)S(1)} %get-tuple-element.103), channel_id=1, source_target_pairs={{0,1},{1,0},{2,3},{3,2},{4,5},{5,4},{6,7},{7,6},{8,9},{9,8},{10,11... | collective-permute-start | bytes 196616 | tf_op jit(solution)/shard_map/ppermute | solution.py:42
  50.3 7.6 %collective-permute-start.36 = (f32[64,256]{1,0:T(8,128)S(1)}, f32[64,256]{1,0:T(8,128)S(1)}, u32[]{:S(2)}, u32[]{:S(2)}) collective-permute-start(f32[64,256]{1,0:T(8,128)S(1)} %get-tuple-element.104), channel_id=1, source_target_pairs={{0,2},{1,3},{2,0},{3,1},{4,6},{5,7},{6,4},{7,5},{8,10},{9,11},{10,... | collective-permute-start | bytes 196616 | tf_op jit(solution)/shard_map/ppermute | solution.py:42
  53.3 6.9 %collective-permute-start.37 = (f32[64,256]{1,0:T(8,128)S(1)}, f32[64,256]{1,0:T(8,128)S(1)}, u32[]{:S(2)}, u32[]{:S(2)}) collective-permute-start(f32[64,256]{1,0:T(8,128)S(1)} %get-tuple-element.105), channel_id=1, source_target_pairs={{0,3},{1,2},{2,1},{3,0},{4,7},{5,6},{6,5},{7,4},{8,11},{9,10},{10,... | collective-permute-start | bytes 196616 | tf_op jit(solution)/shard_map/ppermute | solution.py:42
  53.3 13.0 %collective-permute-start.32 = (f32[128,128]{1,0:T(8,128)S(1)}, f32[128,128]{1,0:T(8,128)S(1)}, u32[]{:S(2)}, u32[]{:S(2)}) collective-permute-start(f32[128,128]{1,0:T(8,128)S(1)} %get-tuple-element.100.refs_0_), channel_id=1, source_target_pairs={{0,1},{1,0},{2,3},{3,2},{4,5},{5,4},{6,7},{7,6},{8,9},{9,8},{10,11... | collective-permute-start | bytes 196616 | tf_op jit(solution)/shard_map/ppermute | solution.py:42
  53.9 13.9 %collective-permute-start.33 = (f32[128,128]{1,0:T(8,128)S(1)}, f32[128,128]{1,0:T(8,128)S(1)}, u32[]{:S(2)}, u32[]{:S(2)}) collective-permute-start(f32[128,128]{1,0:T(8,128)S(1)} %get-tuple-element.100.refs_0_), channel_id=1, source_target_pairs={{0,2},{1,3},{2,0},{3,1},{4,6},{5,7},{6,4},{7,5},{8,10},{9,11},{10,... | collective-permute-start | bytes 196616 | tf_op jit(solution)/shard_map/ppermute | solution.py:42
  57.7 10.0 %collective-permute-start.34 = (f32[128,128]{1,0:T(8,128)S(1)}, f32[128,128]{1,0:T(8,128)S(1)}, u32[]{:S(2)}, u32[]{:S(2)}) collective-permute-start(f32[128,128]{1,0:T(8,128)S(1)} %get-tuple-element.100.refs_0_), channel_id=1, source_target_pairs={{0,3},{1,2},{2,1},{3,0},{4,7},{5,6},{6,5},{7,4},{8,11},{9,10},{10,... | collective-permute-start | bytes 196616 | tf_op jit(solution)/shard_map/ppermute | solution.py:42
  60.2 11.0 %collective-permute-start.38 = (f32[64,256]{1,0:T(8,128)S(1)}, f32[64,256]{1,0:T(8,128)S(1)}, u32[]{:S(2)}, u32[]{:S(2)}) collective-permute-start(f32[64,256]{1,0:T(8,128)S(1)} %add_add_fusion.1.refs_0_), channel_id=1, source_target_pairs={{0,1},{1,0},{2,3},{3,2},{4,5},{5,4},{6,7},{7,6},{8,9},{9,8},{10,11... | collective-permute-start | bytes 196616 | tf_op jit(solution)/shard_map/ppermute | solution.py:42
  62.4 8.8 %collective-permute-start.39 = (f32[64,256]{1,0:T(8,128)S(1)}, f32[64,256]{1,0:T(8,128)S(1)}, u32[]{:S(2)}, u32[]{:S(2)}) collective-permute-start(f32[64,256]{1,0:T(8,128)S(1)} %add_add_fusion.1.refs_0_), channel_id=1, source_target_pairs={{0,2},{1,3},{2,0},{3,1},{4,6},{5,7},{6,4},{7,5},{8,10},{9,11},{10,... | collective-permute-start | bytes 196616 | tf_op jit(solution)/shard_map/ppermute | solution.py:42
  66.3 6.2 %collective-permute-start.40 = (f32[64,256]{1,0:T(8,128)S(1)}, f32[64,256]{1,0:T(8,128)S(1)}, u32[]{:S(2)}, u32[]{:S(2)}) collective-permute-start(f32[64,256]{1,0:T(8,128)S(1)} %add_add_fusion.1.refs_0_), channel_id=1, source_target_pairs={{0,3},{1,2},{2,1},{3,0},{4,7},{5,6},{6,5},{7,4},{8,11},{9,10},{10,... | collective-permute-start | bytes 196616 | tf_op jit(solution)/shard_map/ppermute | solution.py:42
  77.2 4.4 %collective-permute-start.41 = (f32[1,256]{1,0:T(1,128)S(1)}, f32[1,256]{1,0:T(1,128)S(1)}, u32[]{:S(2)}, u32[]{:S(2)}) collective-permute-start(f32[1,256]{1,0:T(1,128)S(1)} %get-tuple-element.110), channel_id=1, source_target_pairs={{0,1},{1,0},{2,3},{3,2},{4,5},{5,4},{6,7},{7,6},{8,9},{9,8},{10,11... | collective-permute-start | bytes 3080 | tf_op jit(solution)/shard_map/ppermute | solution.py:42
  77.9 4.5 %collective-permute-start.42 = (f32[1,256]{1,0:T(1,128)S(1)}, f32[1,256]{1,0:T(1,128)S(1)}, u32[]{:S(2)}, u32[]{:S(2)}) collective-permute-start(f32[1,256]{1,0:T(1,128)S(1)} %get-tuple-element.110), channel_id=1, source_target_pairs={{0,2},{1,3},{2,0},{3,1},{4,6},{5,7},{6,4},{7,5},{8,10},{9,11},{10,... | collective-permute-start | bytes 3080 | tf_op jit(solution)/shard_map/ppermute | solution.py:42
  79.1 5.4 %collective-permute-start.43 = (f32[1,256]{1,0:T(1,128)S(1)}, f32[1,256]{1,0:T(1,128)S(1)}, u32[]{:S(2)}, u32[]{:S(2)}) collective-permute-start(f32[1,256]{1,0:T(1,128)S(1)} %get-tuple-element.110), channel_id=1, source_target_pairs={{0,3},{1,2},{2,1},{3,0},{4,7},{5,6},{6,5},{7,4},{8,11},{9,10},{10,... | collective-permute-start | bytes 3080 | tf_op jit(solution)/shard_map/ppermute | solution.py:42

commit v4 on v3

--- a/solution.py
+++ b/solution.py
@@ -453,6 +453,24 @@
     return both
 
 
+def mean_kernel(lens, *refs):
+    total = refs[0][...]
+    for ref in refs[1:-1]:
+        total = total + ref[...]
+    refs[-1][...] = total / (BIN_BLOCK * lens[...]).astype(F32)
+
+
+def mean(parts, lens):
+    return pl.pallas_call(
+        mean_kernel,
+        out_shape=jax.ShapeDtypeStruct(lens.shape, F32),
+        in_specs=[VMEM] * (1 + len(parts)),
+        out_specs=VMEM,
+        compiler_params=params(4),
+        name="mean",
+    )(lens, *parts)
+
+
 def sum_pieces(pieces, nf):
     return sum([swap(pieces[k], "freq", nf, k) for k in range(1, nf)], pieces[0])
 
@@ -487,7 +505,7 @@
     every = [piece] + [swap(piece, "freq", nf, k) for k in range(1, nf)]
     whitener = whiten(grams)
     coef_re, coef_im, new_re, new_im, squares = update(nf, lens, whitener, p, res_re, res_im, every)
-    errors = sum_over_freq(squares, nf).reshape(waves) / (BIN_BLOCK * lengths).astype(F32)
+    errors = mean([squares] + [swap(squares, "freq", nf, k) for k in range(1, nf)], lens).reshape(waves)
     made = (coef_re, coef_im, new_re, new_im, errors)
 
     def again(carry):

time: 86.4 us -> 86.4 us (level)
  Pallas kernels: 25.3 us -> 26.3 us
  transfers between devices with their start and end apart: 31 -> 31, of which waited for: 14 -> 12; matrix products, arithmetic and copies ran while one was open for 0% -> 0% of each run, Pallas kernels for 7% -> 7%
where the time goes in v4:
time: 86.4 us
  starting transfers between devices  35.7 us (41%)
  Pallas kernels  26.3 us (30%)
  waiting for transfers between devices  22.4 us (26%)
  between operations  1.02 us (1%)
  loops' own time  0.89 us (1%)
    ppermute x31, starting transfers between devices, swap(): return lax.ppermute(array, axis, [(i, i ^ distance) for i in range(size)])  35.7 us
    ppermute x31, waiting for transfers between devices, swap(): return lax.ppermute(array, axis, [(i, i ^ distance) for i in range(size)])  22.4 us
    pallas_call x1, Pallas kernels, project(): pl.pallas_call(functools.partial(project_kernel, cap, nw, nf, places), ou...  10.7 us
    pallas_call x1, Pallas kernels, update(): pl.pallas_call(functools.partial(update_kernel, nf), out_shape=[jax.Shape...  4.69 us
    pallas_call x1, Pallas kernels, pick(): pl.pallas_call(functools.partial(pick_kernel, cap), out_shape=jax.ShapeDt...  3.91 us
    pallas_call x1, Pallas kernels, whiten(): pl.pallas_call(functools.partial(whiten_kernel, len(grams)), out_shape=ja...  3.42 us
    pallas_call x1, Pallas kernels, cross(): pl.pallas_call(functools.partial(cross_kernel, cap), out_shape=jax.ShapeD...  2.19 us
  transfers between devices with their start and end apart: 31, of which 12 were waited for; matrix products, arithmetic and copies ran while one was open for 0% of the time, Pallas kernels for 7%

profile of v4, /device:TPU:0, one launch (start us, length us, event | category | flops | bytes accessed | tf_op | source)
XLA Modules:
  0.0 86.4 jit_solution(8792548478075917382)
XLA Ops:
  0.7 3.9 %pick.1.refs_0_ = f32[56,2048]{1,0:T(8,128)S(1)} custom-call(s32[128]{0:T(128)} %piv.1, s32[256]{0:T(256)} %lens.1, s32[1]{0:T(128)} %constant.33.clone.1.skip_ref, f32[256,2048]{1,0:T(8,128)} %re.5, f32[256,2048]{1,0:T(8,128)} %im.5), custom_call_target="tpu_custom_call" | custom-call | tf_op jit(solution)/shard_map/pick/pallas_call | solution.py:120
  4.6 0.3 collective-permute-start.15
  5.0 2.6 %collective-permute-start.13 = (f32[56,2048]{1,0:T(8,128)S(1)}, f32[56,2048]{1,0:T(8,128)S(1)}, u32[]{:S(2)}, u32[]{:S(2)}) collective-permute-start(f32[56,2048]{1,0:T(8,128)S(1)} %pick.1.refs_0_), channel_id=1, source_target_pairs={{0,8},{4,12},{8,0},{12,4},{16,24},{20,28},{24,16},{28,20},{1,9},{5... | collective-permute-start | bytes 1376264 | tf_op jit(solution)/shard_map/ppermute | solution.py:42
  7.5 1.8 %collective-permute-start.14 = (f32[56,2048]{1,0:T(8,128)S(1)}, f32[56,2048]{1,0:T(8,128)S(1)}, u32[]{:S(2)}, u32[]{:S(2)}) collective-permute-start(f32[56,2048]{1,0:T(8,128)S(1)} %pick.1.refs_0_), channel_id=1, source_target_pairs={{0,16},{4,20},{8,24},{12,28},{16,0},{20,4},{24,8},{28,12},{1,17},{... | collective-permute-start | bytes 1376264 | tf_op jit(solution)/shard_map/ppermute | solution.py:42
  9.3 2.2 %cross.1 = f32[64,512]{1,0:T(8,128)S(1)} custom-call(f32[56,2048]{1,0:T(8,128)S(1)} %collective-permute-done.15.rows.refs_5_, f32[256,2048]{1,0:T(8,128)S(1)} %copy-done, f32[256,2048]{1,0:T(8,128)S(1)} %copy-done.1), custom_call_target="tpu_custom_call" | custom-call | flops 1000 | bytes 1000 | tf_op jit(solution)/shard_map/cross/pallas_call | solution.py:159
  11.5 1.6 %collective-permute-start.22 = (f32[64,512]{1,0:T(8,128)S(1)}, f32[64,512]{1,0:T(8,128)S(1)}, u32[]{:S(2)}, u32[]{:S(2)}) collective-permute-start(f32[64,512]{1,0:T(8,128)S(1)} %cross.1), channel_id=1, source_target_pairs={{0,1},{1,0},{2,3},{3,2},{4,5},{5,4},{6,7},{7,6},{8,9},{9,8},{10,11... | collective-permute-start | bytes 393224 | tf_op jit(solution)/shard_map/ppermute | solution.py:42
  13.2 2.6 %collective-permute-start.23 = (f32[64,512]{1,0:T(8,128)S(1)}, f32[64,512]{1,0:T(8,128)S(1)}, u32[]{:S(2)}, u32[]{:S(2)}) collective-permute-start(f32[64,512]{1,0:T(8,128)S(1)} %cross.1), channel_id=1, source_target_pairs={{0,2},{1,3},{2,0},{3,1},{4,6},{5,7},{6,4},{7,5},{8,10},{9,11},{10,... | collective-permute-start | bytes 393224 | tf_op jit(solution)/shard_map/ppermute | solution.py:42
  15.7 0.2 collective-permute-start.24
  16.0 0.8 orders.1
  16.8 1.8 %collective-permute-done.13.refs_1_ = f32[56,2048]{1,0:T(8,128)S(1)} collective-permute-done((f32[56,2048]{1,0:T(8,128)S(1)}, f32[56,2048]{1,0:T(8,128)S(1)}, u32[]{:S(2)}, u32[]{:S(2)}) %collective-permute-start.13) | collective-permute-done | bytes 458784 | tf_op jit(solution)/shard_map/ppermute | solution.py:42
  18.6 1.5 %collective-permute-done.14.refs_2_ = f32[56,2048]{1,0:T(8,128)S(1)} collective-permute-done((f32[56,2048]{1,0:T(8,128)S(1)}, f32[56,2048]{1,0:T(8,128)S(1)}, u32[]{:S(2)}, u32[]{:S(2)}) %collective-permute-start.14) | collective-permute-done | bytes 458784 | tf_op jit(solution)/shard_map/ppermute | solution.py:42
  20.2 1.8 %collective-permute-start.16 = (f32[56,1024]{1,0:T(8,128)S(1)}, f32[56,1024]{1,0:T(8,128)S(1)}, u32[]{:S(2)}, u32[]{:S(2)}) collective-permute-start(f32[56,1024]{1,0:T(8,128)S(1)} %slice.74), channel_id=1, source_target_pairs={{0,16},{4,20},{8,24},{12,28},{16,0},{20,4},{24,8},{28,12},{1,17},{... | collective-permute-start | bytes 688136 | tf_op jit(solution)/shard_map/ppermute | solution.py:42
  22.0 0.4 collective-permute-start.17
  22.4 3.7 %collective-permute-done.23 = f32[64,512]{1,0:T(8,128)S(1)} collective-permute-done((f32[64,512]{1,0:T(8,128)S(1)}, f32[64,512]{1,0:T(8,128)S(1)}, u32[]{:S(2)}, u32[]{:S(2)}) %collective-permute-start.23) | collective-permute-done | bytes 131104 | tf_op jit(solution)/shard_map/ppermute | solution.py:42
  26.1 0.4 collective-permute-start.26
  26.5 1.4 %collective-permute-start.28 = (f32[64,512]{1,0:T(8,128)S(1)}, f32[64,512]{1,0:T(8,128)S(1)}, u32[]{:S(2)}, u32[]{:S(2)}) collective-permute-start(f32[64,512]{1,0:T(8,128)S(1)} %add_add_fusion.refs_10_), channel_id=1, source_target_pairs={{0,16},{4,20},{8,24},{12,28},{16,0},{20,4},{24,8},{28,12},{1,17},{... | collective-permute-start | bytes 393224 | tf_op jit(solution)/shard_map/ppermute | solution.py:42
  27.9 0.5 collective-permute-start.19
  28.4 1.6 %collective-permute-done.17.refs_4_ = f32[56,1024]{1,0:T(8,128)S(1)} collective-permute-done((f32[56,1024]{1,0:T(8,128)S(1)}, f32[56,1024]{1,0:T(8,128)S(1)}, u32[]{:S(2)}, u32[]{:S(2)}) %collective-permute-start.17) | collective-permute-done | bytes 229408 | tf_op jit(solution)/shard_map/ppermute | solution.py:42
  30.0 0.2 collective-permute-start.30
  30.2 1.2 %collective-permute-done.26.refs_12_ = f32[64,512]{1,0:T(8,128)S(1)} collective-permute-done((f32[64,512]{1,0:T(8,128)S(1)}, f32[64,512]{1,0:T(8,128)S(1)}, u32[]{:S(2)}, u32[]{:S(2)}) %collective-permute-start.26) | collective-permute-done | bytes 131104 | tf_op jit(solution)/shard_map/ppermute | solution.py:42
  31.5 0.5 collective-permute-start.27
  31.9 3.9 %collective-permute-done.30.refs_16_ = f32[64,512]{1,0:T(8,128)S(1)} collective-permute-done((f32[64,512]{1,0:T(8,128)S(1)}, f32[64,512]{1,0:T(8,128)S(1)}, u32[]{:S(2)}, u32[]{:S(2)}) %collective-permute-start.30) | collective-permute-done | bytes 131104 | tf_op jit(solution)/shard_map/ppermute | solution.py:42
  35.9 0.5 collective-permute-start.20
  36.4 0.1 collective-permute-start.21
  36.5 0.8 collective-permute-done.29.refs_15_
  37.2 0.1 collective-permute-start.31
  37.4 1.2 %collective-permute-done.31.refs_17_ = f32[64,512]{1,0:T(8,128)S(1)} collective-permute-done((f32[64,512]{1,0:T(8,128)S(1)}, f32[64,512]{1,0:T(8,128)S(1)}, u32[]{:S(2)}, u32[]{:S(2)}) %collective-permute-start.31) | collective-permute-done | bytes 131104 | tf_op jit(solution)/shard_map/ppermute | solution.py:42
  38.6 10.7 %project.1 = (f32[256,2048]{1,0:T(8,128)S(1)}, f32[128,128]{1,0:T(8,128)S(1)}, f32[64,256]{1,0:T(8,128)S(1)}, f32[64,256]{1,0:T(8,128)S(1)}, f32[64,256]{1,0:T(8,128)S(1)}, /*index=5*/f32[64,256]{1,0:T(8,128)S(1)}) custom-call(bf16[256,448]{1,0:T(8,128)(2,1)S(1)} %get-tuple-element.95.select, bf16[128,256]{1,0:T(8,128)(2,1)S(1)} %get-tuple-element.96.select_c, ...), custom_call_target="tpu_custom_call" | custom-call | tf_op jit(solution)/shard_map/project/pallas_call | solution.py:305
  49.3 1.2 %collective-permute-start.35 = (f32[64,256]{1,0:T(8,128)S(1)}, f32[64,256]{1,0:T(8,128)S(1)}, u32[]{:S(2)}, u32[]{:S(2)}) collective-permute-start(f32[64,256]{1,0:T(8,128)S(1)} %get-tuple-element.103), channel_id=1, source_target_pairs={{0,1},{1,0},{2,3},{3,2},{4,5},{5,4},{6,7},{7,6},{8,9},{9,8},{10,11... | collective-permute-start | bytes 196616 | tf_op jit(solution)/shard_map/ppermute | solution.py:42
  50.6 3.0 %collective-permute-start.36 = (f32[64,256]{1,0:T(8,128)S(1)}, f32[64,256]{1,0:T(8,128)S(1)}, u32[]{:S(2)}, u32[]{:S(2)}) collective-permute-start(f32[64,256]{1,0:T(8,128)S(1)} %get-tuple-element.104), channel_id=1, source_target_pairs={{0,2},{1,3},{2,0},{3,1},{4,6},{5,7},{6,4},{7,5},{8,10},{9,11},{10,... | collective-permute-start | bytes 196616 | tf_op jit(solution)/shard_map/ppermute | solution.py:42
  53.6 0.2 collective-permute-start.37
  53.8 0.3 collective-permute-start.32
  54.1 3.8 %collective-permute-start.33 = (f32[128,128]{1,0:T(8,128)S(1)}, f32[128,128]{1,0:T(8,128)S(1)}, u32[]{:S(2)}, u32[]{:S(2)}) collective-permute-start(f32[128,128]{1,0:T(8,128)S(1)} %get-tuple-element.100.refs_0_), channel_id=1, source_target_pairs={{0,2},{1,3},{2,0},{3,1},{4,6},{5,7},{6,4},{7,5},{8,10},{9,11},{10,... | collective-permute-start | bytes 196616 | tf_op jit(solution)/shard_map/ppermute | solution.py:42
  58.0 0.2 collective-permute-start.34
  58.2 2.3 %collective-permute-done.37 = f32[64,256]{1,0:T(8,128)S(1)} collective-permute-done((f32[64,256]{1,0:T(8,128)S(1)}, f32[64,256]{1,0:T(8,128)S(1)}, u32[]{:S(2)}, u32[]{:S(2)}) %collective-permute-start.37) | collective-permute-done | bytes 65568 | tf_op jit(solution)/shard_map/ppermute | solution.py:42
  60.5 2.2 %collective-permute-start.38 = (f32[64,256]{1,0:T(8,128)S(1)}, f32[64,256]{1,0:T(8,128)S(1)}, u32[]{:S(2)}, u32[]{:S(2)}) collective-permute-start(f32[64,256]{1,0:T(8,128)S(1)} %add_add_fusion.1.refs_0_), channel_id=1, source_target_pairs={{0,1},{1,0},{2,3},{3,2},{4,5},{5,4},{6,7},{7,6},{8,9},{9,8},{10,11... | collective-permute-start | bytes 196616 | tf_op jit(solution)/shard_map/ppermute | solution.py:42
  62.7 3.9 %collective-permute-start.39 = (f32[64,256]{1,0:T(8,128)S(1)}, f32[64,256]{1,0:T(8,128)S(1)}, u32[]{:S(2)}, u32[]{:S(2)}) collective-permute-start(f32[64,256]{1,0:T(8,128)S(1)} %add_add_fusion.1.refs_0_), channel_id=1, source_target_pairs={{0,2},{1,3},{2,0},{3,1},{4,6},{5,7},{6,4},{7,5},{8,10},{9,11},{10,... | collective-permute-start | bytes 196616 | tf_op jit(solution)/shard_map/ppermute | solution.py:42
  66.6 1.4 %collective-permute-start.40 = (f32[64,256]{1,0:T(8,128)S(1)}, f32[64,256]{1,0:T(8,128)S(1)}, u32[]{:S(2)}, u32[]{:S(2)}) collective-permute-start(f32[64,256]{1,0:T(8,128)S(1)} %add_add_fusion.1.refs_0_), channel_id=1, source_target_pairs={{0,3},{1,2},{2,1},{3,0},{4,7},{5,6},{6,5},{7,4},{8,11},{9,10},{10,... | collective-permute-start | bytes 196616 | tf_op jit(solution)/shard_map/ppermute | solution.py:42
  68.0 3.4 %whiten.2.whitener = f32[256,256]{1,0:T(8,128)S(1)} custom-call(f32[128,128]{1,0:T(8,128)S(1)} %get-tuple-element.100.refs_0_, f32[128,128]{1,0:T(8,128)S(1)} %collective-permute-done.32.refs_1_, f32[128,128]{1,0:T(8,128)S(1)} %collective-permute-done.33.refs_2_, f32[128,128]{1,0:T(8,128)S(1)} %collective-permute-done.34.refs_3_), custom_call_target="tpu_custom_call" | custom-call | tf_op jit(solution)/shard_map/whiten/pallas_call | solution.py:362
  71.5 1.3 %collective-permute-done.40.refs_3_ = f32[64,256]{1,0:T(8,128)S(1)} collective-permute-done((f32[64,256]{1,0:T(8,128)S(1)}, f32[64,256]{1,0:T(8,128)S(1)}, u32[]{:S(2)}, u32[]{:S(2)}) %collective-permute-start.40) | collective-permute-done | bytes 65568 | tf_op jit(solution)/shard_map/ppermute | solution.py:42
  72.8 4.7 %update.1 = (f32[256,128]{1,0:T(8,128)}, f32[256,128]{1,0:T(8,128)}, f32[256,2048]{1,0:T(8,128)}, f32[256,2048]{1,0:T(8,128)}, f32[1,256]{1,0:T(1,128)S(1)}) custom-call(s32[1,256]{1,0:T(1,128)S(1)} %bitcast.63, f32[256,256]{1,0:T(8,128)S(1)} %whiten.2.whitener, f32[256,2048]{1,0:T(8,128)S(1)} %get-tuple-element.101.p, f32[256,2048]{1,0:T(8,128)S(1)} %copy-done.3, ...), custom_call_target="tpu_custom_call" | custom-call | tf_op jit(solution)/shard_map/update/pallas_call | solution.py:412
  77.5 0.7 collective-permute-start.41
  78.2 1.2 %collective-permute-start.42 = (f32[1,256]{1,0:T(1,128)S(1)}, f32[1,256]{1,0:T(1,128)S(1)}, u32[]{:S(2)}, u32[]{:S(2)}) collective-permute-start(f32[1,256]{1,0:T(1,128)S(1)} %get-tuple-element.110.refs_0_), channel_id=1, source_target_pairs={{0,2},{1,3},{2,0},{3,1},{4,6},{5,7},{6,4},{7,5},{8,10},{9,11},{10,... | collective-permute-start | bytes 3080 | tf_op jit(solution)/shard_map/ppermute | solution.py:42
  79.4 2.4 %collective-permute-start.43 = (f32[1,256]{1,0:T(1,128)S(1)}, f32[1,256]{1,0:T(1,128)S(1)}, u32[]{:S(2)}, u32[]{:S(2)}) collective-permute-start(f32[1,256]{1,0:T(1,128)S(1)} %get-tuple-element.110.refs_0_), channel_id=1, source_target_pairs={{0,3},{1,2},{2,1},{3,0},{4,7},{5,6},{6,5},{7,4},{8,11},{9,10},{10,... | collective-permute-start | bytes 3080 | tf_op jit(solution)/shard_map/ppermute | solution.py:42
  81.9 0.8 collective-permute-done.42.refs_2_
  82.7 2.1 %collective-permute-done.43.refs_3_ = f32[1,256]{1,0:T(1,128)S(1)} collective-permute-done((f32[1,256]{1,0:T(1,128)S(1)}, f32[1,256]{1,0:T(1,128)S(1)}, u32[]{:S(2)}, u32[]{:S(2)}) %collective-permute-start.43) | collective-permute-done | bytes 1056 | tf_op jit(solution)/shard_map/ppermute | solution.py:42
  84.8 0.6 mean.1
  85.4 0.9 %while.18 = (s32[]{:T(128)}, f32[256,128]{1,0:T(8,128)}, f32[256,128]{1,0:T(8,128)}, f32[256,2048]{1,0:T(8,128)}, f32[256,2048]{1,0:T(8,128)}, /*index=5*/f32[25...) while((s32[]{:T(128)}, f32[256,128]{1,0:T(8,128)}, ...), condition=%wide.region_2.3_spmd, body=%wide.region_0.2_spmd.sunk | while | flops 22968406016 | bytes 205383488 | solution.py:515
  (38 shorter events, 0.2 us)
Async XLA Ops:
  0.6 8.7 %copy-start = (f32[256,2048]{1,0:T(8,128)S(1)}, f32[256,2048]{1,0:T(8,128)}, u32[]{:S(2)}) copy-start(f32[256,2048]{1,0:T(8,128)} %b_re.3) | copy-start | bytes 6291460
  0.6 8.7 %copy-start.1 = (f32[256,2048]{1,0:T(8,128)S(1)}, f32[256,2048]{1,0:T(8,128)}, u32[]{:S(2)}) copy-start(f32[256,2048]{1,0:T(8,128)} %b_im.3) | copy-start | bytes 6291460
  4.6 11.4 %copy-start.7 = (s32[128]{0:T(128)S(1)}, s32[128]{0:T(128)}, u32[]{:S(2)}) copy-start(s32[128]{0:T(128)} %piv.1) | copy-start | bytes 1540
  4.6 34.0 %copy-start.3 = (f32[256,2048]{1,0:T(8,128)S(1)}, f32[256,2048]{1,0:T(8,128)}, u32[]{:S(2)}) copy-start(f32[256,2048]{1,0:T(8,128)} %re.5) | copy-start | bytes 6291460
  4.6 34.0 %copy-start.4 = (f32[256,2048]{1,0:T(8,128)S(1)}, f32[256,2048]{1,0:T(8,128)}, u32[]{:S(2)}) copy-start(f32[256,2048]{1,0:T(8,128)} %im.5) | copy-start | bytes 6291460
  4.6 34.0 %copy-start.6 = (s32[256]{0:T(256)S(1)}, s32[256]{0:T(256)}, u32[]{:S(2)}) copy-start(s32[256]{0:T(256)} %lens.1) | copy-start | bytes 3076
  4.6 4.7 %collective-permute-start.15 = (f32[56,2048]{1,0:T(8,128)S(1)}, f32[56,2048]{1,0:T(8,128)S(1)}, u32[]{:S(2)}, u32[]{:S(2)}) collective-permute-start(f32[56,2048]{1,0:T(8,128)S(1)} %pick.1.refs_0_), channel_id=1, source_target_pairs={{0,4},{4,0},{8,12},{12,8},{16,20},{20,16},{24,28},{28,24},{1,5},{5... | collective-permute-start | bytes 1376264 | tf_op jit(solution)/shard_map/ppermute | solution.py:42
  5.0 13.7 %collective-permute-start.13 = (f32[56,2048]{1,0:T(8,128)S(1)}, f32[56,2048]{1,0:T(8,128)S(1)}, u32[]{:S(2)}, u32[]{:S(2)}) collective-permute-start(f32[56,2048]{1,0:T(8,128)S(1)} %pick.1.refs_0_), channel_id=1, source_target_pairs={{0,8},{4,12},{8,0},{12,4},{16,24},{20,28},{24,16},{28,20},{1,9},{5... | collective-permute-start | bytes 1376264 | tf_op jit(solution)/shard_map/ppermute | solution.py:42
  7.5 12.6 %collective-permute-start.14 = (f32[56,2048]{1,0:T(8,128)S(1)}, f32[56,2048]{1,0:T(8,128)S(1)}, u32[]{:S(2)}, u32[]{:S(2)}) collective-permute-start(f32[56,2048]{1,0:T(8,128)S(1)} %pick.1.refs_0_), channel_id=1, source_target_pairs={{0,16},{4,20},{8,24},{12,28},{16,0},{20,4},{24,8},{28,12},{1,17},{... | collective-permute-start | bytes 1376264 | tf_op jit(solution)/shard_map/ppermute | solution.py:42
  11.5 10.8 %collective-permute-start.22 = (f32[64,512]{1,0:T(8,128)S(1)}, f32[64,512]{1,0:T(8,128)S(1)}, u32[]{:S(2)}, u32[]{:S(2)}) collective-permute-start(f32[64,512]{1,0:T(8,128)S(1)} %cross.1), channel_id=1, source_target_pairs={{0,1},{1,0},{2,3},{3,2},{4,5},{5,4},{6,7},{7,6},{8,9},{9,8},{10,11... | collective-permute-start | bytes 393224 | tf_op jit(solution)/shard_map/ppermute | solution.py:42
  13.2 12.9 %collective-permute-start.23 = (f32[64,512]{1,0:T(8,128)S(1)}, f32[64,512]{1,0:T(8,128)S(1)}, u32[]{:S(2)}, u32[]{:S(2)}) collective-permute-start(f32[64,512]{1,0:T(8,128)S(1)} %cross.1), channel_id=1, source_target_pairs={{0,2},{1,3},{2,0},{3,1},{4,6},{5,7},{6,4},{7,5},{8,10},{9,11},{10,... | collective-permute-start | bytes 393224 | tf_op jit(solution)/shard_map/ppermute | solution.py:42
  15.7 10.3 %collective-permute-start.24 = (f32[64,512]{1,0:T(8,128)S(1)}, f32[64,512]{1,0:T(8,128)S(1)}, u32[]{:S(2)}, u32[]{:S(2)}) collective-permute-start(f32[64,512]{1,0:T(8,128)S(1)} %cross.1), channel_id=1, source_target_pairs={{0,3},{1,2},{2,1},{3,0},{4,7},{5,6},{6,5},{7,4},{8,11},{9,10},{10,... | collective-permute-start | bytes 393224 | tf_op jit(solution)/shard_map/ppermute | solution.py:42
  20.2 7.7 %collective-permute-start.16 = (f32[56,1024]{1,0:T(8,128)S(1)}, f32[56,1024]{1,0:T(8,128)S(1)}, u32[]{:S(2)}, u32[]{:S(2)}) collective-permute-start(f32[56,1024]{1,0:T(8,128)S(1)} %slice.74), channel_id=1, source_target_pairs={{0,16},{4,20},{8,24},{12,28},{16,0},{20,4},{24,8},{28,12},{1,17},{... | collective-permute-start | bytes 688136 | tf_op jit(solution)/shard_map/ppermute | solution.py:42
  22.0 8.0 %collective-permute-start.17 = (f32[56,1024]{1,0:T(8,128)S(1)}, f32[56,1024]{1,0:T(8,128)S(1)}, u32[]{:S(2)}, u32[]{:S(2)}) collective-permute-start(f32[56,1024]{1,0:T(8,128)S(1)} %slice.75), channel_id=1, source_target_pairs={{0,8},{4,12},{8,0},{12,4},{16,24},{20,28},{24,16},{28,20},{1,9},{5... | collective-permute-start | bytes 688136 | tf_op jit(solution)/shard_map/ppermute | solution.py:42
  26.1 5.3 %collective-permute-start.26 = (f32[64,512]{1,0:T(8,128)S(1)}, f32[64,512]{1,0:T(8,128)S(1)}, u32[]{:S(2)}, u32[]{:S(2)}) collective-permute-start(f32[64,512]{1,0:T(8,128)S(1)} %add_add_fusion.refs_10_), channel_id=1, source_target_pairs={{0,8},{4,12},{8,0},{12,4},{16,24},{20,28},{24,16},{28,20},{1,9},{5... | collective-permute-start | bytes 393224 | tf_op jit(solution)/shard_map/ppermute | solution.py:42
  26.5 5.0 %collective-permute-start.28 = (f32[64,512]{1,0:T(8,128)S(1)}, f32[64,512]{1,0:T(8,128)S(1)}, u32[]{:S(2)}, u32[]{:S(2)}) collective-permute-start(f32[64,512]{1,0:T(8,128)S(1)} %add_add_fusion.refs_10_), channel_id=1, source_target_pairs={{0,16},{4,20},{8,24},{12,28},{16,0},{20,4},{24,8},{28,12},{1,17},{... | collective-permute-start | bytes 393224 | tf_op jit(solution)/shard_map/ppermute | solution.py:42
  27.9 10.7 %collective-permute-start.18 = (f32[56,2048]{1,0:T(8,128)S(1)}, f32[56,2048]{1,0:T(8,128)S(1)}, u32[]{:S(2)}, u32[]{:S(2)}) collective-permute-start(f32[56,2048]{1,0:T(8,128)S(1)} %collective-permute-done.13.refs_1_), channel_id=1, source_target_pairs={{0,4},{4,0},{8,12},{12,8},{16,20},{20,16},{24,28},{28,24},{1,5},{5... | collective-permute-start | bytes 1376264 | tf_op jit(solution)/shard_map/ppermute | solution.py:42
  27.9 10.7 %collective-permute-start.19 = (f32[56,2048]{1,0:T(8,128)S(1)}, f32[56,2048]{1,0:T(8,128)S(1)}, u32[]{:S(2)}, u32[]{:S(2)}) collective-permute-start(f32[56,2048]{1,0:T(8,128)S(1)} %collective-permute-done.14.refs_2_), channel_id=1, source_target_pairs={{0,4},{4,0},{8,12},{12,8},{16,20},{20,16},{24,28},{28,24},{1,5},{5... | collective-permute-start | bytes 1376264 | tf_op jit(solution)/shard_map/ppermute | solution.py:42
  30.0 5.9 %collective-permute-start.30 = (f32[64,512]{1,0:T(8,128)S(1)}, f32[64,512]{1,0:T(8,128)S(1)}, u32[]{:S(2)}, u32[]{:S(2)}) collective-permute-start(f32[64,512]{1,0:T(8,128)S(1)} %add_add_fusion.refs_10_), channel_id=1, source_target_pairs={{0,24},{4,28},{8,16},{12,20},{16,8},{20,12},{24,0},{28,4},{1,25},{... | collective-permute-start | bytes 393224 | tf_op jit(solution)/shard_map/ppermute | solution.py:42
  31.4 4.5 %collective-permute-start.25 = (f32[64,512]{1,0:T(8,128)S(1)}, f32[64,512]{1,0:T(8,128)S(1)}, u32[]{:S(2)}, u32[]{:S(2)}) collective-permute-start(f32[64,512]{1,0:T(8,128)S(1)} %add_add_fusion.refs_10_), channel_id=1, source_target_pairs={{0,4},{4,0},{8,12},{12,8},{16,20},{20,16},{24,28},{28,24},{1,5},{5... | collective-permute-start | bytes 393224 | tf_op jit(solution)/shard_map/ppermute | solution.py:42
  31.5 5.0 %collective-permute-start.27 = (f32[64,512]{1,0:T(8,128)S(1)}, f32[64,512]{1,0:T(8,128)S(1)}, u32[]{:S(2)}, u32[]{:S(2)}) collective-permute-start(f32[64,512]{1,0:T(8,128)S(1)} %collective-permute-done.26.refs_12_), channel_id=1, source_target_pairs={{0,4},{4,0},{8,12},{12,8},{16,20},{20,16},{24,28},{28,24},{1,5},{5... | collective-permute-start | bytes 393224 | tf_op jit(solution)/shard_map/ppermute | solution.py:42
  35.9 1.3 %collective-permute-start.29 = (f32[64,512]{1,0:T(8,128)S(1)}, f32[64,512]{1,0:T(8,128)S(1)}, u32[]{:S(2)}, u32[]{:S(2)}) collective-permute-start(f32[64,512]{1,0:T(8,128)S(1)} %collective-permute-done.28.refs_14_), channel_id=1, source_target_pairs={{0,4},{4,0},{8,12},{12,8},{16,20},{20,16},{24,28},{28,24},{1,5},{5... | collective-permute-start | bytes 393224 | tf_op jit(solution)/shard_map/ppermute | solution.py:42
  35.9 2.7 %collective-permute-start.20 = (f32[56,1024]{1,0:T(8,128)S(1)}, f32[56,1024]{1,0:T(8,128)S(1)}, u32[]{:S(2)}, u32[]{:S(2)}) collective-permute-start(f32[56,1024]{1,0:T(8,128)S(1)} %collective-permute-done.16.refs_3_), channel_id=1, source_target_pairs={{0,4},{4,0},{8,12},{12,8},{16,20},{20,16},{24,28},{28,24},{1,5},{5... | collective-permute-start | bytes 688136 | tf_op jit(solution)/shard_map/ppermute | solution.py:42
  36.4 2.2 %collective-permute-start.21 = (f32[56,1024]{1,0:T(8,128)S(1)}, f32[56,1024]{1,0:T(8,128)S(1)}, u32[]{:S(2)}, u32[]{:S(2)}) collective-permute-start(f32[56,1024]{1,0:T(8,128)S(1)} %collective-permute-done.17.refs_4_), channel_id=1, source_target_pairs={{0,4},{4,0},{8,12},{12,8},{16,20},{20,16},{24,28},{28,24},{1,5},{5... | collective-permute-start | bytes 688136 | tf_op jit(solution)/shard_map/ppermute | solution.py:42
  37.2 1.3 %collective-permute-start.31 = (f32[64,512]{1,0:T(8,128)S(1)}, f32[64,512]{1,0:T(8,128)S(1)}, u32[]{:S(2)}, u32[]{:S(2)}) collective-permute-start(f32[64,512]{1,0:T(8,128)S(1)} %collective-permute-done.30.refs_16_), channel_id=1, source_target_pairs={{0,4},{4,0},{8,12},{12,8},{16,20},{20,16},{24,28},{28,24},{1,5},{5... | collective-permute-start | bytes 393224 | tf_op jit(solution)/shard_map/ppermute | solution.py:42
  49.3 8.6 %collective-permute-start.35 = (f32[64,256]{1,0:T(8,128)S(1)}, f32[64,256]{1,0:T(8,128)S(1)}, u32[]{:S(2)}, u32[]{:S(2)}) collective-permute-start(f32[64,256]{1,0:T(8,128)S(1)} %get-tuple-element.103), channel_id=1, source_target_pairs={{0,1},{1,0},{2,3},{3,2},{4,5},{5,4},{6,7},{7,6},{8,9},{9,8},{10,11... | collective-permute-start | bytes 196616 | tf_op jit(solution)/shard_map/ppermute | solution.py:42
  50.6 7.6 %collective-permute-start.36 = (f32[64,256]{1,0:T(8,128)S(1)}, f32[64,256]{1,0:T(8,128)S(1)}, u32[]{:S(2)}, u32[]{:S(2)}) collective-permute-start(f32[64,256]{1,0:T(8,128)S(1)} %get-tuple-element.104), channel_id=1, source_target_pairs={{0,2},{1,3},{2,0},{3,1},{4,6},{5,7},{6,4},{7,5},{8,10},{9,11},{10,... | collective-permute-start | bytes 196616 | tf_op jit(solution)/shard_map/ppermute | solution.py:42
  53.6 6.9 %collective-permute-start.37 = (f32[64,256]{1,0:T(8,128)S(1)}, f32[64,256]{1,0:T(8,128)S(1)}, u32[]{:S(2)}, u32[]{:S(2)}) collective-permute-start(f32[64,256]{1,0:T(8,128)S(1)} %get-tuple-element.105), channel_id=1, source_target_pairs={{0,3},{1,2},{2,1},{3,0},{4,7},{5,6},{6,5},{7,4},{8,11},{9,10},{10,... | collective-permute-start | bytes 196616 | tf_op jit(solution)/shard_map/ppermute | solution.py:42
  53.8 12.8 %collective-permute-start.32 = (f32[128,128]{1,0:T(8,128)S(1)}, f32[128,128]{1,0:T(8,128)S(1)}, u32[]{:S(2)}, u32[]{:S(2)}) collective-permute-start(f32[128,128]{1,0:T(8,128)S(1)} %get-tuple-element.100.refs_0_), channel_id=1, source_target_pairs={{0,1},{1,0},{2,3},{3,2},{4,5},{5,4},{6,7},{7,6},{8,9},{9,8},{10,11... | collective-permute-start | bytes 196616 | tf_op jit(solution)/shard_map/ppermute | solution.py:42
  54.1 13.9 %collective-permute-start.33 = (f32[128,128]{1,0:T(8,128)S(1)}, f32[128,128]{1,0:T(8,128)S(1)}, u32[]{:S(2)}, u32[]{:S(2)}) collective-permute-start(f32[128,128]{1,0:T(8,128)S(1)} %get-tuple-element.100.refs_0_), channel_id=1, source_target_pairs={{0,2},{1,3},{2,0},{3,1},{4,6},{5,7},{6,4},{7,5},{8,10},{9,11},{10,... | collective-permute-start | bytes 196616 | tf_op jit(solution)/shard_map/ppermute | solution.py:42
  58.0 10.0 %collective-permute-start.34 = (f32[128,128]{1,0:T(8,128)S(1)}, f32[128,128]{1,0:T(8,128)S(1)}, u32[]{:S(2)}, u32[]{:S(2)}) collective-permute-start(f32[128,128]{1,0:T(8,128)S(1)} %get-tuple-element.100.refs_0_), channel_id=1, source_target_pairs={{0,3},{1,2},{2,1},{3,0},{4,7},{5,6},{6,5},{7,4},{8,11},{9,10},{10,... | collective-permute-start | bytes 196616 | tf_op jit(solution)/shard_map/ppermute | solution.py:42
  60.5 11.0 %collective-permute-start.38 = (f32[64,256]{1,0:T(8,128)S(1)}, f32[64,256]{1,0:T(8,128)S(1)}, u32[]{:S(2)}, u32[]{:S(2)}) collective-permute-start(f32[64,256]{1,0:T(8,128)S(1)} %add_add_fusion.1.refs_0_), channel_id=1, source_target_pairs={{0,1},{1,0},{2,3},{3,2},{4,5},{5,4},{6,7},{7,6},{8,9},{9,8},{10,11... | collective-permute-start | bytes 196616 | tf_op jit(solution)/shard_map/ppermute | solution.py:42
  62.7 8.8 %collective-permute-start.39 = (f32[64,256]{1,0:T(8,128)S(1)}, f32[64,256]{1,0:T(8,128)S(1)}, u32[]{:S(2)}, u32[]{:S(2)}) collective-permute-start(f32[64,256]{1,0:T(8,128)S(1)} %add_add_fusion.1.refs_0_), channel_id=1, source_target_pairs={{0,2},{1,3},{2,0},{3,1},{4,6},{5,7},{6,4},{7,5},{8,10},{9,11},{10,... | collective-permute-start | bytes 196616 | tf_op jit(solution)/shard_map/ppermute | solution.py:42
  66.6 6.2 %collective-permute-start.40 = (f32[64,256]{1,0:T(8,128)S(1)}, f32[64,256]{1,0:T(8,128)S(1)}, u32[]{:S(2)}, u32[]{:S(2)}) collective-permute-start(f32[64,256]{1,0:T(8,128)S(1)} %add_add_fusion.1.refs_0_), channel_id=1, source_target_pairs={{0,3},{1,2},{2,1},{3,0},{4,7},{5,6},{6,5},{7,4},{8,11},{9,10},{10,... | collective-permute-start | bytes 196616 | tf_op jit(solution)/shard_map/ppermute | solution.py:42
  77.5 4.4 %collective-permute-start.41 = (f32[1,256]{1,0:T(1,128)S(1)}, f32[1,256]{1,0:T(1,128)S(1)}, u32[]{:S(2)}, u32[]{:S(2)}) collective-permute-start(f32[1,256]{1,0:T(1,128)S(1)} %get-tuple-element.110.refs_0_), channel_id=1, source_target_pairs={{0,1},{1,0},{2,3},{3,2},{4,5},{5,4},{6,7},{7,6},{8,9},{9,8},{10,11... | collective-permute-start | bytes 3080 | tf_op jit(solution)/shard_map/ppermute | solution.py:42
  78.2 4.5 %collective-permute-start.42 = (f32[1,256]{1,0:T(1,128)S(1)}, f32[1,256]{1,0:T(1,128)S(1)}, u32[]{:S(2)}, u32[]{:S(2)}) collective-permute-start(f32[1,256]{1,0:T(1,128)S(1)} %get-tuple-element.110.refs_0_), channel_id=1, source_target_pairs={{0,2},{1,3},{2,0},{3,1},{4,6},{5,7},{6,4},{7,5},{8,10},{9,11},{10,... | collective-permute-start | bytes 3080 | tf_op jit(solution)/shard_map/ppermute | solution.py:42
  79.4 5.4 %collective-permute-start.43 = (f32[1,256]{1,0:T(1,128)S(1)}, f32[1,256]{1,0:T(1,128)S(1)}, u32[]{:S(2)}, u32[]{:S(2)}) collective-permute-start(f32[1,256]{1,0:T(1,128)S(1)} %get-tuple-element.110.refs_0_), channel_id=1, source_target_pairs={{0,3},{1,2},{2,1},{3,0},{4,7},{5,6},{6,5},{7,4},{8,11},{9,10},{10,... | collective-permute-start | bytes 3080 | tf_op jit(solution)/shard_map/ppermute | solution.py:42
